TPU v7x, 512 devices: a whole 4x4x16 slice. The times are simulated.
512 devices in a mesh: head: 2 (over y_hi), view: 16 (over z), row: 16 (over y_lo, x, core).
Axes of the slice: x: 4, y: 4 (y_hi: 2, y_lo: 2; y = y_hi * 2 + y_lo), z: 16, core: 2. Of those that a mesh axis runs over, the one named last changes fastest.
Arguments:
- query_feats: bfloat16 [16, 128, 16, 1024], P('view', 'row', None, 'head'), may hold values from -125 to 125
- key_feats: bfloat16 [16, 128, 16, 1024], P('view', 'row', None, 'head'), may hold values from -7 to 7
- value_feats: bfloat16 [16, 128, 16, 1024], P('view', 'row', None, 'head'), may hold values from -6 to 6
- target: bfloat16 [16, 128, 16, 1024], P('view', 'row', None, 'head'), may hold values from -6 to 6
- token_rates: float32 [16, 2, 2048], P('view', 'head', 'row'), may hold values from 5 to 100
- row_reach: int32 [128], P('row'), may hold values from 1 to 2
- view_counts: int32 [16], P('view'), may hold values from 682 to 2048
- w_first: bfloat16 [2, 512, 512], P('head'), may hold values from -0.25 to 0.25
- w_third: bfloat16 [2, 512, 512], P('head'), may hold values from -0.25 to 0.25
- w_second: bfloat16 [2, 512, 512], P('head'), may hold values from -0.25 to 0.25
Outputs:
- fast_out: bfloat16 [16, 128, 16, 1024], P('view', 'row', None, 'head')
All inputs are finite; a program needn't handle non-finite values.
Results may differ from a plain program's by a relative error of at most 0.03.
Values may be sent and summed in bfloat16 or wider, within the bound.
No kernel may reach another device: no remote copies, remote signals or barrier semaphores. Data moves between devices by JAX's collectives and lax.ppermute only.
A program may use at most 64 MiB of HBM per device.

v0:
```python
import math

import jax
import jax.numpy as jnp
from jax import lax
from jax.sharding import Mesh
from jax.sharding import PartitionSpec as P

HD = 512
ATT_HD = 128
HALO = 2
ROW = ("row_0", "row_1", "row_2")


def with_halo(value, sides, width):
    for axis, dim in sides:
        size, length = (lax.axis_size(axis), value.shape[dim])
        up = [(i, (i + 1) % size) for i in range(size - 1)]
        down = [(j, i) for i, j in up]
        last = lax.slice_in_dim(value, length - width, length, axis=dim)
        leading = lax.slice_in_dim(value, 0, width, axis=dim)
        before = lax.ppermute(last, axis, up)
        after = lax.ppermute(leading, axis, down)
        value = jnp.concatenate([before, value, after], axis=dim)
    return value


def cut_along(value, dim, length):
    lengths = value.shape
    parts = value.reshape(*lengths[:dim], length, lengths[dim] // length, *lengths[dim + 1 :])
    return jnp.moveaxis(parts, dim, 0)


def summed_on_arrival(value, axis, dim):
    parts = cut_along(value, dim, lax.axis_size(axis))
    arrived = lax.all_to_all(parts, axis, split_axis=0, concat_axis=0, tiled=True)
    return arrived.sum(axis=0)


def sum_in_two_steps(value, axes, dim):
    far, near = axes
    parts = cut_along(value, dim, lax.axis_size(far))
    nearer = summed_on_arrival(parts, near, dim + 1)
    arrived = lax.all_to_all(nearer, far, split_axis=0, concat_axis=0, tiled=True)
    return arrived.sum(axis=0)


def in_one_piece(arrays, axis, dim, along):
    both = jnp.concatenate(arrays, axis=along)
    whole, at, gathered = (sum_in_two_steps(both, axis, dim), 0, [])
    for a in arrays:
        gathered.append(lax.slice_in_dim(whole, at, at + a.shape[along], axis=along))
        at += a.shape[along]
    return tuple(gathered)


def filled_up(lines, length):
    spare = -len(lines) % length
    return jnp.pad(lines, [(0, spare)] + [(0, 0)] * (lines.ndim - 1))


def copy_for_each(value, axis):
    length = lax.axis_size(axis)
    return lax.all_to_all(
        jnp.broadcast_to(value[None], (length, *value.shape)), axis, 0, 0, tiled=True
    )


def in_order(parts, dim):
    lengths = list(parts.shape[1:])
    lengths[dim] *= parts.shape[0]
    return jnp.moveaxis(parts, 0, dim).reshape(lengths)


def collect(value, axis, dim):
    parts = copy_for_each(value, axis)
    return in_order(parts, dim)


def sum_by_parts(value, axes):
    own = summed_on_arrival(filled_up(value, lax.axis_size(axes)), axes, 0)
    whole = collect(own, axes, 0)
    return whole[: len(value)].reshape(value.shape)


def together(arrays, axis):
    ends = [0]
    for a in arrays:
        ends.append(ends[-1] + a.size)
    so_far = sum_by_parts(jnp.concatenate([a.ravel() for a in arrays]), axis)
    return tuple((so_far[b:e].reshape(a.shape) for a, b, e in zip(arrays, ends, ends[1:])))


def gather_axes(value, axes, dim):
    far, near = axes
    parts = copy_for_each(copy_for_each(value, far), near)
    return in_order(parts.swapaxes(0, 1).reshape(-1, *value.shape), dim)


def sent_together(arrays, axis, dim, along):
    widths = [a.shape[along] for a in arrays]
    both = jnp.concatenate(arrays, axis=along)
    whole = gather_axes(both, axis, dim)
    return tuple(jnp.split(whole, [sum(widths[:k]) for k in range(1, len(widths))], axis=along))


def silu_slope(values_in):
    sigmoid_x = jax.nn.sigmoid(values_in)
    return sigmoid_x * (1.0 + values_in * (1.0 - sigmoid_x))


def attend(
    query_rows,
    key_rows,
    value_rows,
    q_row_ids,
    k_row_ids,
    q_tok,
    k_tok,
    k_valid,
    q_reach,
    grid_rows,
):
    count_q = query_rows.shape[0]
    count_k = key_rows.shape[0]
    groups = query_rows.shape[1] // ATT_HD
    query_heads = query_rows.reshape(count_q, groups, ATT_HD)
    key_heads = key_rows.reshape(count_k, groups, ATT_HD)
    value_heads = value_rows.reshape(count_k, groups, ATT_HD)
    scores = jnp.einsum(
        "qhd,khd->hqk", query_heads, key_heads, preferred_element_type=jnp.float32
    ) / math.sqrt(ATT_HD)
    inside = (k_row_ids >= 0) & (k_row_ids < grid_rows)
    in_band = jnp.abs(k_row_ids[None, :] - q_row_ids[:, None]) <= q_reach[:, None]
    allowed = in_band & inside[None, :] & (k_valid[None, :] | (k_tok[None, :] == q_tok[:, None]))
    scores = jnp.where(allowed[None], scores, -1e30)
    row_top = jnp.max(scores, -1, keepdims=True)
    powers = jnp.exp(scores - row_top)
    weights = (powers / jnp.sum(powers, -1, keepdims=True)).astype(jnp.bfloat16)
    output_rows = jnp.einsum(
        "hqk,khd->qhd", weights, value_heads, preferred_element_type=jnp.float32
    )
    return output_rows.reshape(count_q, groups * ATT_HD).astype(jnp.bfloat16)


def renorm(old_matrix, grad, total_valid):
    old_rows = old_matrix.astype(jnp.float32)
    raised = old_rows + grad / total_valid
    rescale = jnp.sqrt(jnp.sum(old_rows * old_rows, -1, keepdims=True) + 1e-06) / jnp.sqrt(
        jnp.sum(raised * raised, -1, keepdims=True) + 1e-06
    )
    return (raised * rescale).astype(jnp.bfloat16)


def per_device(
    query_feats,
    key_feats,
    value_feats,
    target,
    token_rates,
    row_reach,
    view_counts,
    w_first,
    w_third,
    w_second,
):
    row_count = query_feats.shape[1]
    col_count = query_feats.shape[2]
    feat_width = query_feats.shape[3]
    heads_here = feat_width // HD
    tokens_here = row_count * col_count
    key_span = row_count + 2 * HALO
    grid_rows = lax.axis_size(ROW) * row_count
    row_base = lax.axis_index(ROW) * row_count
    view_total = view_counts[0]
    paired = jnp.stack([key_feats[0], value_feats[0]], 0)
    padded = with_halo(paired, ((ROW, 1),), HALO)
    q_row_ids = row_base + jnp.repeat(jnp.arange(row_count, dtype=jnp.int32), col_count)
    k_row_ids = row_base - HALO + jnp.repeat(jnp.arange(key_span, dtype=jnp.int32), col_count)
    q_tok = q_row_ids * col_count + jnp.tile(jnp.arange(col_count, dtype=jnp.int32), row_count)
    k_tok = k_row_ids * col_count + jnp.tile(jnp.arange(col_count, dtype=jnp.int32), key_span)
    k_valid = k_tok < view_total
    q_reach = jnp.repeat(row_reach, col_count)
    attended = attend(
        query_feats[0].reshape(tokens_here, feat_width),
        padded[0].reshape(key_span * col_count, feat_width),
        padded[1].reshape(key_span * col_count, feat_width),
        q_row_ids,
        k_row_ids,
        q_tok,
        k_tok,
        k_valid,
        q_reach,
        grid_rows,
    )
    attended = attended.reshape(tokens_here, heads_here, HD).astype(jnp.float32)
    fast_keys = (
        attended * lax.rsqrt(jnp.mean(attended * attended, -1, keepdims=True) + 1e-06)
    ).astype(jnp.bfloat16)
    valid_mask = (q_tok < view_total).astype(jnp.float32)
    rates_tok = token_rates[0].T
    scaled = (
        rates_tok[:, :, None]
        * valid_mask[:, None, None]
        * target[0].reshape(tokens_here, heads_here, HD).astype(jnp.float32)
    ).astype(jnp.bfloat16)
    first_proj = jnp.einsum("thi,hij->thj", fast_keys, w_first, preferred_element_type=jnp.float32)
    third_proj = jnp.einsum("thi,hij->thj", fast_keys, w_third, preferred_element_type=jnp.float32)
    gated_rows = (jax.nn.silu(first_proj) * third_proj).astype(jnp.bfloat16)
    back_rows = jnp.einsum("tho,hjo->thj", scaled, w_second, preferred_element_type=jnp.float32)
    back_first = (back_rows * third_proj * silu_slope(first_proj)).astype(jnp.bfloat16)
    back_third = (back_rows * jax.nn.silu(first_proj)).astype(jnp.bfloat16)
    grad_first = jnp.einsum(
        "thi,thj->hij", fast_keys, back_first, preferred_element_type=jnp.float32
    )
    grad_third = jnp.einsum(
        "thi,thj->hij", fast_keys, back_third, preferred_element_type=jnp.float32
    )
    grad_second = jnp.einsum("thj,tho->hjo", gated_rows, scaled, preferred_element_type=jnp.float32)
    share_rows = HD // lax.axis_size(ROW)
    row_offset = lax.axis_index(ROW) * share_rows
    part_first, part_third, part_second = in_one_piece(
        (grad_first, grad_third, grad_second), (("row_0", "row_1"), "row_2"), 1, 0
    )
    part_first, part_third, part_second, total_valid = together(
        (part_first, part_third, part_second, view_total.astype(jnp.float32)), "view"
    )
    own_first = renorm(
        lax.dynamic_slice_in_dim(w_first, row_offset, share_rows, 1), part_first, total_valid
    )
    own_third = renorm(
        lax.dynamic_slice_in_dim(w_third, row_offset, share_rows, 1), part_third, total_valid
    )
    own_second = renorm(
        lax.dynamic_slice_in_dim(w_second, row_offset, share_rows, 1), part_second, total_valid
    )
    new_first, new_third, new_second = sent_together(
        (own_first, own_third, own_second), (("row_0", "row_1"), "row_2"), 1, 0
    )
    applied = (
        jax.nn.silu(
            jnp.einsum("thi,hij->thj", fast_keys, new_first, preferred_element_type=jnp.float32)
        )
        * jnp.einsum("thi,hij->thj", fast_keys, new_third, preferred_element_type=jnp.float32)
    ).astype(jnp.bfloat16)
    fast_out = jnp.einsum(
        "thj,hjo->tho", applied, new_second, preferred_element_type=jnp.float32
    ).astype(jnp.bfloat16)
    return fast_out.reshape(1, row_count, col_count, feat_width)


def solution(mesh):
    torus = Mesh(
        mesh.devices.reshape(mesh.shape["head"], mesh.shape["view"], 2, 4, 2),
        ("head", "view", "row_0", "row_1", "row_2"),
    )
    return jax.shard_map(
        per_device,
        mesh=torus,
        in_specs=(
            P("view", ROW, None, "head"),
            P("view", ROW, None, "head"),
            P("view", ROW, None, "head"),
            P("view", ROW, None, "head"),
            P("view", "head", ROW),
            P(ROW),
            P("view"),
            P("head", None, None),
            P("head", None, None),
            P("head", None, None),
        ),
        out_specs=P("view", ROW, None, "head"),
        check_vma=False,
    )
```

profile of v0, /device:TPU:1, one launch (start us, length us, event | category | flops | bytes accessed | tf_op | source)
XLA Modules:
  0.0 135.6 jit_solution(6673130017847079832)
XLA Ops:
  0.0 0.9 constant_dynamic-update-slice_fusion.1
  0.9 0.9 constant_dynamic-update-slice_fusion
  1.9 4.5 %collective-permute-start = (bf16[2,2,16,512]{3,2,1,0:T(8,128)(2,1)S(1)}, bf16[2,2,16,512]{3,2,1,0:T(8,128)(2,1)S(1)}, u32[]{:S(2)}, u32[]{:S(2)}) collective-permute-start(bf16[2,2,16,512]{3,2,1,0:T(8,128)(2,1)S(1)} %get-tuple-element.20), channel_id=1, source_target_pairs={{0,1},{1,2},{2,3},{3,4},{4,5},{5,6},{6,7},{7,8},{8,9},{9,10},{10,1... | collective-permute-start | bytes 196616 | tf_op jit(solution)/shard_map/ppermute | solution.py:22
  6.4 5.6 %collective-permute-start.1 = (bf16[2,2,16,512]{3,2,1,0:T(8,128)(2,1)S(1)}, bf16[2,2,16,512]{3,2,1,0:T(8,128)(2,1)S(1)}, u32[]{:S(2)}, u32[]{:S(2)}) collective-permute-start(bf16[2,2,16,512]{3,2,1,0:T(8,128)(2,1)S(1)} %get-tuple-element.21), channel_id=1, source_target_pairs={{1,0},{2,1},{3,2},{4,3},{5,4},{6,5},{7,6},{8,7},{9,8},{10,9},{11,1... | collective-permute-start | bytes 196616 | tf_op jit(solution)/shard_map/ppermute | solution.py:23
  12.7 0.7 broadcast_in_dim.26
  13.8 0.7 compare_select_fusion
  14.6 1.4 %convolution_bitcast_fusion.7 = f32[128,1,512]{2,0,1:T(8,128)S(1)} fusion(bf16[1,512,512]{2,1,0:T(8,128)(2,1)} %param.19, bf16[128,1,1,1,1,1,512]{6,0,5,4,3,2,1:T(8,128)(2,1)} %bitcast.156, f32[128]{0:T(128)S(1)} %get-tuple-element.11), kind=kOutput, calls=%fused_computation.16 | convolution fusion | flops 67305472 | bytes 918016 | tf_op jit(solution)/shard_map/tho,hjo->thj/dot_general | solution.py:210
  16.1 0.9 reshape_reshape_squeeze.11
  18.8 0.4 convolution_bitcast_fusion.2
  19.7 0.3 convolution_bitcast_fusion
  20.1 0.3 pad_maximum_fusion
  20.4 0.5 copy.85
  21.0 5.9 %all_to_all.35 = f32[2,8,3,32,512]{4,3,1,2,0:T(8,128)S(1)} all-to-all(f32[2,8,3,32,512]{4,3,1,2,0:T(8,128)S(1)} %bitcast.150), channel_id=1, replica_groups=mesh['head'=2,'view'=16,'row_0'=2,'row_1'=4,'row_2'=2] {'row_2'}, dimensions={0} | all-to-all | bytes 6291456 | tf_op jit(solution)/shard_map/all_to_all | solution.py:36
  26.8 1.6 %reduce_sum.101 = f32[8,3,32,512]{3,2,0,1:T(8,128)} reduce(f32[2,8,3,32,512]{4,3,1,2,0:T(8,128)S(1)} %all_to_all.35, f32[]{:T(128)} %constant.48.clone.1), dimensions={0}, to_apply=%region_3.4 | reduce | flops 393216 | bytes 4718596 | tf_op jit(solution)/shard_map/reduce_sum | solution.py:37
  28.4 2.8 %copy.56 = f32[8,3,32,512]{3,2,1,0:T(8,128)} copy(f32[8,3,32,512]{3,2,0,1:T(8,128)} %reduce_sum.101) | data formatting | bytes 3145728 | tf_op jit(solution)/shard_map/reduce_sum | solution.py:37
  31.2 3.6 %all-to-all-start.1 = ((f32[8,3,32,512]{3,2,1,0:T(8,128)}), f32[8,3,32,512]{3,2,1,0:T(8,128)S(1)}, u32[]{:S(2)}, u32[]{:S(2)}) async-start(f32[8,3,32,512]{3,2,1,0:T(8,128)} %copy.56), calls=%async_computation.1 | async-start | bytes 3145728 | tf_op jit(solution)/shard_map/all_to_all | solution.py:44
  34.8 21.5 %all-to-all-done.1 = f32[8,3,32,512]{3,2,1,0:T(8,128)S(1)} async-done(((f32[8,3,32,512]{3,2,1,0:T(8,128)}), f32[8,3,32,512]{3,2,1,0:T(8,128)S(1)}, u32[]{:S(2)}, u32[]{:S(2)}) %all-to-all-start.1) | async-done | bytes 1572896 | tf_op jit(solution)/shard_map/all_to_all | solution.py:44
  56.8 25.6 %all_to_all.36 = f32[16,1,3073]{2,1,0:T(1,128)S(1)} all-to-all(f32[16,1,3073]{2,1,0:T(1,128)S(1)} %all_to_all.24), channel_id=1, replica_groups=mesh['head'=2,'view'=16,'row_0'=2,'row_1'=4,'row_2'=2] {'view'}, dimensions={0} | all-to-all | bytes 393344 | tf_op jit(solution)/shard_map/all_to_all | solution.py:36
  82.5 0.8 broadcast_in_dim.29
  83.3 9.3 %all-to-all-start.3 = ((f32[16,1,3073]{2,1,0:T(1,128)}), f32[16,1,3073]{2,1,0:T(1,128)S(1)}, u32[]{:S(2)}, u32[]{:S(2)}) async-start(f32[16,1,3073]{2,1,0:T(1,128)} %broadcast_in_dim.29), calls=%async_computation.3 | async-start | bytes 409600 | tf_op jit(solution)/shard_map/all_to_all | solution.py:64
  92.6 12.6 %all-to-all-done.3 = f32[16,1,3073]{2,1,0:T(1,128)S(1)} async-done(((f32[16,1,3073]{2,1,0:T(1,128)}), f32[16,1,3073]{2,1,0:T(1,128)S(1)}, u32[]{:S(2)}, u32[]{:S(2)}) %all-to-all-start.3) | async-done | bytes 196704 | tf_op jit(solution)/shard_map/all_to_all | solution.py:64
  105.2 0.5 reduce.9
  105.8 0.5 slice.60
  106.3 0.7 slice_divide_fusion.2
  107.0 0.9 fusion.36
  107.9 0.8 multiply_convert_fusion.5
  108.8 0.9 fusion.34
  109.7 0.8 multiply_convert_fusion.7
  110.6 0.8 multiply_convert_fusion.6
  111.5 11.5 %all_to_all.37 = bf16[8,3,32,512]{3,2,1,0:T(8,128)(2,1)S(1)} all-to-all(bf16[8,3,32,512]{3,2,1,0:T(8,128)(2,1)S(1)} %broadcast_in_dim.30), channel_id=1, replica_groups=mesh['head'=2,'view'=16,'row_0'=2,'row_1'=4,'row_2'=2] {'row_0','row_1'}, dimensions={0} | all-to-all | bytes 1572864 | tf_op jit(solution)/shard_map/all_to_all | solution.py:64
  123.2 10.7 %all_to_all.38 = bf16[2,8,3,32,512]{4,3,2,1,0:T(8,128)(2,1)S(1)} all-to-all(bf16[2,8,3,32,512]{4,3,2,1,0:T(8,128)(2,1)S(1)} %broadcast_in_dim.31), channel_id=1, replica_groups=mesh['head'=2,'view'=16,'row_0'=2,'row_1'=4,'row_2'=2] {'row_2'}, dimensions={0} | all-to-all | bytes 3145728 | tf_op jit(solution)/shard_map/all_to_all | solution.py:64
  134.5 1.1 convolution_convert_fusion
  (56 shorter events, 4.4 us)
Async XLA Ops:
  1.9 15.1 %collective-permute-start = (bf16[2,2,16,512]{3,2,1,0:T(8,128)(2,1)S(1)}, bf16[2,2,16,512]{3,2,1,0:T(8,128)(2,1)S(1)}, u32[]{:S(2)}, u32[]{:S(2)}) collective-permute-start(bf16[2,2,16,512]{3,2,1,0:T(8,128)(2,1)S(1)} %get-tuple-element.20), channel_id=1, source_target_pairs={{0,1},{1,2},{2,3},{3,4},{4,5},{5,6},{6,7},{7,8},{8,9},{9,10},{10,1... | collective-permute-start | bytes 196616 | tf_op jit(solution)/shard_map/ppermute | solution.py:22
  6.4 10.6 %collective-permute-start.1 = (bf16[2,2,16,512]{3,2,1,0:T(8,128)(2,1)S(1)}, bf16[2,2,16,512]{3,2,1,0:T(8,128)(2,1)S(1)}, u32[]{:S(2)}, u32[]{:S(2)}) collective-permute-start(bf16[2,2,16,512]{3,2,1,0:T(8,128)(2,1)S(1)} %get-tuple-element.21), channel_id=1, source_target_pairs={{1,0},{2,1},{3,2},{4,3},{5,4},{6,5},{7,6},{8,7},{9,8},{10,9},{11,1... | collective-permute-start | bytes 196616 | tf_op jit(solution)/shard_map/ppermute | solution.py:23
  17.1 1.1 copy-start
  17.1 1.3 copy-start.1
  18.2 1.5 %copy-start.2 = (bf16[1,8,16,512]{3,2,1,0:T(8,128)(2,1)S(1)}, bf16[1,8,16,512]{3,2,1,0:T(8,128)(2,1)}, u32[]{:S(2)}) copy-start(bf16[1,8,16,512]{3,2,1,0:T(8,128)(2,1)} %param.13) | copy-start | bytes 393220
  31.2 25.0 %all-to-all-start.1 = ((f32[8,3,32,512]{3,2,1,0:T(8,128)}), f32[8,3,32,512]{3,2,1,0:T(8,128)S(1)}, u32[]{:S(2)}, u32[]{:S(2)}) async-start(f32[8,3,32,512]{3,2,1,0:T(8,128)} %copy.56), calls=%async_computation.1 | async-start | bytes 3145728 | tf_op jit(solution)/shard_map/all_to_all | solution.py:44
  83.3 21.9 %all-to-all-start.3 = ((f32[16,1,3073]{2,1,0:T(1,128)}), f32[16,1,3073]{2,1,0:T(1,128)S(1)}, u32[]{:S(2)}, u32[]{:S(2)}) async-start(f32[16,1,3073]{2,1,0:T(1,128)} %broadcast_in_dim.29), calls=%async_computation.3 | async-start | bytes 409600 | tf_op jit(solution)/shard_map/all_to_all | solution.py:64
where the time goes:
time: 138 us; the launch traced here: 136 us
  blocking collectives  53.6 us (39%)
  waiting for transfers between devices  34 us (25%)
  starting transfers between devices  22.9 us (17%)
  local copies, waits for them, and re-layouts  9.82 us (7%)
  other arithmetic  8.81 us (6%)
  matrix products  5.25 us (4%)
    all_to_all x2, blocking collectives, summed_on_arrival(): lax.all_to_all(parts, axis, split_axis=0, concat_axis=0, tiled=True)  31.5 us
    all_to_all x2, blocking collectives, copy_for_each(): lax.all_to_all(jnp.broadcast_to(value[None], (length, *value.shape)), axi...  22.2 us
    all_to_all x1, waiting for transfers between devices, sum_in_two_steps(): lax.all_to_all(nearer, far, split_axis=0, concat_axis=0, tiled=True)  21.5 us
    all_to_all x1, waiting for transfers between devices, copy_for_each(): lax.all_to_all(jnp.broadcast_to(value[None], (length, *value.shape)), axi...  12.6 us
    all_to_all x1, starting transfers between devices, copy_for_each(): lax.all_to_all(jnp.broadcast_to(value[None], (length, *value.shape)), axi...  9.29 us
    ppermute x1, starting transfers between devices, with_halo(): after = lax.ppermute(leading, axis, down)  5.57 us
    ppermute x1, starting transfers between devices, with_halo(): before = lax.ppermute(last, axis, up)  4.51 us
    all_to_all x1, starting transfers between devices, sum_in_two_steps(): lax.all_to_all(nearer, far, split_axis=0, concat_axis=0, tiled=True)  3.58 us
  transfers between devices with their start and end apart: 4, of which 2 were waited for; matrix products, arithmetic and copies ran while one was open for 3% of the time, Pallas kernels for 0%

commit v1 on v0

v1 whole, which is shorter than its diff:
```python
import math

import jax
import jax.numpy as jnp
from jax import lax
from jax.sharding import Mesh
from jax.sharding import PartitionSpec as P

HD = 512
ATT_HD = 128
HALO = 2
PLANE = ("row_0", "row_1")
ROW = ("row_0", "row_1", "row_2")
SWAP = [(0, 1), (1, 0)]
BF = jnp.bfloat16
F32 = jnp.float32


def silu_slope(values_in):
    sigmoid_x = jax.nn.sigmoid(values_in)
    return sigmoid_x * (1.0 + values_in * (1.0 - sigmoid_x))


def attend(query_rows, key_rows, value_rows, q_row_ids, k_row_ids, q_tok, k_tok, k_valid, q_reach, grid_rows):
    count_q = query_rows.shape[0]
    count_k = key_rows.shape[0]
    groups = query_rows.shape[1] // ATT_HD
    query_heads = query_rows.reshape(count_q, groups, ATT_HD)
    key_heads = key_rows.reshape(count_k, groups, ATT_HD)
    value_heads = value_rows.reshape(count_k, groups, ATT_HD)
    scores = jnp.einsum("qhd,khd->hqk", query_heads, key_heads, preferred_element_type=F32) / math.sqrt(ATT_HD)
    inside = (k_row_ids >= 0) & (k_row_ids < grid_rows)
    in_band = jnp.abs(k_row_ids[None, :] - q_row_ids[:, None]) <= q_reach[:, None]
    allowed = in_band & inside[None, :] & (k_valid[None, :] | (k_tok[None, :] == q_tok[:, None]))
    scores = jnp.where(allowed[None], scores, -1e30)
    row_top = jnp.max(scores, -1, keepdims=True)
    powers = jnp.exp(scores - row_top)
    weights = (powers / jnp.sum(powers, -1, keepdims=True)).astype(BF)
    output_rows = jnp.einsum("hqk,khd->qhd", weights, value_heads, preferred_element_type=F32)
    return output_rows.reshape(count_q, groups * ATT_HD).astype(BF)


def dot(a, b, ca=1, cb=0):
    return lax.dot_general(a, b, (((ca,), (cb,)), ((), ())), preferred_element_type=F32)


def exchange(x, axes):
    return lax.all_to_all(x, axes, 0, 0, tiled=True)


def to_all(x, axes):
    return exchange(jnp.broadcast_to(x[None], (lax.axis_size(axes), *x.shape)), axes)


def halves(x, core):
    w = x.shape[1] // 2
    left, right = x[:, :w], x[:, w:]
    return jnp.where(core == 0, left, right), jnp.where(core == 0, right, left)


def per_device(query_feats, key_feats, value_feats, target, token_rates, row_reach, view_counts, w_first, w_third, w_second):
    _, rows, cols, width = query_feats.shape
    tokens = rows * cols
    span = rows + 2 * HALO
    n_row = lax.axis_size(ROW)
    grid_rows = n_row * rows
    core = lax.axis_index("row_2")
    plane = lax.axis_index(PLANE)
    view = lax.axis_index("view")
    n_plane, n_view = lax.axis_size(PLANE), lax.axis_size("view")
    row_base = lax.axis_index(ROW) * rows
    count = view_counts[0]

    paired = jnp.stack([key_feats[0], value_feats[0]], 0)
    leading, last = paired[:, :HALO], paired[:, rows - HALO :]
    to_core = jnp.where(core == 0, last, leading)
    to_chip = jnp.where(core == 0, leading, last)
    next_chip = [p for i in range(1, n_row - 1, 2) for p in ((i, i + 1), (i + 1, i))]
    from_core = lax.ppermute(to_core, "row_2", SWAP)
    from_chip = lax.ppermute(to_chip, ROW, next_chip)
    before = jnp.where(core == 0, from_chip, from_core)
    after = jnp.where(core == 0, from_core, from_chip)
    padded = jnp.concatenate([before, paired, after], 1)

    q_row_ids = row_base + jnp.repeat(jnp.arange(rows, dtype=jnp.int32), cols)
    k_row_ids = row_base - HALO + jnp.repeat(jnp.arange(span, dtype=jnp.int32), cols)
    q_tok = row_base * cols + jnp.arange(tokens, dtype=jnp.int32)
    k_tok = (row_base - HALO) * cols + jnp.arange(span * cols, dtype=jnp.int32)
    attended = attend(
        query_feats[0].reshape(tokens, width),
        padded[0].reshape(span * cols, width),
        padded[1].reshape(span * cols, width),
        q_row_ids,
        k_row_ids,
        q_tok,
        k_tok,
        k_tok < count,
        jnp.repeat(row_reach, cols),
        grid_rows,
    ).astype(F32)
    fast_keys = (attended * lax.rsqrt(jnp.mean(attended * attended, -1, keepdims=True) + 1e-06)).astype(BF)
    valid = (q_tok < count).astype(F32)
    scaled = (token_rates[0, 0][:, None] * valid[:, None] * target[0].reshape(tokens, width).astype(F32)).astype(BF)

    own = jnp.stack([fast_keys, scaled], 0)
    both = jnp.concatenate([own, lax.ppermute(own, "row_2", SWAP)], 1)
    keys2, scaled2 = both[0], both[1]
    first = dot(keys2, w_first[0])
    third = dot(keys2, w_third[0])
    back = dot(scaled2, w_second[0], 1, 1)
    gated = (jax.nn.silu(first) * third).astype(BF)
    back_first = (back * third * silu_slope(first)).astype(BF)
    back_third = (back * jax.nn.silu(first)).astype(BF)
    keys_half = halves(keys2, core)[0]
    gated_half = halves(gated, core)[0]
    share = HD // 2 // n_plane
    grads = jnp.concatenate(
        [
            dot(a, b, 0, 0).astype(BF).reshape(n_plane, share, width)
            for a, b in ((keys_half, back_first), (keys_half, back_third), (gated_half, scaled2))
        ],
        1,
    )
    part = exchange(grads, PLANE).astype(F32).sum(0)
    few = share // n_view
    part = part.reshape(3, n_view, few, width).swapaxes(0, 1).reshape(n_view, 3 * few, width)
    digits = jnp.stack([count % 16, (count // 16) % 16, count // 256]).astype(F32)
    lane = jnp.arange(width)
    digit_row = jnp.where(lane == 0, digits[0], jnp.where(lane == 1, digits[1], digits[2]))
    extra = jnp.broadcast_to(digit_row, (n_view, 2, width))
    part = jnp.concatenate([part, extra], 1).astype(BF)
    summed = exchange(part, "view").astype(F32).sum(0)
    total = summed[3 * few, 0] + 16.0 * summed[3 * few, 1] + 256.0 * summed[3 * few, 2]
    grad = summed[: 3 * few].reshape(3, few, width)
    at = core * (HD // 2) + plane * share + view * few
    old = jnp.stack([lax.dynamic_slice_in_dim(w[0], at, few, 0) for w in (w_first, w_third, w_second)]).astype(F32)
    raised = old + grad / total
    rescale = jnp.sqrt(jnp.sum(old * old, -1, keepdims=True) + 1e-06) / jnp.sqrt(
        jnp.sum(raised * raised, -1, keepdims=True) + 1e-06
    )
    new = (raised * rescale).astype(BF).reshape(3 * few, width)
    new = jnp.concatenate([new, jnp.zeros((2, width), BF)], 0)
    lines = to_all(new, "view")[:, : 3 * few].reshape(n_view, 3, few, width).swapaxes(0, 1).reshape(3 * share, width)
    mine = to_all(lines, PLANE)
    theirs = lax.ppermute(mine, "row_2", SWAP)
    m1, m3, m2 = (mine[:, k * share : (k + 1) * share].reshape(HD // 2, width) for k in range(3))
    t1, t3, t2 = (theirs[:, k * share : (k + 1) * share].reshape(HD // 2, width) for k in range(3))
    k_mine, k_theirs = halves(fast_keys, core)
    first = dot(k_mine, m1) + dot(k_theirs, t1)
    third = dot(k_mine, m3) + dot(k_theirs, t3)
    applied = (jax.nn.silu(first) * third).astype(BF)
    a_mine, a_theirs = halves(applied, core)
    out = (dot(a_mine, m2) + dot(a_theirs, t2)).astype(BF)
    return out.reshape(1, rows, cols, width)


def solution(mesh):
    torus = Mesh(
        mesh.devices.reshape(mesh.shape["head"], mesh.shape["view"], 2, 4, 2),
        ("head", "view", "row_0", "row_1", "row_2"),
    )
    feats = P("view", ROW, None, "head")
    heads = P("head", None, None)
    return jax.shard_map(
        per_device,
        mesh=torus,
        in_specs=(feats, feats, feats, feats, P("view", "head", ROW), P(ROW), P("view"), heads, heads, heads),
        out_specs=feats,
        check_vma=False,
    )
```

time: 138 us -> 110 us (0.80); the launches traced: 136 us -> 109 us
  blocking collectives: 53.6 us -> 17.5 us
  starting transfers between devices: 22.9 us -> 38.2 us
  other arithmetic: 8.81 us -> 4 us
  local copies, waits for them, and re-layouts: 9.82 us -> 7.73 us
  between operations: 1.06 us -> 3.15 us
    all_to_all x4 -> x1, blocking collectives: 53.6 us -> 17.5 us  [exchange(): return lax.all_to_all(x, axes, 0, 0, tiled=True)]
    ppermute x2 -> x4, starting transfers between devices: 10.1 us -> 17.9 us  [the longest x1 6.56 us: per_device(): theirs = lax.ppermute(mine, 'row_2', SWAP)]
    all_to_all x2 -> x3, starting transfers between devices: 12.9 us -> 20.3 us  [exchange(): return lax.all_to_all(x, axes, 0, 0, tiled=True)]
    reduce_sum x5 -> x4, other arithmetic: 3.71 us -> 0.35 us  [the longest x1 0.12 us: per_device(): jnp.sum(raised * raised, -1, keepdims=True) + 1e-06]
    all_to_all x2 -> x3, waiting for transfers between devices: 34 us -> 31.1 us  [exchange(): return lax.all_to_all(x, axes, 0, 0, tiled=True)]
    ppermute x2 -> x4, waiting for transfers between devices: 0.01 us -> 2.86 us  [the longest x1 1.5 us: per_device(): both = jnp.concatenate([own, lax.ppermute(own, 'row_2', SWAP)], 1)]
    reduce_sum x1 -> x0, local copies, waits for them, and re-layouts: 2.75 us -> none  [summed_on_arrival(): return arrived.sum(axis=0)]
    convert_element_type x5, other arithmetic: 2.56 us -> 0.41 us  [the longest x2 0.17 us: per_device(): (attended * lax.rsqrt(jnp.mean(attended * attended, -1, keepdims=True) +...]
  transfers between devices with their start and end apart: 4 -> 7, of which waited for: 2 -> 5; matrix products, arithmetic and copies ran while one was open for 3% -> 4% of each run, Pallas kernels for 0% -> 0%
where the time goes in v1:
time: 110 us; the launch traced here: 109 us
  starting transfers between devices  38.2 us (35%)
  waiting for transfers between devices  34 us (31%)
  blocking collectives  17.5 us (16%)
  local copies, waits for them, and re-layouts  7.73 us (7%)
  matrix products  4.62 us (4%)
  other arithmetic  4 us (4%)
  between operations  3.15 us (3%)
    all_to_all x3, waiting for transfers between devices, exchange(): return lax.all_to_all(x, axes, 0, 0, tiled=True)  31.1 us
    all_to_all x3, starting transfers between devices, exchange(): return lax.all_to_all(x, axes, 0, 0, tiled=True)  20.3 us
    all_to_all x1, blocking collectives, exchange(): return lax.all_to_all(x, axes, 0, 0, tiled=True)  17.5 us
    ppermute x1, starting transfers between devices, per_device(): theirs = lax.ppermute(mine, 'row_2', SWAP)  6.56 us
    ppermute x1, starting transfers between devices, per_device(): from_core = lax.ppermute(to_core, 'row_2', SWAP)  4.94 us
    ppermute x1, starting transfers between devices, per_device(): from_chip = lax.ppermute(to_chip, ROW, next_chip)  4.51 us
    dot_general x12, matrix products, dot(): lax.dot_general(a, b, (((ca,), (cb,)), ((), ())), preferred_element_type=...  3.75 us
    unnamed x16, local copies, waits for them, and re-layouts  2.55 us
  transfers between devices with their start and end apart: 7, of which 5 were waited for; matrix products, arithmetic and copies ran while one was open for 4% of the time, Pallas kernels for 0%

profile of v1, /device:TPU:1, one launch (start us, length us, event | category | flops | bytes accessed | tf_op | source)
XLA Modules:
  0.0 109.2 jit_solution(10497634754606090943)
XLA Ops:
  0.0 1.0 constant_dynamic-update-slice_fusion.1
  1.0 0.9 constant_dynamic-update-slice_fusion
  2.0 4.5 %collective-permute-start = (bf16[2,2,16,512]{3,2,1,0:T(8,128)(2,1)S(1)}, bf16[2,2,16,512]{3,2,1,0:T(8,128)(2,1)S(1)}, u32[]{:S(2)}, u32[]{:S(2)}) collective-permute-start(bf16[2,2,16,512]{3,2,1,0:T(8,128)(2,1)S(1)} %get-tuple-element.15), channel_id=1, source_target_pairs={{1,2},{2,1},{3,4},{4,3},{5,6},{6,5},{7,8},{8,7},{9,10},{10,9},{11,... | collective-permute-start | bytes 196616 | tf_op jit(solution)/shard_map/ppermute | solution.py:80
  6.5 4.9 %collective-permute-start.1 = (bf16[2,2,16,512]{3,2,1,0:T(8,128)(2,1)S(1)}, bf16[2,2,16,512]{3,2,1,0:T(8,128)(2,1)S(1)}, u32[]{:S(2)}, u32[]{:S(2)}) collective-permute-start(bf16[2,2,16,512]{3,2,1,0:T(8,128)(2,1)S(1)} %get-tuple-element.16), channel_id=1, source_target_pairs={{0,1},{1,0},{2,3},{3,2},{4,5},{5,4},{6,7},{7,6},{8,9},{9,8},{10,11... | collective-permute-start | bytes 196616 | tf_op jit(solution)/shard_map/ppermute | solution.py:79
  13.0 0.3 fusion.52
  13.6 0.3 multiply_reduce_fusion
  14.2 1.9 %collective-permute-start.2 = (bf16[2,128,512]{2,1,0:T(8,128)(2,1)S(1)}, bf16[2,128,512]{2,1,0:T(8,128)(2,1)S(1)}, u32[]{:S(2)}, u32[]{:S(2)}) collective-permute-start(bf16[2,128,512]{2,1,0:T(8,128)(2,1)S(1)} %pad_maximum_fusion.3), channel_id=1, source_target_pairs={{0,1},{1,0},{2,3},{3,2},{4,5},{5,4},{6,7},{7,6},{8,9},{9,8},{10,11... | collective-permute-start | bytes 786440 | tf_op jit(solution)/shard_map/ppermute | solution.py:106
  16.2 1.5 %collective-permute-done.2 = bf16[2,128,512]{2,1,0:T(8,128)(2,1)S(1)} collective-permute-done((bf16[2,128,512]{2,1,0:T(8,128)(2,1)S(1)}, bf16[2,128,512]{2,1,0:T(8,128)(2,1)S(1)}, u32[]{:S(2)}, u32[]{:S(2)}) %collective-permute-start.2) | collective-permute-done | bytes 262176 | tf_op jit(solution)/shard_map/ppermute | solution.py:106
  17.7 0.3 fusion.9
  18.0 0.7 copy-done.6
  18.8 0.3 multiply_convert_fusion
  19.1 0.3 convolution_convert_fusion
  19.4 0.8 copy-done.1
  20.1 0.3 fusion.13
  20.5 0.4 convolution_convert_fusion.1
  20.8 0.4 convolution_convert_fusion.2
  21.3 1.0 pad_maximum_fusion
  22.3 3.5 %all-to-all-start = ((bf16[8,96,512]{2,1,0:T(8,128)(2,1)}), bf16[8,96,512]{2,1,0:T(8,128)(2,1)S(1)}, u32[]{:S(2)}, u32[]{:S(2)}) async-start(bf16[8,96,512]{2,1,0:T(8,128)(2,1)} %pad_maximum_fusion), calls=%async_computation | async-start | bytes 1572864 | tf_op jit(solution)/shard_map/all_to_all | solution.py:48
  26.0 0.7 fusion.51
  26.6 1.9 %select_convert_fusion = bf16[512]{0:T(512)(128)(2,1)S(1)} fusion(bf16[]{:T(256)} %bitcast.22, bf16[]{:T(256)} %bitcast.21, bf16[]{:T(256)} %bitcast.20), kind=kLoop, calls=%fused_computation.81 | loop fusion | flops 2048 | bytes 1030 | tf_op jit(solution)/shard_map/convert.11
  28.5 10.4 %all-to-all-done = bf16[8,96,512]{2,1,0:T(8,128)(2,1)S(1)} async-done(((bf16[8,96,512]{2,1,0:T(8,128)(2,1)}), bf16[8,96,512]{2,1,0:T(8,128)(2,1)S(1)}, u32[]{:S(2)}, u32[]{:S(2)}) %all-to-all-start) | async-done | bytes 786464 | tf_op jit(solution)/shard_map/all_to_all | solution.py:48
  39.1 0.7 copy.33
  39.8 13.2 %all-to-all-start.1 = ((bf16[16,8,512]{2,1,0:T(8,128)(2,1)}), bf16[16,8,512]{2,1,0:T(8,128)(2,1)S(1)}, u32[]{:S(2)}, u32[]{:S(2)}) async-start(bf16[16,8,512]{2,1,0:T(8,128)(2,1)} %copy.33), calls=%async_computation.1 | async-start | bytes 262144 | tf_op jit(solution)/shard_map/all_to_all | solution.py:48
  53.3 11.7 %all-to-all-done.1 = bf16[16,8,512]{2,1,0:T(8,128)(2,1)S(1)} async-done(((bf16[16,8,512]{2,1,0:T(8,128)(2,1)}), bf16[16,8,512]{2,1,0:T(8,128)(2,1)S(1)}, u32[]{:S(2)}, u32[]{:S(2)}) %all-to-all-start.1) | async-done | bytes 131104 | tf_op jit(solution)/shard_map/all_to_all | solution.py:48
  65.0 0.7 fusion.50
  67.9 17.5 %all_to_all.20 = bf16[16,8,512]{2,1,0:T(8,128)(2,1)S(1)} all-to-all(bf16[16,8,512]{2,1,0:T(8,128)(2,1)S(1)} %broadcast_in_dim.72), channel_id=1, replica_groups=mesh['head'=2,'view'=16,'row_0'=2,'row_1'=4,'row_2'=2] {'view'}, dimensions={0} | all-to-all | bytes 262144 | tf_op jit(solution)/shard_map/all_to_all | solution.py:48
  85.6 1.0 broadcast_in_dim.74
  86.5 3.5 %all-to-all-start.3 = ((bf16[8,96,512]{2,1,0:T(8,128)(2,1)}), bf16[8,96,512]{2,1,0:T(8,128)(2,1)S(1)}, u32[]{:S(2)}, u32[]{:S(2)}) async-start(bf16[8,96,512]{2,1,0:T(8,128)(2,1)} %broadcast_in_dim.74), calls=%async_computation.3 | async-start | bytes 1572864 | tf_op jit(solution)/shard_map/all_to_all | solution.py:48
  90.2 9.0 %all-to-all-done.3 = bf16[8,96,512]{2,1,0:T(8,128)(2,1)S(1)} async-done(((bf16[8,96,512]{2,1,0:T(8,128)(2,1)}), bf16[8,96,512]{2,1,0:T(8,128)(2,1)S(1)}, u32[]{:S(2)}, u32[]{:S(2)}) %all-to-all-start.3) | async-done | bytes 786464 | tf_op jit(solution)/shard_map/all_to_all | solution.py:48
  99.3 6.6 %collective-permute-start.3 = (bf16[8,96,512]{2,1,0:T(8,128)(2,1)S(1)}, bf16[8,96,512]{2,1,0:T(8,128)(2,1)S(1)}, u32[]{:S(2)}, u32[]{:S(2)}) collective-permute-start(bf16[8,96,512]{2,1,0:T(8,128)(2,1)S(1)} %all-to-all-done.3), channel_id=1, source_target_pairs={{0,1},{1,0},{2,3},{3,2},{4,5},{5,4},{6,7},{7,6},{8,9},{9,8},{10,11... | collective-permute-start | bytes 2359304 | tf_op jit(solution)/shard_map/ppermute | solution.py:145
  106.3 1.4 %collective-permute-done.3 = bf16[8,96,512]{2,1,0:T(8,128)(2,1)S(1)} collective-permute-done((bf16[8,96,512]{2,1,0:T(8,128)(2,1)S(1)}, bf16[8,96,512]{2,1,0:T(8,128)(2,1)S(1)}, u32[]{:S(2)}, u32[]{:S(2)}) %collective-permute-start.3) | collective-permute-done | bytes 786464 | tf_op jit(solution)/shard_map/ppermute | solution.py:145
  108.4 0.9 fusion.7
  (70 shorter events, 3.6 us)
Async XLA Ops:
  0.0 17.7 %copy-start = (bf16[1,512,512]{2,1,0:T(8,128)(2,1)S(1)}, bf16[1,512,512]{2,1,0:T(8,128)(2,1)}, u32[]{:S(2)}) copy-start(bf16[1,512,512]{2,1,0:T(8,128)(2,1)} %param.17) | copy-start | bytes 1572868
  0.0 12.1 %copy-start.4 = (s32[8]{0:T(128)S(1)}, s32[8]{0:T(128)}, u32[]{:S(2)}) copy-start(s32[8]{0:T(128)} %param.15) | copy-start | bytes 100
  0.0 12.4 %copy-start.5 = (f32[1,1,128]{2,1,0:T(1,128)S(1)}, f32[1,1,128]{2,1,0:T(1,128)}, u32[]{:S(2)}) copy-start(f32[1,1,128]{2,1,0:T(1,128)} %param.14) | copy-start | bytes 1540
  0.0 12.5 %copy-start.2 = (bf16[1,8,16,512]{3,2,1,0:T(8,128)(2,1)S(1)}, bf16[1,8,16,512]{3,2,1,0:T(8,128)(2,1)}, u32[]{:S(2)}) copy-start(bf16[1,8,16,512]{3,2,1,0:T(8,128)(2,1)} %param.13) | copy-start | bytes 393220
  0.0 12.7 %copy-start.3 = (bf16[1,8,16,512]{3,2,1,0:T(8,128)(2,1)S(1)}, bf16[1,8,16,512]{3,2,1,0:T(8,128)(2,1)}, u32[]{:S(2)}) copy-start(bf16[1,8,16,512]{3,2,1,0:T(8,128)(2,1)} %param.10) | copy-start | bytes 393220
  2.0 10.9 %collective-permute-start = (bf16[2,2,16,512]{3,2,1,0:T(8,128)(2,1)S(1)}, bf16[2,2,16,512]{3,2,1,0:T(8,128)(2,1)S(1)}, u32[]{:S(2)}, u32[]{:S(2)}) collective-permute-start(bf16[2,2,16,512]{3,2,1,0:T(8,128)(2,1)S(1)} %get-tuple-element.15), channel_id=1, source_target_pairs={{1,2},{2,1},{3,4},{4,3},{5,6},{6,5},{7,8},{8,7},{9,10},{10,9},{11,... | collective-permute-start | bytes 196616 | tf_op jit(solution)/shard_map/ppermute | solution.py:80
  6.5 6.3 %collective-permute-start.1 = (bf16[2,2,16,512]{3,2,1,0:T(8,128)(2,1)S(1)}, bf16[2,2,16,512]{3,2,1,0:T(8,128)(2,1)S(1)}, u32[]{:S(2)}, u32[]{:S(2)}) collective-permute-start(bf16[2,2,16,512]{3,2,1,0:T(8,128)(2,1)S(1)} %get-tuple-element.16), channel_id=1, source_target_pairs={{0,1},{1,0},{2,3},{3,2},{4,5},{5,4},{6,7},{7,6},{8,9},{9,8},{10,11... | collective-permute-start | bytes 196616 | tf_op jit(solution)/shard_map/ppermute | solution.py:79
  14.2 3.4 %collective-permute-start.2 = (bf16[2,128,512]{2,1,0:T(8,128)(2,1)S(1)}, bf16[2,128,512]{2,1,0:T(8,128)(2,1)S(1)}, u32[]{:S(2)}, u32[]{:S(2)}) collective-permute-start(bf16[2,128,512]{2,1,0:T(8,128)(2,1)S(1)} %pad_maximum_fusion.3), channel_id=1, source_target_pairs={{0,1},{1,0},{2,3},{3,2},{4,5},{5,4},{6,7},{7,6},{8,9},{9,8},{10,11... | collective-permute-start | bytes 786440 | tf_op jit(solution)/shard_map/ppermute | solution.py:106
  17.7 1.0 copy-start.6
  19.1 1.0 copy-start.1
  22.3 16.6 %all-to-all-start = ((bf16[8,96,512]{2,1,0:T(8,128)(2,1)}), bf16[8,96,512]{2,1,0:T(8,128)(2,1)S(1)}, u32[]{:S(2)}, u32[]{:S(2)}) async-start(bf16[8,96,512]{2,1,0:T(8,128)(2,1)} %pad_maximum_fusion), calls=%async_computation | async-start | bytes 1572864 | tf_op jit(solution)/shard_map/all_to_all | solution.py:48
  39.8 25.2 %all-to-all-start.1 = ((bf16[16,8,512]{2,1,0:T(8,128)(2,1)}), bf16[16,8,512]{2,1,0:T(8,128)(2,1)S(1)}, u32[]{:S(2)}, u32[]{:S(2)}) async-start(bf16[16,8,512]{2,1,0:T(8,128)(2,1)} %copy.33), calls=%async_computation.1 | async-start | bytes 262144 | tf_op jit(solution)/shard_map/all_to_all | solution.py:48
  86.5 12.7 %all-to-all-start.3 = ((bf16[8,96,512]{2,1,0:T(8,128)(2,1)}), bf16[8,96,512]{2,1,0:T(8,128)(2,1)S(1)}, u32[]{:S(2)}, u32[]{:S(2)}) async-start(bf16[8,96,512]{2,1,0:T(8,128)(2,1)} %broadcast_in_dim.74), calls=%async_computation.3 | async-start | bytes 1572864 | tf_op jit(solution)/shard_map/all_to_all | solution.py:48
  99.3 8.5 %collective-permute-start.3 = (bf16[8,96,512]{2,1,0:T(8,128)(2,1)S(1)}, bf16[8,96,512]{2,1,0:T(8,128)(2,1)S(1)}, u32[]{:S(2)}, u32[]{:S(2)}) collective-permute-start(bf16[8,96,512]{2,1,0:T(8,128)(2,1)S(1)} %all-to-all-done.3), channel_id=1, source_target_pairs={{0,1},{1,0},{2,3},{3,2},{4,5},{5,4},{6,7},{7,6},{8,9},{9,8},{10,11... | collective-permute-start | bytes 2359304 | tf_op jit(solution)/shard_map/ppermute | solution.py:145

commit v2 on v1

v2 whole, which is shorter than its diff:
```python
import math

import jax
import jax.numpy as jnp
from jax import lax
from jax.experimental import pallas as pl
from jax.experimental.pallas import tpu as pltpu
from jax.sharding import Mesh
from jax.sharding import PartitionSpec as P

HD = 512
ATT_HD = 128
HALO = 2
PLANE = ("row_0", "row_1")
ROW = ("row_0", "row_1", "row_2")
SWAP = [(0, 1), (1, 0)]
BF = jnp.bfloat16
F32 = jnp.float32
VMEM = pl.BlockSpec(memory_space=pltpu.VMEM)
SMEM = pl.BlockSpec(memory_space=pltpu.SMEM)


def dot(a, b, ca=1, cb=0):
    return lax.dot_general(a, b, (((ca,), (cb,)), ((), ())), preferred_element_type=F32)


def exchange(x, axes):
    return lax.all_to_all(x, axes, 0, 0, tiled=True)


def iota(shape, dim):
    return lax.broadcasted_iota(jnp.int32, shape, dim)


def call(kernel, shape, dtype, specs, flops=1 << 20, name=None):
    many = isinstance(shape, list)
    outs = [jax.ShapeDtypeStruct(s, d) for s, d in zip(shape, dtype)] if many else jax.ShapeDtypeStruct(shape, dtype)
    return pl.pallas_call(
        kernel,
        out_shape=outs,
        in_specs=specs,
        out_specs=[VMEM] * len(shape) if many else VMEM,
        compiler_params=pltpu.CompilerParams(vmem_limit_bytes=24 << 20),
        cost_estimate=pl.CostEstimate(flops=flops, bytes_accessed=1 << 20, transcendentals=0),
        name=name,
    )


def edges_kernel(key_ref, value_ref, core_ref, chip_ref):
    core = lax.axis_index("row_2")
    near = HALO * 16
    end = key_ref.shape[0] - near
    to_core = pl.multiple_of((1 - core) * end, near)
    to_chip = pl.multiple_of(core * end, near)
    for i, ref in enumerate((key_ref, value_ref)):
        core_ref[i] = ref[pl.ds(to_core, near), :]
        chip_ref[i] = ref[pl.ds(to_chip, near), :]


def attend_kernel(rows, cols, grid_rows, count_ref, reach_ref, q_ref, k_ref, v_ref, core_ref, chip_ref, target_ref, rate_ref, out_ref):
    core = lax.axis_index("row_2")
    base = lax.axis_index(ROW) * rows
    count = count_ref[0]
    tokens, near = rows * cols, HALO * cols
    span = tokens + 2 * near
    at = iota((1, span), 1)
    below, above = base + rows, base - HALO
    first_core = jnp.where(core == 0, below, above)
    first_chip = jnp.where(core == 0, above, below)
    start = jnp.where(at < tokens, base, jnp.where(at < tokens + near, first_core, first_chip))
    skip = jnp.where(at < tokens, 0, jnp.where(at < tokens + near, tokens, tokens + near))
    k_tok = start * cols + at - skip
    k_row = start + (at - skip) // cols
    q_at = iota((tokens, 1), 0)
    q_line = q_at // cols
    q_tok = base * cols + q_at
    reach = jnp.zeros((tokens, 1), jnp.int32)
    for r in range(rows):
        reach = jnp.where(q_line == r, reach_ref[r], reach)
    inside = (k_row >= 0) & (k_row < grid_rows)
    allowed = (jnp.abs(k_row - (base + q_line)) <= reach) & inside & ((k_tok < count) | (k_tok == q_tok))
    parts = []
    for h in range(q_ref.shape[1] // ATT_HD):
        lanes = slice(h * ATT_HD, (h + 1) * ATT_HD)
        keys = jnp.concatenate([k_ref[:, lanes], core_ref[0, :, lanes], chip_ref[0, :, lanes]], 0)
        values = jnp.concatenate([v_ref[:, lanes], core_ref[1, :, lanes], chip_ref[1, :, lanes]], 0)
        scores = dot(q_ref[:, lanes], keys, 1, 1) * (1.0 / math.sqrt(ATT_HD))
        scores = jnp.where(allowed, scores, -1e30)
        powers = jnp.exp(scores - jnp.max(scores, -1, keepdims=True))
        weights = (powers / jnp.sum(powers, -1, keepdims=True)).astype(BF)
        parts.append(dot(weights, values).astype(BF).astype(F32))
    attended = jnp.concatenate(parts, 1)
    mean = jnp.mean(attended * attended, -1, keepdims=True)
    out_ref[0] = (attended * lax.rsqrt(mean + 1e-06)).astype(BF)
    diagonal = iota((tokens, tokens), 0) == iota((tokens, tokens), 1)
    rates = jnp.sum(jnp.where(diagonal, rate_ref[...], 0.0), 1, keepdims=True)
    valid = jnp.where(q_tok < count, 1.0, 0.0)
    out_ref[1] = (rates * valid * target_ref[...].astype(F32)).astype(BF)


def grads_kernel(n_plane, n_view, own_ref, other_ref, w1_ref, w3_ref, w2_ref, out_ref, old_ref):
    core = lax.axis_index("row_2")
    half = HD // 2
    share = half // n_plane
    few = share // n_view
    keys = jnp.concatenate([own_ref[0], other_ref[0]], 0)
    scaled = jnp.concatenate([own_ref[1], other_ref[1]], 0)
    first = dot(keys, w1_ref[...])
    third = dot(keys, w3_ref[...])
    back = dot(scaled, w2_ref[...], 1, 1)
    sig = jax.nn.sigmoid(first)
    silu = first * sig
    gated = silu * third
    back_first = (back * third * (sig * (1.0 + first * (1.0 - sig)))).astype(BF)
    back_third = (back * silu).astype(BF)
    gated_half = jnp.where(core == 0, gated[:, :half], gated[:, half:]).astype(BF)
    lanes = pl.ds(pl.multiple_of(core * half, half), half)
    keys_half = jnp.concatenate([own_ref[0, :, lanes], other_ref[0, :, lanes]], 0)
    for k, (a, b) in enumerate(((keys_half, back_first), (keys_half, back_third), (gated_half, scaled))):
        g = dot(a, b, 0, 0).astype(BF)
        out_ref[:, k * share : (k + 1) * share, :] = g.reshape(n_plane, share, HD)
    base = pl.multiple_of(core * half + lax.axis_index(PLANE) * share, share)
    at = lax.axis_index("view") * few
    r, c = iota((8, share), 0), iota((8, share), 1)
    old = jnp.zeros((8, HD), F32)
    for k, ref in enumerate((w1_ref, w3_ref, w2_ref)):
        pick = (r - k * few >= 0) & (r - k * few < few) & (c == at + r - k * few)
        old += dot(jnp.where(pick, 1.0, 0.0).astype(BF), ref[pl.ds(base, share), :])
    old_ref[...] = old


def spread_kernel(n_view, few, count_ref, x_ref, out_ref):
    total = jnp.sum(x_ref[...].astype(F32), 0).astype(BF)
    lines = total.shape[0]
    share = lines // 3
    o, i = iota((n_view * 8, lines), 0), iota((n_view * 8, lines), 1)
    r = o % 8
    pick = (r < 3 * few) & (i == (r // few) * share + (o // 8) * few + r % few)
    moved = dot(jnp.where(pick, 1.0, 0.0).astype(BF), total)
    count = count_ref[0]
    lane = iota(moved.shape, 1)
    digits = jnp.where(lane == 0, count % 16, jnp.where(lane == 1, (count // 16) % 16, count // 256))
    moved = jnp.where(iota(moved.shape, 0) % 8 == 3 * few, digits.astype(F32), moved)
    out_ref[...] = moved.astype(BF).reshape(n_view, 8, HD)


def renew_kernel(few, x_ref, old_ref, out_ref):
    summed = jnp.sum(x_ref[...].astype(F32), 0)
    last = summed[3 * few : 3 * few + 1]
    total = last[:, 0:1] + 16.0 * last[:, 1:2] + 256.0 * last[:, 2:3]
    old = old_ref[...]
    raised = old + summed / total
    rescale = jnp.sqrt(jnp.sum(old * old, -1, keepdims=True) + 1e-06) / jnp.sqrt(
        jnp.sum(raised * raised, -1, keepdims=True) + 1e-06
    )
    new = (raised * rescale).astype(BF)
    out_ref[...] = jnp.broadcast_to(new[None], out_ref.shape)


def order_kernel(few, x_ref, out_ref):
    n_view = x_ref.shape[0]
    lines = out_ref.shape[1]
    share = lines // 3
    i, o = iota((lines, n_view * 8), 0), iota((lines, n_view * 8), 1)
    r = o % 8
    pick = (r < 3 * few) & (i == (r // few) * share + (o // 8) * few + r % few)
    moved = dot(jnp.where(pick, 1.0, 0.0).astype(BF), x_ref[...].reshape(n_view * 8, HD)).astype(BF)
    out_ref[...] = jnp.broadcast_to(moved[None], out_ref.shape)


def apply_kernel(own_ref, mine_ref, theirs_ref, out_ref):
    core = lax.axis_index("row_2")
    half = HD // 2
    share = mine_ref.shape[1] // 3

    def matrix(ref, k):
        return ref[:, k * share : (k + 1) * share, :].reshape(half, HD)

    k_mine = own_ref[0, :, pl.ds(pl.multiple_of(core * half, half), half)]
    k_theirs = own_ref[0, :, pl.ds(pl.multiple_of((1 - core) * half, half), half)]
    first = dot(k_mine, matrix(mine_ref, 0)) + dot(k_theirs, matrix(theirs_ref, 0))
    third = dot(k_mine, matrix(mine_ref, 1)) + dot(k_theirs, matrix(theirs_ref, 1))
    applied = (first * jax.nn.sigmoid(first) * third).astype(BF)
    left, right = applied[:, :half], applied[:, half:]
    a_mine = jnp.where(core == 0, left.astype(F32), right.astype(F32)).astype(BF)
    a_theirs = jnp.where(core == 0, right.astype(F32), left.astype(F32)).astype(BF)
    out_ref[...] = (dot(a_mine, matrix(mine_ref, 2)) + dot(a_theirs, matrix(theirs_ref, 2))).astype(BF)


def per_device(query_feats, key_feats, value_feats, target, token_rates, row_reach, view_counts, w_first, w_third, w_second):
    _, rows, cols, width = query_feats.shape
    tokens, near = rows * cols, HALO * cols
    n_row, n_plane, n_view = lax.axis_size(ROW), lax.axis_size(PLANE), lax.axis_size("view")
    share = HD // 2 // n_plane
    few = share // n_view
    flat = lambda x: x.reshape(tokens, width)

    edge = (2, near, width)
    to_core, to_chip = call(edges_kernel, [edge, edge], [BF, BF], [VMEM] * 2)(flat(key_feats), flat(value_feats))
    next_chip = [p for i in range(1, n_row - 1, 2) for p in ((i, i + 1), (i + 1, i))]
    from_core = lax.ppermute(to_core, "row_2", SWAP)
    from_chip = lax.ppermute(to_chip, ROW, next_chip)

    attend = lambda *refs: attend_kernel(rows, cols, n_row * rows, *refs)
    own = call(attend, (2, tokens, width), BF, [SMEM] * 2 + [VMEM] * 7)(
        view_counts, row_reach, flat(query_feats), flat(key_feats), flat(value_feats), from_core, from_chip, flat(target), token_rates[0]
    )
    other = lax.ppermute(own, "row_2", SWAP)
    grads, old = call(lambda *refs: grads_kernel(n_plane, n_view, *refs), [(n_plane, 3 * share, width), (8, width)], [BF, F32], [VMEM] * 5)(
        own, other, w_first[0], w_third[0], w_second[0]
    )
    part = exchange(grads, PLANE)
    part = call(lambda *refs: spread_kernel(n_view, few, *refs), (n_view, 8, width), BF, [SMEM, VMEM])(view_counts, part)
    part = exchange(part, "view")
    new = call(lambda *refs: renew_kernel(few, *refs), (n_view, 8, width), BF, [VMEM] * 2)(part, old)
    new = exchange(new, "view")
    lines = call(lambda *refs: order_kernel(few, *refs), (n_plane, 3 * share, width), BF, [VMEM])(new)
    mine = exchange(lines, PLANE)
    theirs = lax.ppermute(mine, "row_2", SWAP)
    out = call(apply_kernel, (tokens, width), BF, [VMEM] * 3)(own, mine, theirs)
    return out.reshape(1, rows, cols, width)


def solution(mesh):
    torus = Mesh(
        mesh.devices.reshape(mesh.shape["head"], mesh.shape["view"], 2, 4, 2),
        ("head", "view", "row_0", "row_1", "row_2"),
    )
    feats = P("view", ROW, None, "head")
    heads = P("head", None, None)
    return jax.shard_map(
        per_device,
        mesh=torus,
        in_specs=(feats, feats, feats, feats, P("view", "head", ROW), P(ROW), P("view"), heads, heads, heads),
        out_specs=feats,
        check_vma=False,
    )
```

time: 110 us -> 106 us (0.964)
  blocking collectives: 17.5 us -> 69.2 us
  waiting for transfers between devices: 34 us -> 6.39 us
  starting transfers between devices: 38.2 us -> 19.3 us
  Pallas kernels: 0 us -> 4.71 us
  matrix products: 4.62 us -> 0 us
  other arithmetic: 4 us -> 0 us
  local copies, waits for them, and re-layouts: 7.73 us -> 4.7 us
  between operations: 3.15 us -> 0.74 us
    all_to_all x1 -> x4, blocking collectives: 17.5 us -> 69.2 us  [exchange(): return lax.all_to_all(x, axes, 0, 0, tiled=True)]
    all_to_all x3 -> x0, waiting for transfers between devices: 31.1 us -> none  [exchange(): return lax.all_to_all(x, axes, 0, 0, tiled=True)]
    all_to_all x3 -> x0, starting transfers between devices: 20.3 us -> none  [exchange(): return lax.all_to_all(x, axes, 0, 0, tiled=True)]
    pallas_call x0 -> x7, Pallas kernels: none -> 4.71 us  [the longest x1 1.89 us: per_device(): call(attend, (2, tokens, width), BF, [SMEM] * 2 + [VMEM] * 7)]
    dot_general x14 -> x0, matrix products: 4.31 us -> none  [the longest x12 3.75 us: dot(): lax.dot_general(a, b, (((ca,), (cb,)), ((), ())), preferred_element_type=...]
    ppermute x1, starting transfers between devices: 4.94 us -> 8.92 us  [per_device(): from_core = lax.ppermute(to_core, 'row_2', SWAP)]
    ppermute x1, waiting for transfers between devices: 0.01 us -> 3 us  [per_device(): from_chip = lax.ppermute(to_chip, ROW, next_chip)]
    ppermute x1, starting transfers between devices: 4.51 us -> 1.92 us  [per_device(): from_chip = lax.ppermute(to_chip, ROW, next_chip)]
  transfers between devices with their start and end apart: 7 -> 4, of which waited for: 5 -> 3; matrix products, arithmetic and copies ran while one was open for 4% -> 0% of each run, Pallas kernels for 0% -> 0%
where the time goes in v2:
time: 106 us; the launch traced here: 105 us
  blocking collectives  69.2 us (65%)
  starting transfers between devices  19.3 us (18%)
  waiting for transfers between devices  6.39 us (6%)
  Pallas kernels  4.71 us (4%)
  local copies, waits for them, and re-layouts  4.7 us (4%)
    all_to_all x4, blocking collectives, exchange(): return lax.all_to_all(x, axes, 0, 0, tiled=True)  69.2 us
    ppermute x1, starting transfers between devices, per_device(): from_core = lax.ppermute(to_core, 'row_2', SWAP)  8.92 us
    ppermute x1, starting transfers between devices, per_device(): theirs = lax.ppermute(mine, 'row_2', SWAP)  6.59 us
    unnamed x18, local copies, waits for them, and re-layouts  4.7 us
    ppermute x1, waiting for transfers between devices, per_device(): from_chip = lax.ppermute(to_chip, ROW, next_chip)  3 us
  transfers between devices with their start and end apart: 4, of which 3 were waited for; matrix products, arithmetic and copies ran while one was open for 0% of the time, Pallas kernels for 0%

profile of v2, /device:TPU:1, one launch (start us, length us, event | category | flops | bytes accessed | tf_op | source)
XLA Modules:
  0.0 105.1 jit_solution(12880940297144994836)
XLA Ops:
  0.0 0.0 copy-start.7
  0.0 0.0 copy-start.8
  0.0 0.9 copy-done
  0.9 0.0 copy-start.1
  0.9 0.9 copy-done.1
  1.8 0.0 copy-start.3
  1.9 0.0 copy-start.2
  1.9 8.9 %collective-permute-start = (bf16[2,32,512]{2,1,0:T(8,128)(2,1)S(1)}, bf16[2,32,512]{2,1,0:T(8,128)(2,1)S(1)}, u32[]{:S(2)}, u32[]{:S(2)}) collective-permute-start(bf16[2,32,512]{2,1,0:T(8,128)(2,1)S(1)} %get-tuple-element.9), channel_id=1, source_target_pairs={{0,1},{1,0},{2,3},{3,2},{4,5},{5,4},{6,7},{7,6},{8,9},{9,8},{10,11... | collective-permute-start | bytes 196616 | tf_op jit(solution)/shard_map/ppermute | solution.py:201
  10.8 1.9 %collective-permute-start.1 = (bf16[2,32,512]{2,1,0:T(8,128)(2,1)S(1)}, bf16[2,32,512]{2,1,0:T(8,128)(2,1)S(1)}, u32[]{:S(2)}, u32[]{:S(2)}) collective-permute-start(bf16[2,32,512]{2,1,0:T(8,128)(2,1)S(1)} %get-tuple-element.10), channel_id=1, source_target_pairs={{1,2},{2,1},{3,4},{4,3},{5,6},{6,5},{7,8},{8,7},{9,10},{10,9},{11,... | collective-permute-start | bytes 196616 | tf_op jit(solution)/shard_map/ppermute | solution.py:202
  13.4 0.0 collective-permute-done.refs_5_
  13.4 3.0 %collective-permute-done.1.refs_6_ = bf16[2,32,512]{2,1,0:T(8,128)(2,1)S(1)} collective-permute-done((bf16[2,32,512]{2,1,0:T(8,128)(2,1)S(1)}, bf16[2,32,512]{2,1,0:T(8,128)(2,1)S(1)}, u32[]{:S(2)}, u32[]{:S(2)}) %collective-permute-start.1) | collective-permute-done | bytes 65568 | tf_op jit(solution)/shard_map/ppermute | solution.py:202
  16.4 0.0 copy-done.7
  16.4 0.0 copy-done.8
  16.4 0.9 copy-done.5
  17.3 0.9 copy-done.6
  18.2 1.9 %shard_map.101.refs_0_.own_ref = bf16[2,128,512]{2,1,0:T(8,128)(2,1)S(1)} custom-call(s32[1]{0:T(128)S(6)} %copy.11.refs_0_, s32[8]{0:T(128)S(1)} %copy-done.7, bf16[128,512]{1,0:T(8,128)(2,1)S(1)} %bitcast.16, bf16[128,512]{1,0:T(8,128)(2,1)S(1)} %bitcast.10, bf16[128,512]{1,0:T(8,128)(2,1)S(1)} %bitcast.12, ...), custom_call_target="tpu_custom_call" | custom-call | flops 1048576 | bytes 1048576 | tf_op jit(solution)/shard_map/pallas_call | solution.py:205
  20.1 1.9 %collective-permute-start.2 = (bf16[2,128,512]{2,1,0:T(8,128)(2,1)S(1)}, bf16[2,128,512]{2,1,0:T(8,128)(2,1)S(1)}, u32[]{:S(2)}, u32[]{:S(2)}) collective-permute-start(bf16[2,128,512]{2,1,0:T(8,128)(2,1)S(1)} %shard_map.101.refs_0_.own_ref), channel_id=1, source_target_pairs={{0,1},{1,0},{2,3},{3,2},{4,5},{5,4},{6,7},{7,6},{8,9},{9,8},{10,11... | collective-permute-start | bytes 786440 | tf_op jit(solution)/shard_map/ppermute | solution.py:208
  22.0 1.5 %collective-permute-done.2.refs_1_ = bf16[2,128,512]{2,1,0:T(8,128)(2,1)S(1)} collective-permute-done((bf16[2,128,512]{2,1,0:T(8,128)(2,1)S(1)}, bf16[2,128,512]{2,1,0:T(8,128)(2,1)S(1)}, u32[]{:S(2)}, u32[]{:S(2)}) %collective-permute-start.2) | collective-permute-done | bytes 262176 | tf_op jit(solution)/shard_map/ppermute | solution.py:208
  23.5 0.0 copy-done.3
  23.5 0.0 copy-done.2
  23.5 1.0 copy-done.4
  24.6 1.0 shard_map.102
  25.6 15.5 %all_to_all.20.refs_1_ = bf16[8,96,512]{2,1,0:T(8,128)(2,1)S(1)} all-to-all(bf16[8,96,512]{2,1,0:T(8,128)(2,1)S(1)} %get-tuple-element.11), channel_id=1, replica_groups=mesh['head'=2,'view'=16,'row_0'=2,'row_1'=4,'row_2'=2] {'row_0','row_1'}, dimensions={0} | all-to-all | bytes 1572864 | tf_op jit(solution)/shard_map/all_to_all | solution.py:28
  41.1 0.3 shard_map.103
  41.4 24.5 %all_to_all.21.refs_0_ = bf16[16,8,512]{2,1,0:T(8,128)(2,1)S(1)} all-to-all(bf16[16,8,512]{2,1,0:T(8,128)(2,1)S(1)} %shard_map.103), channel_id=1, replica_groups=mesh['head'=2,'view'=16,'row_0'=2,'row_1'=4,'row_2'=2] {'view'}, dimensions={0} | all-to-all | bytes 262144 | tf_op jit(solution)/shard_map/all_to_all | solution.py:28
  65.8 0.2 shard_map.104
  66.1 17.5 %all_to_all.22.refs_0_ = bf16[16,8,512]{2,1,0:T(8,128)(2,1)S(1)} all-to-all(bf16[16,8,512]{2,1,0:T(8,128)(2,1)S(1)} %shard_map.104), channel_id=1, replica_groups=mesh['head'=2,'view'=16,'row_0'=2,'row_1'=4,'row_2'=2] {'view'}, dimensions={0} | all-to-all | bytes 262144 | tf_op jit(solution)/shard_map/all_to_all | solution.py:28
  83.6 0.2 shard_map.105
  83.8 11.6 %all_to_all.23.mine_ref = bf16[8,96,512]{2,1,0:T(8,128)(2,1)S(1)} all-to-all(bf16[8,96,512]{2,1,0:T(8,128)(2,1)S(1)} %shard_map.105), channel_id=1, replica_groups=mesh['head'=2,'view'=16,'row_0'=2,'row_1'=4,'row_2'=2] {'row_0','row_1'}, dimensions={0} | all-to-all | bytes 1572864 | tf_op jit(solution)/shard_map/all_to_all | solution.py:28
  95.4 6.6 %collective-permute-start.3 = (bf16[8,96,512]{2,1,0:T(8,128)(2,1)S(1)}, bf16[8,96,512]{2,1,0:T(8,128)(2,1)S(1)}, u32[]{:S(2)}, u32[]{:S(2)}) collective-permute-start(bf16[8,96,512]{2,1,0:T(8,128)(2,1)S(1)} %all_to_all.23.mine_ref), channel_id=1, source_target_pairs={{0,1},{1,0},{2,3},{3,2},{4,5},{5,4},{6,7},{7,6},{8,9},{9,8},{10,11... | collective-permute-start | bytes 2359304 | tf_op jit(solution)/shard_map/ppermute | solution.py:219
  102.0 1.9 %collective-permute-done.3.theirs_ref = bf16[8,96,512]{2,1,0:T(8,128)(2,1)S(1)} collective-permute-done((bf16[8,96,512]{2,1,0:T(8,128)(2,1)S(1)}, bf16[8,96,512]{2,1,0:T(8,128)(2,1)S(1)}, u32[]{:S(2)}, u32[]{:S(2)}) %collective-permute-start.3) | collective-permute-done | bytes 786464 | tf_op jit(solution)/shard_map/ppermute | solution.py:219
  103.9 1.1 %shard_map.106 = bf16[128,512]{1,0:T(8,128)(2,1)} custom-call(bf16[2,128,512]{2,1,0:T(8,128)(2,1)S(1)} %shard_map.101.refs_0_.own_ref, bf16[8,96,512]{2,1,0:T(8,128)(2,1)S(1)} %all_to_all.23.mine_ref, bf16[8,96,512]{2,1,0:T(8,128)(2,1)S(1)} %collective-permute-done.3.theirs_ref), custom_call_target="tpu_custom_call" | custom-call | flops 1048576 | bytes 1048576 | tf_op jit(solution)/shard_map/pallas_call | solution.py:220
  (5 shorter events, 0.0 us)
Async XLA Ops:
  0.0 16.4 %copy-start.7 = (s32[8]{0:T(128)S(1)}, s32[8]{0:T(128)}, u32[]{:S(2)}) copy-start(s32[8]{0:T(128)} %refs_1_.1) | copy-start | bytes 100
  0.0 16.4 %copy-start.8 = (f32[1,1,128]{2,1,0:T(1,128)S(1)}, f32[1,1,128]{2,1,0:T(1,128)}, u32[]{:S(2)}) copy-start(f32[1,1,128]{2,1,0:T(1,128)} %param.14) | copy-start | bytes 1540
  0.0 0.9 copy-start
  0.9 0.9 copy-start.1
  1.8 21.7 %copy-start.3 = (bf16[1,512,512]{2,1,0:T(8,128)(2,1)S(1)}, bf16[1,512,512]{2,1,0:T(8,128)(2,1)}, u32[]{:S(2)}) copy-start(bf16[1,512,512]{2,1,0:T(8,128)(2,1)} %param.18) | copy-start | bytes 1572868
  1.9 21.7 %copy-start.2 = (bf16[1,512,512]{2,1,0:T(8,128)(2,1)S(1)}, bf16[1,512,512]{2,1,0:T(8,128)(2,1)}, u32[]{:S(2)}) copy-start(bf16[1,512,512]{2,1,0:T(8,128)(2,1)} %param.17) | copy-start | bytes 1572868
  1.9 11.5 %collective-permute-start = (bf16[2,32,512]{2,1,0:T(8,128)(2,1)S(1)}, bf16[2,32,512]{2,1,0:T(8,128)(2,1)S(1)}, u32[]{:S(2)}, u32[]{:S(2)}) collective-permute-start(bf16[2,32,512]{2,1,0:T(8,128)(2,1)S(1)} %get-tuple-element.9), channel_id=1, source_target_pairs={{0,1},{1,0},{2,3},{3,2},{4,5},{5,4},{6,7},{7,6},{8,9},{9,8},{10,11... | collective-permute-start | bytes 196616 | tf_op jit(solution)/shard_map/ppermute | solution.py:201
  10.8 5.6 %collective-permute-start.1 = (bf16[2,32,512]{2,1,0:T(8,128)(2,1)S(1)}, bf16[2,32,512]{2,1,0:T(8,128)(2,1)S(1)}, u32[]{:S(2)}, u32[]{:S(2)}) collective-permute-start(bf16[2,32,512]{2,1,0:T(8,128)(2,1)S(1)} %get-tuple-element.10), channel_id=1, source_target_pairs={{1,2},{2,1},{3,4},{4,3},{5,6},{6,5},{7,8},{8,7},{9,10},{10,9},{11,... | collective-permute-start | bytes 196616 | tf_op jit(solution)/shard_map/ppermute | solution.py:202
  16.4 0.9 copy-start.5
  17.3 0.9 copy-start.6
  20.1 3.4 %collective-permute-start.2 = (bf16[2,128,512]{2,1,0:T(8,128)(2,1)S(1)}, bf16[2,128,512]{2,1,0:T(8,128)(2,1)S(1)}, u32[]{:S(2)}, u32[]{:S(2)}) collective-permute-start(bf16[2,128,512]{2,1,0:T(8,128)(2,1)S(1)} %shard_map.101.refs_0_.own_ref), channel_id=1, source_target_pairs={{0,1},{1,0},{2,3},{3,2},{4,5},{5,4},{6,7},{7,6},{8,9},{9,8},{10,11... | collective-permute-start | bytes 786440 | tf_op jit(solution)/shard_map/ppermute | solution.py:208
  23.5 1.0 copy-start.4
  95.4 8.5 %collective-permute-start.3 = (bf16[8,96,512]{2,1,0:T(8,128)(2,1)S(1)}, bf16[8,96,512]{2,1,0:T(8,128)(2,1)S(1)}, u32[]{:S(2)}, u32[]{:S(2)}) collective-permute-start(bf16[8,96,512]{2,1,0:T(8,128)(2,1)S(1)} %all_to_all.23.mine_ref), channel_id=1, source_target_pairs={{0,1},{1,0},{2,3},{3,2},{4,5},{5,4},{6,7},{7,6},{8,9},{9,8},{10,11... | collective-permute-start | bytes 2359304 | tf_op jit(solution)/shard_map/ppermute | solution.py:219

commit v3 on v2

v3 whole, which is shorter than its diff:
```python
import math

import jax
import jax.numpy as jnp
from jax import lax
from jax.experimental import pallas as pl
from jax.experimental.pallas import tpu as pltpu
from jax.sharding import Mesh
from jax.sharding import PartitionSpec as P

HD = 512
ATT_HD = 128
HALO = 2
PLANE = ("row_0", "row_1")
ROW = ("row_0", "row_1", "row_2")
SWAP = [(0, 1), (1, 0)]
BF = jnp.bfloat16
F32 = jnp.float32
VMEM = pl.BlockSpec(memory_space=pltpu.VMEM)
SMEM = pl.BlockSpec(memory_space=pltpu.SMEM)
HBM = pl.BlockSpec(memory_space=pltpu.HBM)


def dot(a, b, ca=1, cb=0):
    return lax.dot_general(a, b, (((ca,), (cb,)), ((), ())), preferred_element_type=F32)


def exchange(x, axes):
    return lax.all_to_all(x, axes, 0, 0, tiled=True)


def iota(shape, dim):
    return lax.broadcasted_iota(jnp.int32, shape, dim)


def call(kernel, shapes, specs, copies=0):
    many = isinstance(shapes, list)
    outs = [jax.ShapeDtypeStruct(*s) for s in shapes] if many else jax.ShapeDtypeStruct(*shapes)
    return pl.pallas_call(
        kernel,
        out_shape=outs,
        in_specs=specs,
        out_specs=[VMEM] * len(shapes) if many else VMEM,
        scratch_shapes=[pltpu.SemaphoreType.DMA((copies,))] if copies else [],
        compiler_params=pltpu.CompilerParams(vmem_limit_bytes=24 << 20),
        cost_estimate=pl.CostEstimate(flops=1 << 20, bytes_accessed=1 << 20, transcendentals=0),
    )


def edges_kernel(q_in, k_in, v_in, t_in, q_ref, k_ref, v_ref, t_ref, core_ref, chip_ref, sems):
    core = lax.axis_index("row_2")
    near = HALO * 16
    end = k_in.shape[0] - near
    to_core = pl.ds(pl.multiple_of((1 - core) * end, near), near)
    to_chip = pl.ds(pl.multiple_of(core * end, near), near)
    pairs = []
    for i, ref in enumerate((k_in, v_in)):
        pairs += [(ref.at[to_core], core_ref.at[i]), (ref.at[to_chip], chip_ref.at[i])]
    pairs += [(k_in, k_ref), (v_in, v_ref), (q_in, q_ref), (t_in, t_ref)]
    copies = [pltpu.make_async_copy(a, b, sems.at[n]) for n, (a, b) in enumerate(pairs)]
    for c in copies:
        c.start()
    for c in copies:
        c.wait()


def attend_kernel(rows, cols, grid_rows, count_ref, reach_ref, q_ref, k_ref, v_ref, core_ref, chip_ref, target_ref, rate_ref, w1_in, w3_in, w2_in, out_ref, w1_ref, w3_ref, w2_ref, sems):
    copies = [
        pltpu.make_async_copy(a, b, sems.at[n])
        for n, (a, b) in enumerate(((w1_in, w1_ref), (w3_in, w3_ref), (w2_in, w2_ref)))
    ]
    for c in copies:
        c.start()
    core = lax.axis_index("row_2")
    base = lax.axis_index(ROW) * rows
    count = count_ref[0]
    tokens, near = rows * cols, HALO * cols
    span = tokens + 2 * near
    at = iota((1, span), 1)
    below, above = base + rows, base - HALO
    first_core = jnp.where(core == 0, below, above)
    first_chip = jnp.where(core == 0, above, below)
    start = jnp.where(at < tokens, base, jnp.where(at < tokens + near, first_core, first_chip))
    skip = jnp.where(at < tokens, 0, jnp.where(at < tokens + near, tokens, tokens + near))
    k_tok = start * cols + at - skip
    k_row = start + (at - skip) // cols
    q_at = iota((tokens, 1), 0)
    q_line = q_at // cols
    q_tok = base * cols + q_at
    reach = jnp.zeros((tokens, 1), jnp.int32)
    for r in range(rows):
        reach = jnp.where(q_line == r, reach_ref[r], reach)
    inside = (k_row >= 0) & (k_row < grid_rows)
    allowed = (jnp.abs(k_row - (base + q_line)) <= reach) & inside & ((k_tok < count) | (k_tok == q_tok))
    parts = []
    for h in range(q_ref.shape[1] // ATT_HD):
        lanes = slice(h * ATT_HD, (h + 1) * ATT_HD)
        keys = jnp.concatenate([k_ref[:, lanes], core_ref[0, :, lanes], chip_ref[0, :, lanes]], 0)
        values = jnp.concatenate([v_ref[:, lanes], core_ref[1, :, lanes], chip_ref[1, :, lanes]], 0)
        scores = dot(q_ref[:, lanes], keys, 1, 1) * (1.0 / math.sqrt(ATT_HD))
        scores = jnp.where(allowed, scores, -1e30)
        powers = jnp.exp(scores - jnp.max(scores, -1, keepdims=True))
        weights = (powers / jnp.sum(powers, -1, keepdims=True)).astype(BF)
        parts.append(dot(weights, values).astype(BF).astype(F32))
    attended = jnp.concatenate(parts, 1)
    mean = jnp.mean(attended * attended, -1, keepdims=True)
    out_ref[0] = (attended * lax.rsqrt(mean + 1e-06)).astype(BF)
    diagonal = iota((tokens, tokens), 0) == iota((tokens, tokens), 1)
    rates = jnp.sum(jnp.where(diagonal, rate_ref[...], 0.0), 1, keepdims=True)
    valid = jnp.where(q_tok < count, 1.0, 0.0)
    out_ref[1] = (rates * valid * target_ref[...].astype(F32)).astype(BF)
    for c in copies:
        c.wait()


def grads_kernel(n_plane, n_near, own_ref, other_ref, w1_ref, w3_ref, w2_ref, out_ref, old_ref):
    core = lax.axis_index("row_2")
    half = HD // 2
    share = half // n_plane
    few = share // n_near
    keys = jnp.concatenate([own_ref[0], other_ref[0]], 0)
    scaled = jnp.concatenate([own_ref[1], other_ref[1]], 0)
    first = dot(keys, w1_ref[...])
    third = dot(keys, w3_ref[...])
    back = dot(scaled, w2_ref[...], 1, 1)
    sig = jax.nn.sigmoid(first)
    silu = first * sig
    gated = silu * third
    back_first = (back * third * (sig * (1.0 + first * (1.0 - sig)))).astype(BF)
    back_third = (back * silu).astype(BF)
    gated_half = jnp.where(core == 0, gated[:, :half], gated[:, half:]).astype(BF)
    lanes = pl.ds(pl.multiple_of(core * half, half), half)
    keys_half = jnp.concatenate([own_ref[0, :, lanes], other_ref[0, :, lanes]], 0)
    for k, (a, b) in enumerate(((keys_half, back_first), (keys_half, back_third), (gated_half, scaled))):
        g = dot(a, b, 0, 0).astype(BF)
        out_ref[:, k * share : (k + 1) * share, :] = g.reshape(n_plane, share, HD)
    base = pl.multiple_of(core * half + lax.axis_index(PLANE) * share, share)
    at = lax.axis_index("near") * few
    pick = jnp.where(iota((few, share), 1) == at + iota((few, share), 0), 1.0, 0.0).astype(BF)
    for k, ref in enumerate((w1_ref, w3_ref, w2_ref)):
        old_ref[:, k * HD : (k + 1) * HD] = dot(pick, ref[pl.ds(base, share), :])


def spread_kernel(n_near, few, count_ref, x_ref, out_ref):
    total = jnp.sum(x_ref[...].astype(F32), 0)
    share = total.shape[0] // 3
    for k in range(3):
        for u in range(n_near):
            at = k * share + u * few
            out_ref[u, :, k * HD : (k + 1) * HD] = total[at : at + few].astype(BF)
    count = count_ref[0]
    lane = iota((few, 128), 1)
    digits = jnp.where(lane == 0, count % 16, jnp.where(lane == 1, (count // 16) % 16, count // 256))
    digits = digits.astype(F32).astype(BF)
    for u in range(n_near):
        out_ref[u, :, 3 * HD :] = digits


def gather_kernel(x_ref, out_ref):
    total = jnp.sum(x_ref[...].astype(F32), 0).astype(BF)
    out_ref[...] = jnp.broadcast_to(total[None], out_ref.shape)


def renew_kernel(x_ref, old_ref, out_ref):
    summed = jnp.sum(x_ref[...].astype(F32), 0)
    last = summed[0:1, 3 * HD :]
    total = last[:, 0:1] + 16.0 * last[:, 1:2] + 256.0 * last[:, 2:3]
    for k in range(3):
        lanes = slice(k * HD, (k + 1) * HD)
        old = old_ref[:, lanes]
        raised = old + summed[:, lanes] / total
        rescale = jnp.sqrt(jnp.sum(old * old, -1, keepdims=True) + 1e-06) / jnp.sqrt(
            jnp.sum(raised * raised, -1, keepdims=True) + 1e-06
        )
        new = (raised * rescale).astype(BF)
        for u in range(out_ref.shape[0]):
            out_ref[u, :, lanes] = new


def order_kernel(x_ref, out_ref):
    n_near = x_ref.shape[0]
    x = x_ref[...].astype(F32)
    lines = jnp.concatenate([x[u, :, k * HD : (k + 1) * HD] for k in range(3) for u in range(n_near)], 0).astype(BF)
    out_ref[...] = jnp.broadcast_to(lines[None], out_ref.shape)


def apply_kernel(own_ref, mine_ref, theirs_ref, out_ref):
    core = lax.axis_index("row_2")
    half = HD // 2
    share = mine_ref.shape[1] // 3

    def matrix(ref, k):
        return ref[:, k * share : (k + 1) * share, :].reshape(half, HD)

    k_mine = own_ref[0, :, pl.ds(pl.multiple_of(core * half, half), half)]
    k_theirs = own_ref[0, :, pl.ds(pl.multiple_of((1 - core) * half, half), half)]
    first = dot(k_mine, matrix(mine_ref, 0)) + dot(k_theirs, matrix(theirs_ref, 0))
    third = dot(k_mine, matrix(mine_ref, 1)) + dot(k_theirs, matrix(theirs_ref, 1))
    applied = (first * jax.nn.sigmoid(first) * third).astype(BF)
    left, right = applied[:, :half], applied[:, half:]
    a_mine = jnp.where(core == 0, left.astype(F32), right.astype(F32)).astype(BF)
    a_theirs = jnp.where(core == 0, right.astype(F32), left.astype(F32)).astype(BF)
    out_ref[...] = (dot(a_mine, matrix(mine_ref, 2)) + dot(a_theirs, matrix(theirs_ref, 2))).astype(BF)


def per_device(query_feats, key_feats, value_feats, target, token_rates, row_reach, view_counts, w_first, w_third, w_second):
    _, rows, cols, width = query_feats.shape
    tokens, near = rows * cols, HALO * cols
    n_row, n_plane, n_near, n_far = (lax.axis_size(axes) for axes in (ROW, PLANE, "near", "far"))
    share = HD // 2 // n_plane
    few = share // n_near
    flat = lambda x: x.reshape(tokens, width)
    in_hbm = lambda x: pltpu.with_memory_space_constraint(x, pltpu.HBM)

    block, edge, matrix = ((tokens, width), BF), ((2, near, width), BF), ((HD, HD), BF)
    query, key, value, aim, to_core, to_chip = call(edges_kernel, [block] * 4 + [edge] * 2, [HBM] * 4, 8)(
        *(in_hbm(flat(x)) for x in (query_feats, key_feats, value_feats, target))
    )
    next_chip = [p for i in range(1, n_row - 1, 2) for p in ((i, i + 1), (i + 1, i))]
    from_core = lax.ppermute(to_core, "row_2", SWAP)
    from_chip = lax.ppermute(to_chip, ROW, next_chip)

    attend = lambda *refs: attend_kernel(rows, cols, n_row * rows, *refs)
    own, w1, w3, w2 = call(attend, [((2, tokens, width), BF)] + [matrix] * 3, [SMEM] * 2 + [VMEM] * 7 + [HBM] * 3, 3)(
        view_counts, row_reach, query, key, value, from_core, from_chip, aim, token_rates[0], *(in_hbm(w[0]) for w in (w_first, w_third, w_second))
    )
    other = lax.ppermute(own, "row_2", SWAP)
    grads = lambda *refs: grads_kernel(n_plane, n_near, *refs)
    part, old = call(grads, [((n_plane, 3 * share, width), BF), ((few, 3 * width), F32)], [VMEM] * 5)(own, other, w1, w3, w2)
    part = exchange(part, PLANE)
    spread = lambda *refs: spread_kernel(n_near, few, *refs)
    part = call(spread, ((n_near, few, 3 * width + 128), BF), [SMEM, VMEM])(view_counts, part)
    part = exchange(part, "near")
    part = call(gather_kernel, ((n_far, few, 3 * width + 128), BF), [VMEM])(part)
    part = exchange(part, "far")
    new = call(renew_kernel, ((n_near, few, 3 * width), BF), [VMEM] * 2)(part, old)
    new = exchange(new, "near")
    lines = call(order_kernel, ((n_plane, 3 * share, width), BF), [VMEM])(new)
    mine = exchange(lines, PLANE)
    theirs = lax.ppermute(mine, "row_2", SWAP)
    out = call(apply_kernel, ((tokens, width), BF), [VMEM] * 3)(own, mine, theirs)
    return out.reshape(1, rows, cols, width)


def solution(mesh):
    torus = Mesh(
        mesh.devices.reshape(mesh.shape["head"], mesh.shape["view"] // 4, 4, 2, 4, 2),
        ("head", "far", "near", "row_0", "row_1", "row_2"),
    )
    views = ("far", "near")
    feats = P(views, ROW, None, "head")
    heads = P("head", None, None)
    return jax.shard_map(
        per_device,
        mesh=torus,
        in_specs=(feats, feats, feats, feats, P(views, "head", ROW), P(ROW), P(views), heads, heads, heads),
        out_specs=feats,
        check_vma=False,
    )
```

time: 106 us -> 102 us (0.962)
  local copies, waits for them, and re-layouts: 4.7 us -> 0.67 us
  blocking collectives: 69.2 us -> 66.1 us
  Pallas kernels: 4.71 us -> 6.61 us
  starting transfers between devices: 19.3 us -> 21.2 us
    unnamed x18 -> x4, local copies, waits for them, and re-layouts: 4.7 us -> 0.67 us
    all_to_all x4 -> x5, blocking collectives: 69.2 us -> 66.1 us  [exchange(): return lax.all_to_all(x, axes, 0, 0, tiled=True)]
    ppermute x1, starting transfers between devices: 6.59 us -> 8.57 us  [per_device(): theirs = lax.ppermute(mine, 'row_2', SWAP)]
    pallas_call x7 -> x8, Pallas kernels: 4.71 us -> 6.61 us  [the longest x1 2.87 us: per_device(): call(attend, [((2, tokens, width), BF)] + [matrix] * 3, [SMEM] * 2 + [VME...]
where the time goes in v3:
time: 102 us
  blocking collectives  66.1 us (65%)
  starting transfers between devices  21.2 us (21%)
  Pallas kernels  6.61 us (6%)
  waiting for transfers between devices  6.39 us (6%)
    all_to_all x5, blocking collectives, exchange(): return lax.all_to_all(x, axes, 0, 0, tiled=True)  66.1 us
    ppermute x1, starting transfers between devices, per_device(): from_core = lax.ppermute(to_core, 'row_2', SWAP)  8.79 us
    ppermute x1, starting transfers between devices, per_device(): theirs = lax.ppermute(mine, 'row_2', SWAP)  8.57 us
    ppermute x1, waiting for transfers between devices, per_device(): from_chip = lax.ppermute(to_chip, ROW, next_chip)  3 us
    pallas_call x1, Pallas kernels, per_device(): call(attend, [((2, tokens, width), BF)] + [matrix] * 3, [SMEM] * 2 + [VME...  2.87 us
  transfers between devices with their start and end apart: 4, of which 3 were waited for; matrix products, arithmetic and copies ran while one was open for 0% of the time, Pallas kernels for 0%

profile of v3, /device:TPU:1, one launch (start us, length us, event | category | flops | bytes accessed | tf_op | source)
XLA Modules:
  0.0 101.7 jit_solution(10410262765686826466)
XLA Ops:
  0.0 1.2 %shard_map.100 = (bf16[128,512]{1,0:T(8,128)(2,1)S(1)}, bf16[128,512]{1,0:T(8,128)(2,1)S(1)}, bf16[128,512]{1,0:T(8,128)(2,1)S(1)}, bf16[128,512]{1,0:T(8,128)(2...) custom-call(bf16[128,512]{1,0:T(8,128)(2,1)} %bitcast.13, bf16[128,512]{1,0:T(8,128)(2,1)} %bitcast.14, ...), custom_call_target="tpu_custom_call" | custom-call | flops 1048576 | bytes 1048576 | tf_op jit(solution)/shard_map/pallas_call | solution.py:216
  1.2 8.8 %collective-permute-start = (bf16[2,32,512]{2,1,0:T(8,128)(2,1)S(1)}, bf16[2,32,512]{2,1,0:T(8,128)(2,1)S(1)}, u32[]{:S(2)}, u32[]{:S(2)}) collective-permute-start(bf16[2,32,512]{2,1,0:T(8,128)(2,1)S(1)} %get-tuple-element.20), channel_id=1, source_target_pairs={{0,1},{1,0},{2,3},{3,2},{4,5},{5,4},{6,7},{7,6},{8,9},{9,8},{10,11... | collective-permute-start | bytes 196616 | tf_op jit(solution)/shard_map/ppermute | solution.py:220
  10.0 1.9 %collective-permute-start.1 = (bf16[2,32,512]{2,1,0:T(8,128)(2,1)S(1)}, bf16[2,32,512]{2,1,0:T(8,128)(2,1)S(1)}, u32[]{:S(2)}, u32[]{:S(2)}) collective-permute-start(bf16[2,32,512]{2,1,0:T(8,128)(2,1)S(1)} %get-tuple-element.21), channel_id=1, source_target_pairs={{1,2},{2,1},{3,4},{4,3},{5,6},{6,5},{7,8},{8,7},{9,10},{10,9},{11,... | collective-permute-start | bytes 196616 | tf_op jit(solution)/shard_map/ppermute | solution.py:221
  12.6 0.0 collective-permute-done.refs_5_
  12.6 3.0 %collective-permute-done.1.refs_6_ = bf16[2,32,512]{2,1,0:T(8,128)(2,1)S(1)} collective-permute-done((bf16[2,32,512]{2,1,0:T(8,128)(2,1)S(1)}, bf16[2,32,512]{2,1,0:T(8,128)(2,1)S(1)}, u32[]{:S(2)}, u32[]{:S(2)}) %collective-permute-start.1) | collective-permute-done | bytes 65568 | tf_op jit(solution)/shard_map/ppermute | solution.py:221
  15.6 0.0 copy-start
  15.6 0.0 copy-start.1
  15.6 0.7 copy-done
  16.3 0.0 copy-done.1
  16.3 2.9 %shard_map.101 = (bf16[2,128,512]{2,1,0:T(8,128)(2,1)S(1)}, bf16[512,512]{1,0:T(8,128)(2,1)S(1)}, bf16[512,512]{1,0:T(8,128)(2,1)S(1)}, bf16[512,512]{1,0:T(8,128)(2,1)S(1)}) custom-call(s32[1]{0:T(128)S(6)} %copy.11.refs_0_, s32[8]{0:T(128)S(1)} %copy-done, bf16[128,512]{1,0:T(8,128)(2,1)S(1)} %get-tuple-element.17.refs_2_, ...), custom_call_target="tpu_custom_call" | custom-call | flops 1048576 | bytes 1048576 | tf_op jit(solution)/shard_map/pallas_call | solution.py:224
  19.2 1.9 %collective-permute-start.2 = (bf16[2,128,512]{2,1,0:T(8,128)(2,1)S(1)}, bf16[2,128,512]{2,1,0:T(8,128)(2,1)S(1)}, u32[]{:S(2)}, u32[]{:S(2)}) collective-permute-start(bf16[2,128,512]{2,1,0:T(8,128)(2,1)S(1)} %get-tuple-element.23.refs_0_.own_ref), channel_id=1, source_target_pairs={{0,1},{1,0},{2,3},{3,2},{4,5},{5,4},{6,7},{7,6},{8,9},{9,8},{10,11... | collective-permute-start | bytes 786440 | tf_op jit(solution)/shard_map/ppermute | solution.py:227
  21.1 1.5 %collective-permute-done.2.refs_1_ = bf16[2,128,512]{2,1,0:T(8,128)(2,1)S(1)} collective-permute-done((bf16[2,128,512]{2,1,0:T(8,128)(2,1)S(1)}, bf16[2,128,512]{2,1,0:T(8,128)(2,1)S(1)}, u32[]{:S(2)}, u32[]{:S(2)}) %collective-permute-start.2) | collective-permute-done | bytes 262176 | tf_op jit(solution)/shard_map/ppermute | solution.py:227
  22.6 1.0 shard_map.102
  23.6 15.5 %all_to_all.25.refs_1_ = bf16[8,96,512]{2,1,0:T(8,128)(2,1)S(1)} all-to-all(bf16[8,96,512]{2,1,0:T(8,128)(2,1)S(1)} %get-tuple-element.27), channel_id=1, replica_groups=mesh['head'=2,'far'=4,'near'=4,'row_0'=2,'row_1'=4,'row_2'=2] {'row_0','..., dimensions={0} | all-to-all | bytes 1572864 | tf_op jit(solution)/shard_map/all_to_all | solution.py:29
  39.1 0.1 shard_map.103
  39.2 7.9 %all_to_all.26.x_ref = bf16[4,8,1664]{2,1,0:T(8,128)(2,1)S(1)} all-to-all(bf16[4,8,1664]{2,1,0:T(8,128)(2,1)S(1)} %shard_map.103), channel_id=1, replica_groups=mesh['head'=2,'far'=4,'near'=4,'row_0'=2,'row_1'=4,'row_2'=2] {'near'}, dimensions={0} | all-to-all | bytes 212992 | tf_op jit(solution)/shard_map/all_to_all | solution.py:29
  47.2 23.8 %all_to_all.27.x_ref = bf16[4,8,1664]{2,1,0:T(8,128)(2,1)S(1)} all-to-all(bf16[4,8,1664]{2,1,0:T(8,128)(2,1)S(1)} %shard_map.104), channel_id=1, replica_groups=mesh['head'=2,'far'=4,'near'=4,'row_0'=2,'row_1'=4,'row_2'=2] {'far'}, dimensions={0} | all-to-all | bytes 212992 | tf_op jit(solution)/shard_map/all_to_all | solution.py:29
  71.0 0.2 shard_map.105
  71.2 7.4 %all_to_all.28.x_ref = bf16[4,8,1536]{2,1,0:T(8,128)(2,1)S(1)} all-to-all(bf16[4,8,1536]{2,1,0:T(8,128)(2,1)S(1)} %shard_map.105), channel_id=1, replica_groups=mesh['head'=2,'far'=4,'near'=4,'row_0'=2,'row_1'=4,'row_2'=2] {'near'}, dimensions={0} | all-to-all | bytes 196608 | tf_op jit(solution)/shard_map/all_to_all | solution.py:29
  78.7 0.1 shard_map.106
  78.7 11.4 %all_to_all.29.mine_ref = bf16[8,96,512]{2,1,0:T(8,128)(2,1)S(1)} all-to-all(bf16[8,96,512]{2,1,0:T(8,128)(2,1)S(1)} %shard_map.106), channel_id=1, replica_groups=mesh['head'=2,'far'=4,'near'=4,'row_0'=2,'row_1'=4,'row_2'=2] {'row_0','..., dimensions={0} | all-to-all | bytes 1572864 | tf_op jit(solution)/shard_map/all_to_all | solution.py:29
  90.1 8.6 %collective-permute-start.3 = (bf16[8,96,512]{2,1,0:T(8,128)(2,1)S(1)}, bf16[8,96,512]{2,1,0:T(8,128)(2,1)S(1)}, u32[]{:S(2)}, u32[]{:S(2)}) collective-permute-start(bf16[8,96,512]{2,1,0:T(8,128)(2,1)S(1)} %all_to_all.29.mine_ref), channel_id=1, source_target_pairs={{0,1},{1,0},{2,3},{3,2},{4,5},{5,4},{6,7},{7,6},{8,9},{9,8},{10,11... | collective-permute-start | bytes 2359304 | tf_op jit(solution)/shard_map/ppermute | solution.py:240
  98.7 1.9 %collective-permute-done.3.theirs_ref = bf16[8,96,512]{2,1,0:T(8,128)(2,1)S(1)} collective-permute-done((bf16[8,96,512]{2,1,0:T(8,128)(2,1)S(1)}, bf16[8,96,512]{2,1,0:T(8,128)(2,1)S(1)}, u32[]{:S(2)}, u32[]{:S(2)}) %collective-permute-start.3) | collective-permute-done | bytes 786464 | tf_op jit(solution)/shard_map/ppermute | solution.py:240
  100.6 1.1 %shard_map.107 = bf16[128,512]{1,0:T(8,128)(2,1)} custom-call(bf16[2,128,512]{2,1,0:T(8,128)(2,1)S(1)} %get-tuple-element.23.refs_0_.own_ref, bf16[8,96,512]{2,1,0:T(8,128)(2,1)S(1)} %all_to_all.29.mine_ref, bf16[8,96,512]{2,1,0:T(8,128)(2,1)S(1)} %collective-permute-done.3.theirs_ref), custom_call_target="tpu_custom_call" | custom-call | flops 1048576 | bytes 1048576 | tf_op jit(solution)/shard_map/pallas_call | solution.py:241
  (1 shorter events, 0.0 us)
Async XLA Ops:
  1.2 11.4 %collective-permute-start = (bf16[2,32,512]{2,1,0:T(8,128)(2,1)S(1)}, bf16[2,32,512]{2,1,0:T(8,128)(2,1)S(1)}, u32[]{:S(2)}, u32[]{:S(2)}) collective-permute-start(bf16[2,32,512]{2,1,0:T(8,128)(2,1)S(1)} %get-tuple-element.20), channel_id=1, source_target_pairs={{0,1},{1,0},{2,3},{3,2},{4,5},{5,4},{6,7},{7,6},{8,9},{9,8},{10,11... | collective-permute-start | bytes 196616 | tf_op jit(solution)/shard_map/ppermute | solution.py:220
  10.0 5.6 %collective-permute-start.1 = (bf16[2,32,512]{2,1,0:T(8,128)(2,1)S(1)}, bf16[2,32,512]{2,1,0:T(8,128)(2,1)S(1)}, u32[]{:S(2)}, u32[]{:S(2)}) collective-permute-start(bf16[2,32,512]{2,1,0:T(8,128)(2,1)S(1)} %get-tuple-element.21), channel_id=1, source_target_pairs={{1,2},{2,1},{3,4},{4,3},{5,6},{6,5},{7,8},{8,7},{9,10},{10,9},{11,... | collective-permute-start | bytes 196616 | tf_op jit(solution)/shard_map/ppermute | solution.py:221
  15.6 0.7 copy-start
  15.6 0.7 copy-start.1
  19.2 3.4 %collective-permute-start.2 = (bf16[2,128,512]{2,1,0:T(8,128)(2,1)S(1)}, bf16[2,128,512]{2,1,0:T(8,128)(2,1)S(1)}, u32[]{:S(2)}, u32[]{:S(2)}) collective-permute-start(bf16[2,128,512]{2,1,0:T(8,128)(2,1)S(1)} %get-tuple-element.23.refs_0_.own_ref), channel_id=1, source_target_pairs={{0,1},{1,0},{2,3},{3,2},{4,5},{5,4},{6,7},{7,6},{8,9},{9,8},{10,11... | collective-permute-start | bytes 786440 | tf_op jit(solution)/shard_map/ppermute | solution.py:227
  90.1 10.5 %collective-permute-start.3 = (bf16[8,96,512]{2,1,0:T(8,128)(2,1)S(1)}, bf16[8,96,512]{2,1,0:T(8,128)(2,1)S(1)}, u32[]{:S(2)}, u32[]{:S(2)}) collective-permute-start(bf16[8,96,512]{2,1,0:T(8,128)(2,1)S(1)} %all_to_all.29.mine_ref), channel_id=1, source_target_pairs={{0,1},{1,0},{2,3},{3,2},{4,5},{5,4},{6,7},{7,6},{8,9},{9,8},{10,11... | collective-permute-start | bytes 2359304 | tf_op jit(solution)/shard_map/ppermute | solution.py:240

commit v4 on v3

--- a/solution.py
+++ b/solution.py
@@ -47,7 +47,14 @@
     )
 
 
-def edges_kernel(q_in, k_in, v_in, t_in, q_ref, k_ref, v_ref, t_ref, core_ref, chip_ref, sems):
+def start_all(pairs, sems):
+    copies = [pltpu.make_async_copy(a, b, sems.at[n]) for n, (a, b) in enumerate(pairs)]
+    for c in copies:
+        c.start()
+    return copies
+
+
+def edges_kernel(k_in, v_in, core_ref, chip_ref, sems):
     core = lax.axis_index("row_2")
     near = HALO * 16
     end = k_in.shape[0] - near
@@ -56,21 +63,24 @@
     pairs = []
     for i, ref in enumerate((k_in, v_in)):
         pairs += [(ref.at[to_core], core_ref.at[i]), (ref.at[to_chip], chip_ref.at[i])]
-    pairs += [(k_in, k_ref), (v_in, v_ref), (q_in, q_ref), (t_in, t_ref)]
-    copies = [pltpu.make_async_copy(a, b, sems.at[n]) for n, (a, b) in enumerate(pairs)]
-    for c in copies:
-        c.start()
-    for c in copies:
+    for c in start_all(pairs, sems):
         c.wait()
 
 
-def attend_kernel(rows, cols, grid_rows, count_ref, reach_ref, q_ref, k_ref, v_ref, core_ref, chip_ref, target_ref, rate_ref, w1_in, w3_in, w2_in, out_ref, w1_ref, w3_ref, w2_ref, sems):
-    copies = [
-        pltpu.make_async_copy(a, b, sems.at[n])
-        for n, (a, b) in enumerate(((w1_in, w1_ref), (w3_in, w3_ref), (w2_in, w2_ref)))
-    ]
-    for c in copies:
-        c.start()
+def prepare_kernel(rows, cols, count_ref, edge_ref, rate_ref, q_in, k_in, v_in, t_in, q_ref, k_ref, v_ref, scaled_ref, t_ref, sems):
+    copies = start_all([(t_in, t_ref), (q_in, q_ref), (k_in, k_ref), (v_in, v_ref)], sems)
+    tokens = rows * cols
+    diagonal = iota((tokens, tokens), 0) == iota((tokens, tokens), 1)
+    rates = jnp.sum(jnp.where(diagonal, rate_ref[...], 0.0), 1, keepdims=True)
+    q_tok = lax.axis_index(ROW) * tokens + iota((tokens, 1), 0)
+    valid = jnp.where(q_tok < count_ref[0], 1.0, 0.0)
+    copies[0].wait()
+    scaled_ref[...] = (rates * valid * t_ref[...].astype(F32)).astype(BF)
+    for c in copies[1:]:
+        c.wait()
+
+
+def attend_kernel(rows, cols, grid_rows, count_ref, reach_ref, q_ref, k_ref, v_ref, core_ref, chip_ref, scaled_ref, out_ref):
     core = lax.axis_index("row_2")
     base = lax.axis_index(ROW) * rows
     count = count_ref[0]
@@ -105,40 +115,57 @@
     attended = jnp.concatenate(parts, 1)
     mean = jnp.mean(attended * attended, -1, keepdims=True)
     out_ref[0] = (attended * lax.rsqrt(mean + 1e-06)).astype(BF)
-    diagonal = iota((tokens, tokens), 0) == iota((tokens, tokens), 1)
-    rates = jnp.sum(jnp.where(diagonal, rate_ref[...], 0.0), 1, keepdims=True)
-    valid = jnp.where(q_tok < count, 1.0, 0.0)
-    out_ref[1] = (rates * valid * target_ref[...].astype(F32)).astype(BF)
-    for c in copies:
-        c.wait()
-
-
-def grads_kernel(n_plane, n_near, own_ref, other_ref, w1_ref, w3_ref, w2_ref, out_ref, old_ref):
-    core = lax.axis_index("row_2")
-    half = HD // 2
-    share = half // n_plane
-    few = share // n_near
-    keys = jnp.concatenate([own_ref[0], other_ref[0]], 0)
-    scaled = jnp.concatenate([own_ref[1], other_ref[1]], 0)
+    out_ref[1] = scaled_ref[...]
+
+
+def forward(keys, scaled, w1_ref, w3_ref, w2_ref):
     first = dot(keys, w1_ref[...])
     third = dot(keys, w3_ref[...])
     back = dot(scaled, w2_ref[...], 1, 1)
     sig = jax.nn.sigmoid(first)
     silu = first * sig
-    gated = silu * third
-    back_first = (back * third * (sig * (1.0 + first * (1.0 - sig)))).astype(BF)
-    back_third = (back * silu).astype(BF)
-    gated_half = jnp.where(core == 0, gated[:, :half], gated[:, half:]).astype(BF)
-    lanes = pl.ds(pl.multiple_of(core * half, half), half)
-    keys_half = jnp.concatenate([own_ref[0, :, lanes], other_ref[0, :, lanes]], 0)
-    for k, (a, b) in enumerate(((keys_half, back_first), (keys_half, back_third), (gated_half, scaled))):
-        g = dot(a, b, 0, 0).astype(BF)
-        out_ref[:, k * share : (k + 1) * share, :] = g.reshape(n_plane, share, HD)
+    back_first = back * third * (sig * (1.0 + first * (1.0 - sig)))
+    return back_first.astype(BF), (back * silu).astype(BF), silu * third
+
+
+def own_half(x, core):
+    half = x.shape[1] // 2
+    return jnp.where(core == 0, x[:, :half], x[:, half:])
+
+
+def forward_kernel(n_plane, n_near, own_ref, w1_ref, w3_ref, w2_ref, out_ref, gated_ref, old_ref):
+    core = lax.axis_index("row_2")
+    half = HD // 2
+    share = half // n_plane
+    few = share // n_near
+    back_first, back_third, gated = forward(own_ref[0], own_ref[1], w1_ref, w3_ref, w2_ref)
+    out_ref[0] = back_first
+    out_ref[1] = back_third
+    gated_ref[...] = own_half(gated, core).astype(BF)
     base = pl.multiple_of(core * half + lax.axis_index(PLANE) * share, share)
     at = lax.axis_index("near") * few
     pick = jnp.where(iota((few, share), 1) == at + iota((few, share), 0), 1.0, 0.0).astype(BF)
     for k, ref in enumerate((w1_ref, w3_ref, w2_ref)):
         old_ref[:, k * HD : (k + 1) * HD] = dot(pick, ref[pl.ds(base, share), :])
+
+
+def grads_kernel(n_plane, own_ref, mine_ref, mine_gated_ref, other_ref, w1_ref, w3_ref, w2_ref, out_ref):
+    core = lax.axis_index("row_2")
+    half = HD // 2
+    share = half // n_plane
+    back_first, back_third, gated = forward(other_ref[0], other_ref[1], w1_ref, w3_ref, w2_ref)
+    lanes = pl.ds(pl.multiple_of(core * half, half), half)
+    both = lambda a, b: jnp.concatenate([a, b], 0)
+    keys = both(own_ref[0, :, lanes], other_ref[0, :, lanes])
+    gated = both(mine_gated_ref[...], own_half(gated, core).astype(BF))
+    pairs = (
+        (keys, both(mine_ref[0], back_first)),
+        (keys, both(mine_ref[1], back_third)),
+        (gated, both(own_ref[1], other_ref[1])),
+    )
+    for k, (a, b) in enumerate(pairs):
+        g = dot(a, b, 0, 0).astype(BF)
+        out_ref[:, k * share : (k + 1) * share, :] = g.reshape(n_plane, share, HD)
 
 
 def spread_kernel(n_near, few, count_ref, x_ref, out_ref):
@@ -184,22 +211,26 @@
     out_ref[...] = jnp.broadcast_to(lines[None], out_ref.shape)
 
 
-def apply_kernel(own_ref, mine_ref, theirs_ref, out_ref):
-    core = lax.axis_index("row_2")
-    half = HD // 2
-    share = mine_ref.shape[1] // 3
-
-    def matrix(ref, k):
-        return ref[:, k * share : (k + 1) * share, :].reshape(half, HD)
-
-    k_mine = own_ref[0, :, pl.ds(pl.multiple_of(core * half, half), half)]
-    k_theirs = own_ref[0, :, pl.ds(pl.multiple_of((1 - core) * half, half), half)]
-    first = dot(k_mine, matrix(mine_ref, 0)) + dot(k_theirs, matrix(theirs_ref, 0))
-    third = dot(k_mine, matrix(mine_ref, 1)) + dot(k_theirs, matrix(theirs_ref, 1))
-    applied = (first * jax.nn.sigmoid(first) * third).astype(BF)
-    left, right = applied[:, :half], applied[:, half:]
-    a_mine = jnp.where(core == 0, left.astype(F32), right.astype(F32)).astype(BF)
-    a_theirs = jnp.where(core == 0, right.astype(F32), left.astype(F32)).astype(BF)
+def matrix(ref, k):
+    share = ref.shape[1] // 3
+    return ref[:, k * share : (k + 1) * share, :].reshape(ref.shape[0] * share, HD)
+
+
+def half_kernel(own_ref, mine_ref, out_ref):
+    half = HD // 2
+    keys = own_ref[0, :, pl.ds(pl.multiple_of(lax.axis_index("row_2") * half, half), half)]
+    out_ref[0] = dot(keys, matrix(mine_ref, 0))
+    out_ref[1] = dot(keys, matrix(mine_ref, 1))
+
+
+def apply_kernel(own_ref, part_ref, mine_ref, theirs_ref, out_ref):
+    core = lax.axis_index("row_2")
+    half = HD // 2
+    keys = own_ref[0, :, pl.ds(pl.multiple_of((1 - core) * half, half), half)]
+    first = part_ref[0] + dot(keys, matrix(theirs_ref, 0))
+    third = part_ref[1] + dot(keys, matrix(theirs_ref, 1))
+    applied = first * jax.nn.sigmoid(first) * third
+    a_mine, a_theirs = own_half(applied, core).astype(BF), own_half(applied, 1 - core).astype(BF)
     out_ref[...] = (dot(a_mine, matrix(mine_ref, 2)) + dot(a_theirs, matrix(theirs_ref, 2))).astype(BF)
 
 
@@ -212,21 +243,27 @@
     flat = lambda x: x.reshape(tokens, width)
     in_hbm = lambda x: pltpu.with_memory_space_constraint(x, pltpu.HBM)
 
-    block, edge, matrix = ((tokens, width), BF), ((2, near, width), BF), ((HD, HD), BF)
-    query, key, value, aim, to_core, to_chip = call(edges_kernel, [block] * 4 + [edge] * 2, [HBM] * 4, 8)(
-        *(in_hbm(flat(x)) for x in (query_feats, key_feats, value_feats, target))
-    )
+    block, edge = ((tokens, width), BF), ((2, near, width), BF)
+    query, key, value, aim = (in_hbm(flat(x)) for x in (query_feats, key_feats, value_feats, target))
+    to_core, to_chip = call(edges_kernel, [edge] * 2, [HBM] * 2, 4)(key, value)
     next_chip = [p for i in range(1, n_row - 1, 2) for p in ((i, i + 1), (i + 1, i))]
+    from_chip = lax.ppermute(to_chip, ROW, next_chip)
     from_core = lax.ppermute(to_core, "row_2", SWAP)
-    from_chip = lax.ppermute(to_chip, ROW, next_chip)
-
+
+    prepare = lambda *refs: prepare_kernel(rows, cols, *refs)
+    query, key, value, scaled, _ = call(prepare, [block] * 5, [SMEM] + [VMEM] * 2 + [HBM] * 4, 4)(
+        view_counts, to_core, token_rates[0], query, key, value, aim
+    )
     attend = lambda *refs: attend_kernel(rows, cols, n_row * rows, *refs)
-    own, w1, w3, w2 = call(attend, [((2, tokens, width), BF)] + [matrix] * 3, [SMEM] * 2 + [VMEM] * 7 + [HBM] * 3, 3)(
-        view_counts, row_reach, query, key, value, from_core, from_chip, aim, token_rates[0], *(in_hbm(w[0]) for w in (w_first, w_third, w_second))
+    own = call(attend, ((2, tokens, width), BF), [SMEM] * 2 + [VMEM] * 6)(
+        view_counts, row_reach, query, key, value, from_core, from_chip, scaled
     )
     other = lax.ppermute(own, "row_2", SWAP)
-    grads = lambda *refs: grads_kernel(n_plane, n_near, *refs)
-    part, old = call(grads, [((n_plane, 3 * share, width), BF), ((few, 3 * width), F32)], [VMEM] * 5)(own, other, w1, w3, w2)
+    ws = w_first[0], w_third[0], w_second[0]
+    ahead = lambda *refs: forward_kernel(n_plane, n_near, *refs)
+    back, gated, old = call(ahead, [((2, tokens, width), BF), ((tokens, width // 2), BF), ((few, 3 * width), F32)], [VMEM] * 4)(own, *ws)
+    grads = lambda *refs: grads_kernel(n_plane, *refs)
+    part = call(grads, ((n_plane, 3 * share, width), BF), [VMEM] * 7)(own, back, gated, other, *ws)
     part = exchange(part, PLANE)
     spread = lambda *refs: spread_kernel(n_near, few, *refs)
     part = call(spread, ((n_near, few, 3 * width + 128), BF), [SMEM, VMEM])(view_counts, part)
@@ -238,7 +275,8 @@
     lines = call(order_kernel, ((n_plane, 3 * share, width), BF), [VMEM])(new)
     mine = exchange(lines, PLANE)
     theirs = lax.ppermute(mine, "row_2", SWAP)
-    out = call(apply_kernel, ((tokens, width), BF), [VMEM] * 3)(own, mine, theirs)
+    part = call(half_kernel, ((2, tokens, width), F32), [VMEM] * 2)(own, mine)
+    out = call(apply_kernel, ((tokens, width), BF), [VMEM] * 4)(own, part, mine, theirs)
     return out.reshape(1, rows, cols, width)
 
 

time: 102 us -> 99 us (0.971)
  waiting for transfers between devices: 6.39 us -> 2.62 us
  Pallas kernels: 6.61 us -> 7.69 us
    ppermute x1, starting transfers between devices: 8.79 us -> 4.94 us  [per_device(): from_core = lax.ppermute(to_core, 'row_2', SWAP)]
    ppermute x1, waiting for transfers between devices: 3 us -> 0.01 us  [per_device(): from_chip = lax.ppermute(to_chip, ROW, next_chip)]
    ppermute x1, starting transfers between devices: 1.92 us -> 4.51 us  [per_device(): from_chip = lax.ppermute(to_chip, ROW, next_chip)]
    pallas_call x4 -> x7, Pallas kernels: 6.22 us -> 7.3 us  [the longest x1 1.88 us: per_device(): call(attend, ((2, tokens, width), BF), [SMEM] * 2 + [VMEM] * 6)]
  transfers between devices with their start and end apart: 4 -> 4, of which waited for: 3 -> 2; matrix products, arithmetic and copies ran while one was open for 0% -> 0% of each run, Pallas kernels for 0% -> 3%
where the time goes in v4:
time: 99 us; the launch traced here: 98.6 us
  blocking collectives  66.7 us (67%)
  starting transfers between devices  20.8 us (21%)
  Pallas kernels  7.69 us (8%)
  waiting for transfers between devices  2.62 us (3%)
    all_to_all x5, blocking collectives, exchange(): return lax.all_to_all(x, axes, 0, 0, tiled=True)  66.7 us
    ppermute x1, starting transfers between devices, per_device(): theirs = lax.ppermute(mine, 'row_2', SWAP)  9.39 us
    ppermute x1, starting transfers between devices, per_device(): from_core = lax.ppermute(to_core, 'row_2', SWAP)  4.94 us
    ppermute x1, starting transfers between devices, per_device(): from_chip = lax.ppermute(to_chip, ROW, next_chip)  4.51 us
  transfers between devices with their start and end apart: 4, of which 2 were waited for; matrix products, arithmetic and copies ran while one was open for 0% of the time, Pallas kernels for 3%

profile of v4, /device:TPU:1, one launch (start us, length us, event | category | flops | bytes accessed | tf_op | source)
XLA Modules:
  0.0 98.6 jit_solution(14644781158075436012)
XLA Ops:
  0.0 0.0 copy-start.3
  0.0 0.9 shard_map.100
  0.9 4.5 %collective-permute-start.1 = (bf16[2,32,512]{2,1,0:T(8,128)(2,1)S(1)}, bf16[2,32,512]{2,1,0:T(8,128)(2,1)S(1)}, u32[]{:S(2)}, u32[]{:S(2)}) collective-permute-start(bf16[2,32,512]{2,1,0:T(8,128)(2,1)S(1)} %get-tuple-element.18), channel_id=1, source_target_pairs={{1,2},{2,1},{3,4},{4,3},{5,6},{6,5},{7,8},{8,7},{9,10},{10,9},{11,... | collective-permute-start | bytes 196616 | tf_op jit(solution)/shard_map/ppermute | solution.py:250
  5.4 0.0 copy-start.4
  5.4 4.9 %collective-permute-start = (bf16[2,32,512]{2,1,0:T(8,128)(2,1)S(1)}, bf16[2,32,512]{2,1,0:T(8,128)(2,1)S(1)}, u32[]{:S(2)}, u32[]{:S(2)}) collective-permute-start(bf16[2,32,512]{2,1,0:T(8,128)(2,1)S(1)} %get-tuple-element.14.refs_1_), channel_id=1, source_target_pairs={{0,1},{1,0},{2,3},{3,2},{4,5},{5,4},{6,7},{7,6},{8,9},{9,8},{10,11... | collective-permute-start | bytes 196616 | tf_op jit(solution)/shard_map/ppermute | solution.py:251
  11.0 0.0 copy-done.3
  11.0 0.0 copy-start.1
  11.1 1.9 %shard_map.101 = (bf16[128,512]{1,0:T(8,128)(2,1)S(1)}, bf16[128,512]{1,0:T(8,128)(2,1)S(1)}, bf16[128,512]{1,0:T(8,128)(2,1)S(1)}, bf16[128,512]{1,0:T(8,128)(2,1)S(1)}, bf16[128,512]{1,0:T(8,128)(2,1)}) custom-call(s32[1]{0:T(128)S(6)} %copy.11.refs_0_, bf16[2,32,512]{2,1,0:T(8,128)(2,1)S(1)} %get-tuple-element.14.refs_1_, f32[1,128]{1,0:T(1,128)S(1)} %bitcast.15, ...), custom_call_target="tpu_custom_call" | custom-call | flops 1048576 | bytes 1048576 | tf_op jit(solution)/shard_map/pallas_call | solution.py:254
  12.9 0.0 copy-start
  12.9 0.0 collective-permute-done.1.refs_6_
  12.9 0.0 collective-permute-done.refs_5_
  13.0 0.0 copy-done.4
  13.0 1.9 %shard_map.102.refs_0_.own_ref = bf16[2,128,512]{2,1,0:T(8,128)(2,1)S(1)} custom-call(s32[1]{0:T(128)S(6)} %copy.11.refs_0_, s32[8]{0:T(128)S(1)} %copy-done.4, bf16[128,512]{1,0:T(8,128)(2,1)S(1)} %get-tuple-element.15.refs_2_, bf16[128,512]{1,0:T(8,128)(2,1)S(1)} %get-tuple-element.16.refs_3_, bf16[128,512]{1,0:T(8,128)(2,1)S(1)} %get-tuple-element.17.refs_4_, ...), custom_call_target="tpu_custom_call" | custom-call | flops 1048576 | bytes 1048576 | tf_op jit(solution)/shard_map/pallas_call | solution.py:258
  14.9 1.9 %collective-permute-start.2 = (bf16[2,128,512]{2,1,0:T(8,128)(2,1)S(1)}, bf16[2,128,512]{2,1,0:T(8,128)(2,1)S(1)}, u32[]{:S(2)}, u32[]{:S(2)}) collective-permute-start(bf16[2,128,512]{2,1,0:T(8,128)(2,1)S(1)} %shard_map.102.refs_0_.own_ref), channel_id=1, source_target_pairs={{0,1},{1,0},{2,3},{3,2},{4,5},{5,4},{6,7},{7,6},{8,9},{9,8},{10,11... | collective-permute-start | bytes 786440 | tf_op jit(solution)/shard_map/ppermute | solution.py:261
  16.8 0.0 copy-done.2
  16.8 0.0 copy-done.1
  16.8 0.0 copy-done
  16.8 0.5 shard_map.103
  17.3 1.0 collective-permute-done.2.refs_3_
  18.3 0.9 shard_map.104
  19.1 15.5 %all_to_all.25.refs_1_ = bf16[8,96,512]{2,1,0:T(8,128)(2,1)S(1)} all-to-all(bf16[8,96,512]{2,1,0:T(8,128)(2,1)S(1)} %shard_map.104), channel_id=1, replica_groups=mesh['head'=2,'far'=4,'near'=4,'row_0'=2,'row_1'=4,'row_2'=2] {'row_0','..., dimensions={0} | all-to-all | bytes 1572864 | tf_op jit(solution)/shard_map/all_to_all | solution.py:29
  34.7 0.1 shard_map.105
  34.8 8.5 %all_to_all.26.x_ref = bf16[4,8,1664]{2,1,0:T(8,128)(2,1)S(1)} all-to-all(bf16[4,8,1664]{2,1,0:T(8,128)(2,1)S(1)} %shard_map.105), channel_id=1, replica_groups=mesh['head'=2,'far'=4,'near'=4,'row_0'=2,'row_1'=4,'row_2'=2] {'near'}, dimensions={0} | all-to-all | bytes 212992 | tf_op jit(solution)/shard_map/all_to_all | solution.py:29
  43.3 23.9 %all_to_all.27.x_ref = bf16[4,8,1664]{2,1,0:T(8,128)(2,1)S(1)} all-to-all(bf16[4,8,1664]{2,1,0:T(8,128)(2,1)S(1)} %shard_map.106), channel_id=1, replica_groups=mesh['head'=2,'far'=4,'near'=4,'row_0'=2,'row_1'=4,'row_2'=2] {'far'}, dimensions={0} | all-to-all | bytes 212992 | tf_op jit(solution)/shard_map/all_to_all | solution.py:29
  67.1 0.2 shard_map.107
  67.4 7.2 %all_to_all.28.x_ref = bf16[4,8,1536]{2,1,0:T(8,128)(2,1)S(1)} all-to-all(bf16[4,8,1536]{2,1,0:T(8,128)(2,1)S(1)} %shard_map.107), channel_id=1, replica_groups=mesh['head'=2,'far'=4,'near'=4,'row_0'=2,'row_1'=4,'row_2'=2] {'near'}, dimensions={0} | all-to-all | bytes 196608 | tf_op jit(solution)/shard_map/all_to_all | solution.py:29
  74.5 0.1 shard_map.108
  74.6 11.6 %all_to_all.29.mine_ref = bf16[8,96,512]{2,1,0:T(8,128)(2,1)S(1)} all-to-all(bf16[8,96,512]{2,1,0:T(8,128)(2,1)S(1)} %shard_map.108), channel_id=1, replica_groups=mesh['head'=2,'far'=4,'near'=4,'row_0'=2,'row_1'=4,'row_2'=2] {'row_0','..., dimensions={0} | all-to-all | bytes 1572864 | tf_op jit(solution)/shard_map/all_to_all | solution.py:29
  86.2 9.4 %collective-permute-start.3 = (bf16[8,96,512]{2,1,0:T(8,128)(2,1)S(1)}, bf16[8,96,512]{2,1,0:T(8,128)(2,1)S(1)}, u32[]{:S(2)}, u32[]{:S(2)}) collective-permute-start(bf16[8,96,512]{2,1,0:T(8,128)(2,1)S(1)} %all_to_all.29.mine_ref), channel_id=1, source_target_pairs={{0,1},{1,0},{2,3},{3,2},{4,5},{5,4},{6,7},{7,6},{8,9},{9,8},{10,11... | collective-permute-start | bytes 2359304 | tf_op jit(solution)/shard_map/ppermute | solution.py:277
  95.6 0.2 shard_map.109.part_ref
  95.8 1.7 %collective-permute-done.3.theirs_ref = bf16[8,96,512]{2,1,0:T(8,128)(2,1)S(1)} collective-permute-done((bf16[8,96,512]{2,1,0:T(8,128)(2,1)S(1)}, bf16[8,96,512]{2,1,0:T(8,128)(2,1)S(1)}, u32[]{:S(2)}, u32[]{:S(2)}) %collective-permute-start.3) | collective-permute-done | bytes 786464 | tf_op jit(solution)/shard_map/ppermute | solution.py:277
  97.5 1.1 %shard_map.110 = bf16[128,512]{1,0:T(8,128)(2,1)} custom-call(bf16[2,128,512]{2,1,0:T(8,128)(2,1)S(1)} %shard_map.102.refs_0_.own_ref, f32[2,128,512]{2,1,0:T(8,128)S(1)} %shard_map.109.part_ref, bf16[8,96,512]{2,1,0:T(8,128)(2,1)S(1)} %all_to_all.29.mine_ref, bf16[8,96,512]{2,1,0:T(8,128)(2,1)S(1)} %collective-permute-done.3.theirs_ref), custom_call_target="tpu_custom_call" | custom-call | flops 1048576 | bytes 1048576 | tf_op jit(solution)/shard_map/pallas_call | solution.py:279
  (2 shorter events, 0.0 us)
Async XLA Ops:
  0.0 11.0 %copy-start.3 = (f32[1,1,128]{2,1,0:T(1,128)S(1)}, f32[1,1,128]{2,1,0:T(1,128)}, u32[]{:S(2)}) copy-start(f32[1,1,128]{2,1,0:T(1,128)} %param.14) | copy-start | bytes 1540
  0.0 16.8 %copy-start.2 = (bf16[1,512,512]{2,1,0:T(8,128)(2,1)S(1)}, bf16[1,512,512]{2,1,0:T(8,128)(2,1)}, u32[]{:S(2)}) copy-start(bf16[1,512,512]{2,1,0:T(8,128)(2,1)} %param.19) | copy-start | bytes 1572868
  0.9 12.0 %collective-permute-start.1 = (bf16[2,32,512]{2,1,0:T(8,128)(2,1)S(1)}, bf16[2,32,512]{2,1,0:T(8,128)(2,1)S(1)}, u32[]{:S(2)}, u32[]{:S(2)}) collective-permute-start(bf16[2,32,512]{2,1,0:T(8,128)(2,1)S(1)} %get-tuple-element.18), channel_id=1, source_target_pairs={{1,2},{2,1},{3,4},{4,3},{5,6},{6,5},{7,8},{8,7},{9,10},{10,9},{11,... | collective-permute-start | bytes 196616 | tf_op jit(solution)/shard_map/ppermute | solution.py:250
  5.4 7.5 %copy-start.4 = (s32[8]{0:T(128)S(1)}, s32[8]{0:T(128)}, u32[]{:S(2)}) copy-start(s32[8]{0:T(128)} %refs_1_.1) | copy-start | bytes 100
  5.4 7.5 %collective-permute-start = (bf16[2,32,512]{2,1,0:T(8,128)(2,1)S(1)}, bf16[2,32,512]{2,1,0:T(8,128)(2,1)S(1)}, u32[]{:S(2)}, u32[]{:S(2)}) collective-permute-start(bf16[2,32,512]{2,1,0:T(8,128)(2,1)S(1)} %get-tuple-element.14.refs_1_), channel_id=1, source_target_pairs={{0,1},{1,0},{2,3},{3,2},{4,5},{5,4},{6,7},{7,6},{8,9},{9,8},{10,11... | collective-permute-start | bytes 196616 | tf_op jit(solution)/shard_map/ppermute | solution.py:251
  11.0 5.7 %copy-start.1 = (bf16[1,512,512]{2,1,0:T(8,128)(2,1)S(1)}, bf16[1,512,512]{2,1,0:T(8,128)(2,1)}, u32[]{:S(2)}) copy-start(bf16[1,512,512]{2,1,0:T(8,128)(2,1)} %param.18) | copy-start | bytes 1572868
  12.9 3.9 %copy-start = (bf16[1,512,512]{2,1,0:T(8,128)(2,1)S(1)}, bf16[1,512,512]{2,1,0:T(8,128)(2,1)}, u32[]{:S(2)}) copy-start(bf16[1,512,512]{2,1,0:T(8,128)(2,1)} %param.17) | copy-start | bytes 1572868
  14.9 3.4 %collective-permute-start.2 = (bf16[2,128,512]{2,1,0:T(8,128)(2,1)S(1)}, bf16[2,128,512]{2,1,0:T(8,128)(2,1)S(1)}, u32[]{:S(2)}, u32[]{:S(2)}) collective-permute-start(bf16[2,128,512]{2,1,0:T(8,128)(2,1)S(1)} %shard_map.102.refs_0_.own_ref), channel_id=1, source_target_pairs={{0,1},{1,0},{2,3},{3,2},{4,5},{5,4},{6,7},{7,6},{8,9},{9,8},{10,11... | collective-permute-start | bytes 786440 | tf_op jit(solution)/shard_map/ppermute | solution.py:261
  86.2 11.3 %collective-permute-start.3 = (bf16[8,96,512]{2,1,0:T(8,128)(2,1)S(1)}, bf16[8,96,512]{2,1,0:T(8,128)(2,1)S(1)}, u32[]{:S(2)}, u32[]{:S(2)}) collective-permute-start(bf16[8,96,512]{2,1,0:T(8,128)(2,1)S(1)} %all_to_all.29.mine_ref), channel_id=1, source_target_pairs={{0,1},{1,0},{2,3},{3,2},{4,5},{5,4},{6,7},{7,6},{8,9},{9,8},{10,11... | collective-permute-start | bytes 2359304 | tf_op jit(solution)/shard_map/ppermute | solution.py:277

commit v5 on v4

--- a/solution.py
+++ b/solution.py
@@ -54,7 +54,7 @@
     return copies
 
 
-def edges_kernel(k_in, v_in, core_ref, chip_ref, sems):
+def edges_kernel(q_in, k_in, v_in, t_in, r_in, core_ref, chip_ref, q_ref, k_ref, v_ref, t_ref, r_ref, sems):
     core = lax.axis_index("row_2")
     near = HALO * 16
     end = k_in.shape[0] - near
@@ -63,21 +63,16 @@
     pairs = []
     for i, ref in enumerate((k_in, v_in)):
         pairs += [(ref.at[to_core], core_ref.at[i]), (ref.at[to_chip], chip_ref.at[i])]
-    for c in start_all(pairs, sems):
+    for c in start_all(pairs + [(r_in, r_ref), (t_in, t_ref), (q_in, q_ref), (k_in, k_ref), (v_in, v_ref)], sems):
         c.wait()
 
 
-def prepare_kernel(rows, cols, count_ref, edge_ref, rate_ref, q_in, k_in, v_in, t_in, q_ref, k_ref, v_ref, scaled_ref, t_ref, sems):
-    copies = start_all([(t_in, t_ref), (q_in, q_ref), (k_in, k_ref), (v_in, v_ref)], sems)
-    tokens = rows * cols
+def scale_kernel(tokens, count_ref, edge_ref, rate_ref, t_ref, out_ref):
     diagonal = iota((tokens, tokens), 0) == iota((tokens, tokens), 1)
-    rates = jnp.sum(jnp.where(diagonal, rate_ref[...], 0.0), 1, keepdims=True)
-    q_tok = lax.axis_index(ROW) * tokens + iota((tokens, 1), 0)
+    q_tok = lax.axis_index(ROW) * tokens + iota((1, tokens), 1)
     valid = jnp.where(q_tok < count_ref[0], 1.0, 0.0)
-    copies[0].wait()
-    scaled_ref[...] = (rates * valid * t_ref[...].astype(F32)).astype(BF)
-    for c in copies[1:]:
-        c.wait()
+    rates = jnp.sum(jnp.where(diagonal, rate_ref[...] * valid, 0.0), 1, keepdims=True)
+    out_ref[...] = (rates * t_ref[...].astype(F32)).astype(BF)
 
 
 def attend_kernel(rows, cols, grid_rows, count_ref, reach_ref, q_ref, k_ref, v_ref, core_ref, chip_ref, scaled_ref, out_ref):
@@ -86,7 +81,7 @@
     count = count_ref[0]
     tokens, near = rows * cols, HALO * cols
     span = tokens + 2 * near
-    at = iota((1, span), 1)
+    at = iota((span, 1), 0)
     below, above = base + rows, base - HALO
     first_core = jnp.where(core == 0, below, above)
     first_chip = jnp.where(core == 0, above, below)
@@ -94,24 +89,24 @@
     skip = jnp.where(at < tokens, 0, jnp.where(at < tokens + near, tokens, tokens + near))
     k_tok = start * cols + at - skip
     k_row = start + (at - skip) // cols
-    q_at = iota((tokens, 1), 0)
+    q_at = iota((1, tokens), 1)
     q_line = q_at // cols
     q_tok = base * cols + q_at
-    reach = jnp.zeros((tokens, 1), jnp.int32)
+    reach = jnp.zeros((1, tokens), jnp.int32)
     for r in range(rows):
         reach = jnp.where(q_line == r, reach_ref[r], reach)
-    inside = (k_row >= 0) & (k_row < grid_rows)
-    allowed = (jnp.abs(k_row - (base + q_line)) <= reach) & inside & ((k_tok < count) | (k_tok == q_tok))
+    valid = (k_tok < count) & (k_row >= 0) & (k_row < grid_rows)
+    k_row = jnp.where(valid, k_row, -(1 << 20))
+    allowed = (jnp.abs(k_row - (base + q_line)) <= reach) | (k_tok == q_tok)
     parts = []
     for h in range(q_ref.shape[1] // ATT_HD):
         lanes = slice(h * ATT_HD, (h + 1) * ATT_HD)
         keys = jnp.concatenate([k_ref[:, lanes], core_ref[0, :, lanes], chip_ref[0, :, lanes]], 0)
         values = jnp.concatenate([v_ref[:, lanes], core_ref[1, :, lanes], chip_ref[1, :, lanes]], 0)
-        scores = dot(q_ref[:, lanes], keys, 1, 1) * (1.0 / math.sqrt(ATT_HD))
-        scores = jnp.where(allowed, scores, -1e30)
-        powers = jnp.exp(scores - jnp.max(scores, -1, keepdims=True))
-        weights = (powers / jnp.sum(powers, -1, keepdims=True)).astype(BF)
-        parts.append(dot(weights, values).astype(BF).astype(F32))
+        scores = jnp.where(allowed, dot(keys, q_ref[:, lanes], 1, 1), -1e30)
+        powers = jnp.exp2((scores - jnp.max(scores, 0, keepdims=True)) * (math.log2(math.e) / math.sqrt(ATT_HD)))
+        weights = (powers * (1.0 / jnp.sum(powers, 0, keepdims=True))).astype(BF)
+        parts.append(dot(weights, values, 0, 0).astype(BF).astype(F32))
     attended = jnp.concatenate(parts, 1)
     mean = jnp.mean(attended * attended, -1, keepdims=True)
     out_ref[0] = (attended * lax.rsqrt(mean + 1e-06)).astype(BF)
@@ -245,15 +240,14 @@
 
     block, edge = ((tokens, width), BF), ((2, near, width), BF)
     query, key, value, aim = (in_hbm(flat(x)) for x in (query_feats, key_feats, value_feats, target))
-    to_core, to_chip = call(edges_kernel, [edge] * 2, [HBM] * 2, 4)(key, value)
+    to_core, to_chip, query, key, value, aim, rates = call(edges_kernel, [edge] * 2 + [block] * 4 + [((1, tokens), F32)], [HBM] * 5, 9)(
+        query, key, value, aim, in_hbm(token_rates[0])
+    )
     next_chip = [p for i in range(1, n_row - 1, 2) for p in ((i, i + 1), (i + 1, i))]
     from_chip = lax.ppermute(to_chip, ROW, next_chip)
     from_core = lax.ppermute(to_core, "row_2", SWAP)
 
-    prepare = lambda *refs: prepare_kernel(rows, cols, *refs)
-    query, key, value, scaled, _ = call(prepare, [block] * 5, [SMEM] + [VMEM] * 2 + [HBM] * 4, 4)(
-        view_counts, to_core, token_rates[0], query, key, value, aim
-    )
+    scaled = call(lambda *refs: scale_kernel(tokens, *refs), block, [SMEM] + [VMEM] * 3)(view_counts, to_core, rates, aim)
     attend = lambda *refs: attend_kernel(rows, cols, n_row * rows, *refs)
     own = call(attend, ((2, tokens, width), BF), [SMEM] * 2 + [VMEM] * 6)(
         view_counts, row_reach, query, key, value, from_core, from_chip, scaled

time: 99 us -> 98 us (0.990)
  Pallas kernels: 7.69 us -> 6.42 us
  blocking collectives: 66.7 us -> 67.7 us
    pallas_call x2, Pallas kernels: 2.75 us -> 1.43 us  [the longest x1 1.32 us: per_device(): call(edges_kernel, [edge] * 2 + [block] * 4 + [((1, tokens), F32)], [HBM]...]
    all_to_all x5, blocking collectives: 66.7 us -> 67.7 us  [exchange(): return lax.all_to_all(x, axes, 0, 0, tiled=True)]
  transfers between devices with their start and end apart: 4 -> 4, of which waited for: 2 -> 3; matrix products, arithmetic and copies ran while one was open for 0% -> 0% of each run, Pallas kernels for 3% -> 1%
where the time goes in v5:
time: 98 us; the launch traced here: 97.6 us
  blocking collectives  67.7 us (69%)
  starting transfers between devices  20.3 us (21%)
  Pallas kernels  6.42 us (7%)
  waiting for transfers between devices  2.36 us (2%)
    all_to_all x5, blocking collectives, exchange(): return lax.all_to_all(x, axes, 0, 0, tiled=True)  67.7 us
    ppermute x1, starting transfers between devices, per_device(): theirs = lax.ppermute(mine, 'row_2', SWAP)  8.57 us
    ppermute x1, starting transfers between devices, per_device(): from_core = lax.ppermute(to_core, 'row_2', SWAP)  4.94 us
    ppermute x1, starting transfers between devices, per_device(): from_chip = lax.ppermute(to_chip, ROW, next_chip)  4.51 us
    ppermute x1, starting transfers between devices, per_device(): other = lax.ppermute(own, 'row_2', SWAP)  2.26 us
  transfers between devices with their start and end apart: 4, of which 3 were waited for; matrix products, arithmetic and copies ran while one was open for 0% of the time, Pallas kernels for 1%

profile of v5, /device:TPU:1, one launch (start us, length us, event | category | flops | bytes accessed | tf_op | source)
XLA Modules:
  0.0 97.6 jit_solution(6941350903778915366)
XLA Ops:
  0.0 0.0 copy-start.2
  0.0 1.3 %shard_map.100 = (bf16[2,32,512]{2,1,0:T(8,128)(2,1)S(1)}, bf16[2,32,512]{2,1,0:T(8,128)(2,1)S(1)}, bf16[128,512]{1,0:T(8,128)(2,1)S(1)}, bf16[128,512]{1,0:T(8,...) custom-call(bf16[128,512]{1,0:T(8,128)(2,1)} %bitcast.15, ...), custom_call_target="tpu_custom_call" | custom-call | flops 1048576 | bytes 1048576 | tf_op jit(solution)/shard_map/pallas_call | solution.py:243
  1.3 0.0 copy-start.3
  1.3 4.5 %collective-permute-start.1 = (bf16[2,32,512]{2,1,0:T(8,128)(2,1)S(1)}, bf16[2,32,512]{2,1,0:T(8,128)(2,1)S(1)}, u32[]{:S(2)}, u32[]{:S(2)}) collective-permute-start(bf16[2,32,512]{2,1,0:T(8,128)(2,1)S(1)} %get-tuple-element.19), channel_id=1, source_target_pairs={{1,2},{2,1},{3,4},{4,3},{5,6},{6,5},{7,8},{8,7},{9,10},{10,9},{11,... | collective-permute-start | bytes 196616 | tf_op jit(solution)/shard_map/ppermute | solution.py:247
  5.9 4.9 %collective-permute-start = (bf16[2,32,512]{2,1,0:T(8,128)(2,1)S(1)}, bf16[2,32,512]{2,1,0:T(8,128)(2,1)S(1)}, u32[]{:S(2)}, u32[]{:S(2)}) collective-permute-start(bf16[2,32,512]{2,1,0:T(8,128)(2,1)S(1)} %get-tuple-element.18.refs_1_), channel_id=1, source_target_pairs={{0,1},{1,0},{2,3},{3,2},{4,5},{5,4},{6,7},{7,6},{8,9},{9,8},{10,11... | collective-permute-start | bytes 196616 | tf_op jit(solution)/shard_map/ppermute | solution.py:248
  11.5 0.0 copy-start.1
  11.5 0.1 shard_map.101.refs_7_
  11.6 0.0 copy-start
  11.6 0.0 collective-permute-done.1.refs_6_
  11.6 0.1 collective-permute-done.refs_5_
  11.7 0.0 copy-done.3
  11.7 1.9 %shard_map.102.refs_0_.own_ref = bf16[2,128,512]{2,1,0:T(8,128)(2,1)S(1)} custom-call(s32[1]{0:T(128)S(6)} %copy.11.refs_0_, s32[8]{0:T(128)S(1)} %copy-done.3, bf16[128,512]{1,0:T(8,128)(2,1)S(1)} %get-tuple-element.15.refs_2_, bf16[128,512]{1,0:T(8,128)(2,1)S(1)} %get-tuple-element.16.refs_3_, bf16[128,512]{1,0:T(8,128)(2,1)S(1)} %get-tuple-element.17.refs_4_, ...), custom_call_target="tpu_custom_call" | custom-call | flops 1048576 | bytes 1048576 | tf_op jit(solution)/shard_map/pallas_call | solution.py:252
  13.6 2.3 %collective-permute-start.2 = (bf16[2,128,512]{2,1,0:T(8,128)(2,1)S(1)}, bf16[2,128,512]{2,1,0:T(8,128)(2,1)S(1)}, u32[]{:S(2)}, u32[]{:S(2)}) collective-permute-start(bf16[2,128,512]{2,1,0:T(8,128)(2,1)S(1)} %shard_map.102.refs_0_.own_ref), channel_id=1, source_target_pairs={{0,1},{1,0},{2,3},{3,2},{4,5},{5,4},{6,7},{7,6},{8,9},{9,8},{10,11... | collective-permute-start | bytes 786440 | tf_op jit(solution)/shard_map/ppermute | solution.py:255
  15.9 0.0 copy-done.2
  15.9 0.0 copy-done.1
  15.9 0.0 copy-done
  15.9 0.5 shard_map.103
  16.4 0.6 collective-permute-done.2.refs_3_
  17.1 0.9 shard_map.104
  17.9 15.5 %all_to_all.25.refs_1_ = bf16[8,96,512]{2,1,0:T(8,128)(2,1)S(1)} all-to-all(bf16[8,96,512]{2,1,0:T(8,128)(2,1)S(1)} %shard_map.104), channel_id=1, replica_groups=mesh['head'=2,'far'=4,'near'=4,'row_0'=2,'row_1'=4,'row_2'=2] {'row_0','..., dimensions={0} | all-to-all | bytes 1572864 | tf_op jit(solution)/shard_map/all_to_all | solution.py:29
  33.4 0.1 shard_map.105
  33.5 9.6 %all_to_all.26.x_ref = bf16[4,8,1664]{2,1,0:T(8,128)(2,1)S(1)} all-to-all(bf16[4,8,1664]{2,1,0:T(8,128)(2,1)S(1)} %shard_map.105), channel_id=1, replica_groups=mesh['head'=2,'far'=4,'near'=4,'row_0'=2,'row_1'=4,'row_2'=2] {'near'}, dimensions={0} | all-to-all | bytes 212992 | tf_op jit(solution)/shard_map/all_to_all | solution.py:29
  43.1 23.8 %all_to_all.27.x_ref = bf16[4,8,1664]{2,1,0:T(8,128)(2,1)S(1)} all-to-all(bf16[4,8,1664]{2,1,0:T(8,128)(2,1)S(1)} %shard_map.106), channel_id=1, replica_groups=mesh['head'=2,'far'=4,'near'=4,'row_0'=2,'row_1'=4,'row_2'=2] {'far'}, dimensions={0} | all-to-all | bytes 212992 | tf_op jit(solution)/shard_map/all_to_all | solution.py:29
  66.9 0.2 shard_map.107
  67.1 7.4 %all_to_all.28.x_ref = bf16[4,8,1536]{2,1,0:T(8,128)(2,1)S(1)} all-to-all(bf16[4,8,1536]{2,1,0:T(8,128)(2,1)S(1)} %shard_map.107), channel_id=1, replica_groups=mesh['head'=2,'far'=4,'near'=4,'row_0'=2,'row_1'=4,'row_2'=2] {'near'}, dimensions={0} | all-to-all | bytes 196608 | tf_op jit(solution)/shard_map/all_to_all | solution.py:29
  74.6 0.1 shard_map.108
  74.6 11.4 %all_to_all.29.mine_ref = bf16[8,96,512]{2,1,0:T(8,128)(2,1)S(1)} all-to-all(bf16[8,96,512]{2,1,0:T(8,128)(2,1)S(1)} %shard_map.108), channel_id=1, replica_groups=mesh['head'=2,'far'=4,'near'=4,'row_0'=2,'row_1'=4,'row_2'=2] {'row_0','..., dimensions={0} | all-to-all | bytes 1572864 | tf_op jit(solution)/shard_map/all_to_all | solution.py:29
  86.0 8.6 %collective-permute-start.3 = (bf16[8,96,512]{2,1,0:T(8,128)(2,1)S(1)}, bf16[8,96,512]{2,1,0:T(8,128)(2,1)S(1)}, u32[]{:S(2)}, u32[]{:S(2)}) collective-permute-start(bf16[8,96,512]{2,1,0:T(8,128)(2,1)S(1)} %all_to_all.29.mine_ref), channel_id=1, source_target_pairs={{0,1},{1,0},{2,3},{3,2},{4,5},{5,4},{6,7},{7,6},{8,9},{9,8},{10,11... | collective-permute-start | bytes 2359304 | tf_op jit(solution)/shard_map/ppermute | solution.py:271
  94.6 0.2 shard_map.109.part_ref
  94.8 1.7 %collective-permute-done.3.theirs_ref = bf16[8,96,512]{2,1,0:T(8,128)(2,1)S(1)} collective-permute-done((bf16[8,96,512]{2,1,0:T(8,128)(2,1)S(1)}, bf16[8,96,512]{2,1,0:T(8,128)(2,1)S(1)}, u32[]{:S(2)}, u32[]{:S(2)}) %collective-permute-start.3) | collective-permute-done | bytes 786464 | tf_op jit(solution)/shard_map/ppermute | solution.py:271
  96.5 1.1 %shard_map.110 = bf16[128,512]{1,0:T(8,128)(2,1)} custom-call(bf16[2,128,512]{2,1,0:T(8,128)(2,1)S(1)} %shard_map.102.refs_0_.own_ref, f32[2,128,512]{2,1,0:T(8,128)S(1)} %shard_map.109.part_ref, bf16[8,96,512]{2,1,0:T(8,128)(2,1)S(1)} %all_to_all.29.mine_ref, bf16[8,96,512]{2,1,0:T(8,128)(2,1)S(1)} %collective-permute-done.3.theirs_ref), custom_call_target="tpu_custom_call" | custom-call | flops 1048576 | bytes 1048576 | tf_op jit(solution)/shard_map/pallas_call | solution.py:273
  (1 shorter events, 0.0 us)
Async XLA Ops:
  0.0 15.9 %copy-start.2 = (bf16[1,512,512]{2,1,0:T(8,128)(2,1)S(1)}, bf16[1,512,512]{2,1,0:T(8,128)(2,1)}, u32[]{:S(2)}) copy-start(bf16[1,512,512]{2,1,0:T(8,128)(2,1)} %param.19) | copy-start | bytes 1572868
  1.3 10.4 %copy-start.3 = (s32[8]{0:T(128)S(1)}, s32[8]{0:T(128)}, u32[]{:S(2)}) copy-start(s32[8]{0:T(128)} %refs_1_.1) | copy-start | bytes 100
  1.3 10.3 %collective-permute-start.1 = (bf16[2,32,512]{2,1,0:T(8,128)(2,1)S(1)}, bf16[2,32,512]{2,1,0:T(8,128)(2,1)S(1)}, u32[]{:S(2)}, u32[]{:S(2)}) collective-permute-start(bf16[2,32,512]{2,1,0:T(8,128)(2,1)S(1)} %get-tuple-element.19), channel_id=1, source_target_pairs={{1,2},{2,1},{3,4},{4,3},{5,6},{6,5},{7,8},{8,7},{9,10},{10,9},{11,... | collective-permute-start | bytes 196616 | tf_op jit(solution)/shard_map/ppermute | solution.py:247
  5.9 5.8 %collective-permute-start = (bf16[2,32,512]{2,1,0:T(8,128)(2,1)S(1)}, bf16[2,32,512]{2,1,0:T(8,128)(2,1)S(1)}, u32[]{:S(2)}, u32[]{:S(2)}) collective-permute-start(bf16[2,32,512]{2,1,0:T(8,128)(2,1)S(1)} %get-tuple-element.18.refs_1_), channel_id=1, source_target_pairs={{0,1},{1,0},{2,3},{3,2},{4,5},{5,4},{6,7},{7,6},{8,9},{9,8},{10,11... | collective-permute-start | bytes 196616 | tf_op jit(solution)/shard_map/ppermute | solution.py:248
  11.5 4.5 %copy-start.1 = (bf16[1,512,512]{2,1,0:T(8,128)(2,1)S(1)}, bf16[1,512,512]{2,1,0:T(8,128)(2,1)}, u32[]{:S(2)}) copy-start(bf16[1,512,512]{2,1,0:T(8,128)(2,1)} %param.18) | copy-start | bytes 1572868
  11.6 4.3 %copy-start = (bf16[1,512,512]{2,1,0:T(8,128)(2,1)S(1)}, bf16[1,512,512]{2,1,0:T(8,128)(2,1)}, u32[]{:S(2)}) copy-start(bf16[1,512,512]{2,1,0:T(8,128)(2,1)} %param.17) | copy-start | bytes 1572868
  13.6 3.4 %collective-permute-start.2 = (bf16[2,128,512]{2,1,0:T(8,128)(2,1)S(1)}, bf16[2,128,512]{2,1,0:T(8,128)(2,1)S(1)}, u32[]{:S(2)}, u32[]{:S(2)}) collective-permute-start(bf16[2,128,512]{2,1,0:T(8,128)(2,1)S(1)} %shard_map.102.refs_0_.own_ref), channel_id=1, source_target_pairs={{0,1},{1,0},{2,3},{3,2},{4,5},{5,4},{6,7},{7,6},{8,9},{9,8},{10,11... | collective-permute-start | bytes 786440 | tf_op jit(solution)/shard_map/ppermute | solution.py:255
  86.0 10.5 %collective-permute-start.3 = (bf16[8,96,512]{2,1,0:T(8,128)(2,1)S(1)}, bf16[8,96,512]{2,1,0:T(8,128)(2,1)S(1)}, u32[]{:S(2)}, u32[]{:S(2)}) collective-permute-start(bf16[8,96,512]{2,1,0:T(8,128)(2,1)S(1)} %all_to_all.29.mine_ref), channel_id=1, source_target_pairs={{0,1},{1,0},{2,3},{3,2},{4,5},{5,4},{6,7},{7,6},{8,9},{9,8},{10,11... | collective-permute-start | bytes 2359304 | tf_op jit(solution)/shard_map/ppermute | solution.py:271

commit v6 on v5

--- a/solution.py
+++ b/solution.py
@@ -33,15 +33,15 @@
     return lax.broadcasted_iota(jnp.int32, shape, dim)
 
 
-def call(kernel, shapes, specs, copies=0):
+def call(kernel, shapes, specs, scratch=(), out=VMEM):
     many = isinstance(shapes, list)
     outs = [jax.ShapeDtypeStruct(*s) for s in shapes] if many else jax.ShapeDtypeStruct(*shapes)
     return pl.pallas_call(
         kernel,
         out_shape=outs,
         in_specs=specs,
-        out_specs=[VMEM] * len(shapes) if many else VMEM,
-        scratch_shapes=[pltpu.SemaphoreType.DMA((copies,))] if copies else [],
+        out_specs=[out] * len(shapes) if many else out,
+        scratch_shapes=scratch,
         compiler_params=pltpu.CompilerParams(vmem_limit_bytes=24 << 20),
         cost_estimate=pl.CostEstimate(flops=1 << 20, bytes_accessed=1 << 20, transcendentals=0),
     )
@@ -54,16 +54,26 @@
     return copies
 
 
-def edges_kernel(q_in, k_in, v_in, t_in, r_in, core_ref, chip_ref, q_ref, k_ref, v_ref, t_ref, r_ref, sems):
-    core = lax.axis_index("row_2")
-    near = HALO * 16
+def edges_kernel(
+    cols, q_in, k_in, v_in, t_in, rate_in, reach_in, core_ref, chip_ref, q_ref, k_ref, v_ref, t_ref, rate_ref, reach_ref, sems, reach_smem
+):
+    core = lax.axis_index("row_2")
+    near = HALO * cols
     end = k_in.shape[0] - near
     to_core = pl.ds(pl.multiple_of((1 - core) * end, near), near)
     to_chip = pl.ds(pl.multiple_of(core * end, near), near)
-    pairs = []
+    pairs = [(reach_in, reach_smem)]
     for i, ref in enumerate((k_in, v_in)):
         pairs += [(ref.at[to_core], core_ref.at[i]), (ref.at[to_chip], chip_ref.at[i])]
-    for c in start_all(pairs + [(r_in, r_ref), (t_in, t_ref), (q_in, q_ref), (k_in, k_ref), (v_in, v_ref)], sems):
+    pairs += [(rate_in, rate_ref), (t_in, t_ref), (q_in, q_ref), (k_in, k_ref), (v_in, v_ref)]
+    copies = start_all(pairs, sems)
+    copies[0].wait()
+    line = iota(reach_ref.shape, 1) // cols
+    reach = jnp.zeros(reach_ref.shape, jnp.int32)
+    for r in range(reach_smem.shape[0]):
+        reach = jnp.where(line == r, reach_smem[r], reach)
+    reach_ref[...] = reach
+    for c in copies[1:]:
         c.wait()
 
 
@@ -78,7 +88,6 @@
 def attend_kernel(rows, cols, grid_rows, count_ref, reach_ref, q_ref, k_ref, v_ref, core_ref, chip_ref, scaled_ref, out_ref):
     core = lax.axis_index("row_2")
     base = lax.axis_index(ROW) * rows
-    count = count_ref[0]
     tokens, near = rows * cols, HALO * cols
     span = tokens + 2 * near
     at = iota((span, 1), 0)
@@ -90,26 +99,25 @@
     k_tok = start * cols + at - skip
     k_row = start + (at - skip) // cols
     q_at = iota((1, tokens), 1)
-    q_line = q_at // cols
+    q_row = base + q_at // cols
     q_tok = base * cols + q_at
-    reach = jnp.zeros((1, tokens), jnp.int32)
-    for r in range(rows):
-        reach = jnp.where(q_line == r, reach_ref[r], reach)
-    valid = (k_tok < count) & (k_row >= 0) & (k_row < grid_rows)
+    valid = (k_tok < count_ref[0]) & (k_row >= 0) & (k_row < grid_rows)
     k_row = jnp.where(valid, k_row, -(1 << 20))
-    allowed = (jnp.abs(k_row - (base + q_line)) <= reach) | (k_tok == q_tok)
-    parts = []
-    for h in range(q_ref.shape[1] // ATT_HD):
-        lanes = slice(h * ATT_HD, (h + 1) * ATT_HD)
-        keys = jnp.concatenate([k_ref[:, lanes], core_ref[0, :, lanes], chip_ref[0, :, lanes]], 0)
-        values = jnp.concatenate([v_ref[:, lanes], core_ref[1, :, lanes], chip_ref[1, :, lanes]], 0)
-        scores = jnp.where(allowed, dot(keys, q_ref[:, lanes], 1, 1), -1e30)
-        powers = jnp.exp2((scores - jnp.max(scores, 0, keepdims=True)) * (math.log2(math.e) / math.sqrt(ATT_HD)))
-        weights = (powers * (1.0 / jnp.sum(powers, 0, keepdims=True))).astype(BF)
-        parts.append(dot(weights, values, 0, 0).astype(BF).astype(F32))
-    attended = jnp.concatenate(parts, 1)
-    mean = jnp.mean(attended * attended, -1, keepdims=True)
-    out_ref[0] = (attended * lax.rsqrt(mean + 1e-06)).astype(BF)
+    allowed = (jnp.abs(k_row - q_row) <= reach_ref[...]) | (k_tok == q_tok)
+    heads = [slice(at, at + ATT_HD) for at in range(0, q_ref.shape[1], ATT_HD)]
+    factor = math.log2(math.e) / math.sqrt(ATT_HD)
+    keys = [jnp.concatenate([k_ref[:, h], core_ref[0, :, h], chip_ref[0, :, h]], 0) for h in heads]
+    values = [jnp.concatenate([v_ref[:, h], core_ref[1, :, h], chip_ref[1, :, h]], 0) for h in heads]
+    scores = [jnp.where(allowed, dot(k, q_ref[:, h], 1, 1), -1e30) for k, h in zip(keys, heads)]
+    tops = [jnp.max(s, 0, keepdims=True) for s in scores]
+    powers = [jnp.exp2((s - t) * factor) for s, t in zip(scores, tops)]
+    sums = [jnp.sum(p, 0, keepdims=True) for p in powers]
+    weights = [(p * (1.0 / s)).astype(BF) for p, s in zip(powers, sums)]
+    attended = [dot(w, v, 0, 0).astype(BF).astype(F32) for w, v in zip(weights, values)]
+    mean = sum(jnp.sum(a * a, -1, keepdims=True) for a in attended) / q_ref.shape[1]
+    inverse = lax.rsqrt(mean + 1e-06)
+    for a, h in zip(attended, heads):
+        out_ref[0, :, h] = (a * inverse).astype(BF)
     out_ref[1] = scaled_ref[...]
 
 
@@ -218,7 +226,7 @@
     out_ref[1] = dot(keys, matrix(mine_ref, 1))
 
 
-def apply_kernel(own_ref, part_ref, mine_ref, theirs_ref, out_ref):
+def apply_kernel(own_ref, part_ref, mine_ref, theirs_ref, out_hbm, out_ref, sems):
     core = lax.axis_index("row_2")
     half = HD // 2
     keys = own_ref[0, :, pl.ds(pl.multiple_of((1 - core) * half, half), half)]
@@ -226,7 +234,16 @@
     third = part_ref[1] + dot(keys, matrix(theirs_ref, 1))
     applied = first * jax.nn.sigmoid(first) * third
     a_mine, a_theirs = own_half(applied, core).astype(BF), own_half(applied, 1 - core).astype(BF)
-    out_ref[...] = (dot(a_mine, matrix(mine_ref, 2)) + dot(a_theirs, matrix(theirs_ref, 2))).astype(BF)
+    rows = out_ref.shape[0] // 2
+    copies = []
+    for n in range(2):
+        lines = slice(n * rows, (n + 1) * rows)
+        out_ref[lines, :] = (dot(a_mine[lines], matrix(mine_ref, 2)) + dot(a_theirs[lines], matrix(theirs_ref, 2))).astype(BF)
+        at = pl.ds(n * rows, rows)
+        copies.append(pltpu.make_async_copy(out_ref.at[at], out_hbm.at[at], sems.at[n]))
+        copies[n].start()
+    for c in copies:
+        c.wait()
 
 
 def per_device(query_feats, key_feats, value_feats, target, token_rates, row_reach, view_counts, w_first, w_third, w_second):
@@ -240,17 +257,21 @@
 
     block, edge = ((tokens, width), BF), ((2, near, width), BF)
     query, key, value, aim = (in_hbm(flat(x)) for x in (query_feats, key_feats, value_feats, target))
-    to_core, to_chip, query, key, value, aim, rates = call(edges_kernel, [edge] * 2 + [block] * 4 + [((1, tokens), F32)], [HBM] * 5, 9)(
-        query, key, value, aim, in_hbm(token_rates[0])
-    )
+    row_of = lambda dtype: ((1, tokens), dtype)
+    to_core, to_chip, query, key, value, aim, rates, reach = call(
+        lambda *refs: edges_kernel(cols, *refs),
+        [edge] * 2 + [block] * 4 + [row_of(F32), row_of(jnp.int32)],
+        [HBM] * 6,
+        [pltpu.SemaphoreType.DMA((10,)), pltpu.SMEM(row_reach.shape, jnp.int32)],
+    )(query, key, value, aim, in_hbm(token_rates[0]), in_hbm(row_reach))
     next_chip = [p for i in range(1, n_row - 1, 2) for p in ((i, i + 1), (i + 1, i))]
     from_chip = lax.ppermute(to_chip, ROW, next_chip)
     from_core = lax.ppermute(to_core, "row_2", SWAP)
 
     scaled = call(lambda *refs: scale_kernel(tokens, *refs), block, [SMEM] + [VMEM] * 3)(view_counts, to_core, rates, aim)
     attend = lambda *refs: attend_kernel(rows, cols, n_row * rows, *refs)
-    own = call(attend, ((2, tokens, width), BF), [SMEM] * 2 + [VMEM] * 6)(
-        view_counts, row_reach, query, key, value, from_core, from_chip, scaled
+    own = call(attend, ((2, tokens, width), BF), [SMEM] + [VMEM] * 7)(
+        view_counts, reach, query, key, value, from_core, from_chip, scaled
     )
     other = lax.ppermute(own, "row_2", SWAP)
     ws = w_first[0], w_third[0], w_second[0]
@@ -270,7 +291,8 @@
     mine = exchange(lines, PLANE)
     theirs = lax.ppermute(mine, "row_2", SWAP)
     part = call(half_kernel, ((2, tokens, width), F32), [VMEM] * 2)(own, mine)
-    out = call(apply_kernel, ((tokens, width), BF), [VMEM] * 4)(own, part, mine, theirs)
+    scratch = [pltpu.VMEM((tokens, width), BF), pltpu.SemaphoreType.DMA((2,))]
+    out = call(apply_kernel, block, [VMEM] * 4, scratch, HBM)(own, part, mine, theirs)
     return out.reshape(1, rows, cols, width)
 
 

time: 98 us -> 96.7 us (0.987)
  Pallas kernels: 6.42 us -> 5.2 us
    pallas_call x3, Pallas kernels: 4.33 us -> 3.12 us  [the longest x1 1.33 us: per_device(): call(lambda *refs: edges_kernel(cols, *refs), [edge] * 2 + [block] * 4 +...]
where the time goes in v6:
time: 96.7 us; the launch traced here: 96.3 us
  blocking collectives  67.7 us (70%)
  starting transfers between devices  20.3 us (21%)
  Pallas kernels  5.2 us (5%)
  waiting for transfers between devices  2.36 us (2%)
    all_to_all x5, blocking collectives, exchange(): return lax.all_to_all(x, axes, 0, 0, tiled=True)  67.7 us
    ppermute x1, starting transfers between devices, per_device(): theirs = lax.ppermute(mine, 'row_2', SWAP)  8.57 us
    ppermute x1, starting transfers between devices, per_device(): from_core = lax.ppermute(to_core, 'row_2', SWAP)  4.94 us
    ppermute x1, starting transfers between devices, per_device(): from_chip = lax.ppermute(to_chip, ROW, next_chip)  4.51 us
    ppermute x1, starting transfers between devices, per_device(): other = lax.ppermute(own, 'row_2', SWAP)  2.26 us
  transfers between devices with their start and end apart: 4, of which 3 were waited for; matrix products, arithmetic and copies ran while one was open for 0% of the time, Pallas kernels for 1%

profile of v6, /device:TPU:1, one launch (start us, length us, event | category | flops | bytes accessed | tf_op | source)
XLA Modules:
  0.0 96.3 jit_solution(18107735781459530788)
XLA Ops:
  0.0 0.0 copy-start.2
  0.0 1.3 %shard_map.100 = (bf16[2,32,512]{2,1,0:T(8,128)(2,1)S(1)}, bf16[2,32,512]{2,1,0:T(8,128)(2,1)S(1)}, bf16[128,512]{1,0:T(8,128)(2,1)S(1)}, bf16[128,512]{1,0:T(8,...) custom-call(bf16[128,512]{1,0:T(8,128)(2,1)} %bitcast.15, ...), custom_call_target="tpu_custom_call" | custom-call | flops 1048576 | bytes 1048576 | tf_op jit(solution)/shard_map/pallas_call | solution.py:261
  1.3 4.5 %collective-permute-start.1 = (bf16[2,32,512]{2,1,0:T(8,128)(2,1)S(1)}, bf16[2,32,512]{2,1,0:T(8,128)(2,1)S(1)}, u32[]{:S(2)}, u32[]{:S(2)}) collective-permute-start(bf16[2,32,512]{2,1,0:T(8,128)(2,1)S(1)} %get-tuple-element.21), channel_id=1, source_target_pairs={{1,2},{2,1},{3,4},{4,3},{5,6},{6,5},{7,8},{8,7},{9,10},{10,9},{11,... | collective-permute-start | bytes 196616 | tf_op jit(solution)/shard_map/ppermute | solution.py:268
  5.9 4.9 %collective-permute-start = (bf16[2,32,512]{2,1,0:T(8,128)(2,1)S(1)}, bf16[2,32,512]{2,1,0:T(8,128)(2,1)S(1)}, u32[]{:S(2)}, u32[]{:S(2)}) collective-permute-start(bf16[2,32,512]{2,1,0:T(8,128)(2,1)S(1)} %get-tuple-element.20.refs_1_), channel_id=1, source_target_pairs={{0,1},{1,0},{2,3},{3,2},{4,5},{5,4},{6,7},{7,6},{8,9},{9,8},{10,11... | collective-permute-start | bytes 196616 | tf_op jit(solution)/shard_map/ppermute | solution.py:269
  11.5 0.0 copy-start.1
  11.5 0.1 shard_map.101.refs_7_
  11.6 0.0 copy-start
  11.6 0.0 collective-permute-done.1.refs_6_
  11.6 0.1 collective-permute-done.refs_5_
  11.7 0.7 shard_map.102.refs_0_.own_ref
  12.4 2.3 %collective-permute-start.2 = (bf16[2,128,512]{2,1,0:T(8,128)(2,1)S(1)}, bf16[2,128,512]{2,1,0:T(8,128)(2,1)S(1)}, u32[]{:S(2)}, u32[]{:S(2)}) collective-permute-start(bf16[2,128,512]{2,1,0:T(8,128)(2,1)S(1)} %shard_map.102.refs_0_.own_ref), channel_id=1, source_target_pairs={{0,1},{1,0},{2,3},{3,2},{4,5},{5,4},{6,7},{7,6},{8,9},{9,8},{10,11... | collective-permute-start | bytes 786440 | tf_op jit(solution)/shard_map/ppermute | solution.py:276
  14.6 0.0 copy-done.2
  14.6 0.0 copy-done.1
  14.7 0.0 copy-done
  14.7 0.5 shard_map.103
  15.2 0.6 collective-permute-done.2.refs_3_
  15.8 0.8 shard_map.104
  16.6 15.5 %all_to_all.25.refs_1_ = bf16[8,96,512]{2,1,0:T(8,128)(2,1)S(1)} all-to-all(bf16[8,96,512]{2,1,0:T(8,128)(2,1)S(1)} %shard_map.104), channel_id=1, replica_groups=mesh['head'=2,'far'=4,'near'=4,'row_0'=2,'row_1'=4,'row_2'=2] {'row_0','..., dimensions={0} | all-to-all | bytes 1572864 | tf_op jit(solution)/shard_map/all_to_all | solution.py:29
  32.1 0.1 shard_map.105
  32.2 9.6 %all_to_all.26.x_ref = bf16[4,8,1664]{2,1,0:T(8,128)(2,1)S(1)} all-to-all(bf16[4,8,1664]{2,1,0:T(8,128)(2,1)S(1)} %shard_map.105), channel_id=1, replica_groups=mesh['head'=2,'far'=4,'near'=4,'row_0'=2,'row_1'=4,'row_2'=2] {'near'}, dimensions={0} | all-to-all | bytes 212992 | tf_op jit(solution)/shard_map/all_to_all | solution.py:29
  41.8 23.8 %all_to_all.27.x_ref = bf16[4,8,1664]{2,1,0:T(8,128)(2,1)S(1)} all-to-all(bf16[4,8,1664]{2,1,0:T(8,128)(2,1)S(1)} %shard_map.106), channel_id=1, replica_groups=mesh['head'=2,'far'=4,'near'=4,'row_0'=2,'row_1'=4,'row_2'=2] {'far'}, dimensions={0} | all-to-all | bytes 212992 | tf_op jit(solution)/shard_map/all_to_all | solution.py:29
  65.6 0.2 shard_map.107
  65.8 7.4 %all_to_all.28.x_ref = bf16[4,8,1536]{2,1,0:T(8,128)(2,1)S(1)} all-to-all(bf16[4,8,1536]{2,1,0:T(8,128)(2,1)S(1)} %shard_map.107), channel_id=1, replica_groups=mesh['head'=2,'far'=4,'near'=4,'row_0'=2,'row_1'=4,'row_2'=2] {'near'}, dimensions={0} | all-to-all | bytes 196608 | tf_op jit(solution)/shard_map/all_to_all | solution.py:29
  73.3 0.1 shard_map.108
  73.3 11.4 %all_to_all.29.mine_ref = bf16[8,96,512]{2,1,0:T(8,128)(2,1)S(1)} all-to-all(bf16[8,96,512]{2,1,0:T(8,128)(2,1)S(1)} %shard_map.108), channel_id=1, replica_groups=mesh['head'=2,'far'=4,'near'=4,'row_0'=2,'row_1'=4,'row_2'=2] {'row_0','..., dimensions={0} | all-to-all | bytes 1572864 | tf_op jit(solution)/shard_map/all_to_all | solution.py:29
  84.7 8.6 %collective-permute-start.3 = (bf16[8,96,512]{2,1,0:T(8,128)(2,1)S(1)}, bf16[8,96,512]{2,1,0:T(8,128)(2,1)S(1)}, u32[]{:S(2)}, u32[]{:S(2)}) collective-permute-start(bf16[8,96,512]{2,1,0:T(8,128)(2,1)S(1)} %all_to_all.29.mine_ref), channel_id=1, source_target_pairs={{0,1},{1,0},{2,3},{3,2},{4,5},{5,4},{6,7},{7,6},{8,9},{9,8},{10,11... | collective-permute-start | bytes 2359304 | tf_op jit(solution)/shard_map/ppermute | solution.py:292
  93.3 0.2 shard_map.109.part_ref
  93.6 1.7 %collective-permute-done.3.theirs_ref = bf16[8,96,512]{2,1,0:T(8,128)(2,1)S(1)} collective-permute-done((bf16[8,96,512]{2,1,0:T(8,128)(2,1)S(1)}, bf16[8,96,512]{2,1,0:T(8,128)(2,1)S(1)}, u32[]{:S(2)}, u32[]{:S(2)}) %collective-permute-start.3) | collective-permute-done | bytes 786464 | tf_op jit(solution)/shard_map/ppermute | solution.py:292
  95.2 1.1 %shard_map.110 = bf16[128,512]{1,0:T(8,128)(2,1)} custom-call(bf16[2,128,512]{2,1,0:T(8,128)(2,1)S(1)} %shard_map.102.refs_0_.own_ref, f32[2,128,512]{2,1,0:T(8,128)S(1)} %shard_map.109.part_ref, bf16[8,96,512]{2,1,0:T(8,128)(2,1)S(1)} %all_to_all.29.mine_ref, bf16[8,96,512]{2,1,0:T(8,128)(2,1)S(1)} %collective-permute-done.3.theirs_ref), custom_call_target="tpu_custom_call" | custom-call | flops 1048576 | bytes 1048576 | tf_op jit(solution)/shard_map/pallas_call | solution.py:295
  (1 shorter events, 0.0 us)
Async XLA Ops:
  0.0 14.6 %copy-start.2 = (bf16[1,512,512]{2,1,0:T(8,128)(2,1)S(1)}, bf16[1,512,512]{2,1,0:T(8,128)(2,1)}, u32[]{:S(2)}) copy-start(bf16[1,512,512]{2,1,0:T(8,128)(2,1)} %param.19) | copy-start | bytes 1572868
  1.3 10.3 %collective-permute-start.1 = (bf16[2,32,512]{2,1,0:T(8,128)(2,1)S(1)}, bf16[2,32,512]{2,1,0:T(8,128)(2,1)S(1)}, u32[]{:S(2)}, u32[]{:S(2)}) collective-permute-start(bf16[2,32,512]{2,1,0:T(8,128)(2,1)S(1)} %get-tuple-element.21), channel_id=1, source_target_pairs={{1,2},{2,1},{3,4},{4,3},{5,6},{6,5},{7,8},{8,7},{9,10},{10,9},{11,... | collective-permute-start | bytes 196616 | tf_op jit(solution)/shard_map/ppermute | solution.py:268
  5.9 5.8 %collective-permute-start = (bf16[2,32,512]{2,1,0:T(8,128)(2,1)S(1)}, bf16[2,32,512]{2,1,0:T(8,128)(2,1)S(1)}, u32[]{:S(2)}, u32[]{:S(2)}) collective-permute-start(bf16[2,32,512]{2,1,0:T(8,128)(2,1)S(1)} %get-tuple-element.20.refs_1_), channel_id=1, source_target_pairs={{0,1},{1,0},{2,3},{3,2},{4,5},{5,4},{6,7},{7,6},{8,9},{9,8},{10,11... | collective-permute-start | bytes 196616 | tf_op jit(solution)/shard_map/ppermute | solution.py:269
  11.5 3.2 %copy-start.1 = (bf16[1,512,512]{2,1,0:T(8,128)(2,1)S(1)}, bf16[1,512,512]{2,1,0:T(8,128)(2,1)}, u32[]{:S(2)}) copy-start(bf16[1,512,512]{2,1,0:T(8,128)(2,1)} %param.18) | copy-start | bytes 1572868
  11.6 3.1 %copy-start = (bf16[1,512,512]{2,1,0:T(8,128)(2,1)S(1)}, bf16[1,512,512]{2,1,0:T(8,128)(2,1)}, u32[]{:S(2)}) copy-start(bf16[1,512,512]{2,1,0:T(8,128)(2,1)} %param.17) | copy-start | bytes 1572868
  12.4 3.4 %collective-permute-start.2 = (bf16[2,128,512]{2,1,0:T(8,128)(2,1)S(1)}, bf16[2,128,512]{2,1,0:T(8,128)(2,1)S(1)}, u32[]{:S(2)}, u32[]{:S(2)}) collective-permute-start(bf16[2,128,512]{2,1,0:T(8,128)(2,1)S(1)} %shard_map.102.refs_0_.own_ref), channel_id=1, source_target_pairs={{0,1},{1,0},{2,3},{3,2},{4,5},{5,4},{6,7},{7,6},{8,9},{9,8},{10,11... | collective-permute-start | bytes 786440 | tf_op jit(solution)/shard_map/ppermute | solution.py:276
  84.7 10.5 %collective-permute-start.3 = (bf16[8,96,512]{2,1,0:T(8,128)(2,1)S(1)}, bf16[8,96,512]{2,1,0:T(8,128)(2,1)S(1)}, u32[]{:S(2)}, u32[]{:S(2)}) collective-permute-start(bf16[8,96,512]{2,1,0:T(8,128)(2,1)S(1)} %all_to_all.29.mine_ref), channel_id=1, source_target_pairs={{0,1},{1,0},{2,3},{3,2},{4,5},{5,4},{6,7},{7,6},{8,9},{9,8},{10,11... | collective-permute-start | bytes 2359304 | tf_op jit(solution)/shard_map/ppermute | solution.py:292

commit v7 on v6

--- a/solution.py
+++ b/solution.py
@@ -284,7 +284,8 @@
     part = call(spread, ((n_near, few, 3 * width + 128), BF), [SMEM, VMEM])(view_counts, part)
     part = exchange(part, "near")
     part = call(gather_kernel, ((n_far, few, 3 * width + 128), BF), [VMEM])(part)
-    part = exchange(part, "far")
+    groups = [[(n_near * ((f + 2) % n_far)) + u for f in range(n_far)] for u in range(n_near)]
+    part = lax.all_to_all(part, ("far", "near"), 0, 0, tiled=True, axis_index_groups=groups)
     new = call(renew_kernel, ((n_near, few, 3 * width), BF), [VMEM] * 2)(part, old)
     new = exchange(new, "near")
     lines = call(order_kernel, ((n_plane, 3 * share, width), BF), [VMEM])(new)

time: 96.7 us -> 89.1 us (0.921)
  blocking collectives: 67.7 us -> 61 us
    all_to_all x5 -> x4, blocking collectives: 67.7 us -> 44.4 us  [exchange(): return lax.all_to_all(x, axes, 0, 0, tiled=True)]
    all_to_all x0 -> x1, blocking collectives: none -> 16.6 us  [per_device(): lax.all_to_all(part, ('far', 'near'), 0, 0, tiled=True, axis_index_groups...]
where the time goes in v7:
time: 89.1 us; the launch traced here: 88.7 us
  blocking collectives  61 us (68%)
  starting transfers between devices  19.4 us (22%)
  Pallas kernels  5.2 us (6%)
  waiting for transfers between devices  2.36 us (3%)
    all_to_all x4, blocking collectives, exchange(): return lax.all_to_all(x, axes, 0, 0, tiled=True)  44.4 us
    all_to_all x1, blocking collectives, per_device(): lax.all_to_all(part, ('far', 'near'), 0, 0, tiled=True, axis_index_groups...  16.6 us
    ppermute x1, starting transfers between devices, per_device(): theirs = lax.ppermute(mine, 'row_2', SWAP)  7.65 us
    ppermute x1, starting transfers between devices, per_device(): from_core = lax.ppermute(to_core, 'row_2', SWAP)  4.94 us
    ppermute x1, starting transfers between devices, per_device(): from_chip = lax.ppermute(to_chip, ROW, next_chip)  4.51 us
    ppermute x1, starting transfers between devices, per_device(): other = lax.ppermute(own, 'row_2', SWAP)  2.26 us
  transfers between devices with their start and end apart: 4, of which 3 were waited for; matrix products, arithmetic and copies ran while one was open for 0% of the time, Pallas kernels for 1%

profile of v7, /device:TPU:1, one launch (start us, length us, event | category | flops | bytes accessed | tf_op | source)
XLA Modules:
  0.0 88.7 jit_solution(17392368714081329883)
XLA Ops:
  0.0 0.0 copy-start.2
  0.0 1.3 %shard_map.100 = (bf16[2,32,512]{2,1,0:T(8,128)(2,1)S(1)}, bf16[2,32,512]{2,1,0:T(8,128)(2,1)S(1)}, bf16[128,512]{1,0:T(8,128)(2,1)S(1)}, bf16[128,512]{1,0:T(8,...) custom-call(bf16[128,512]{1,0:T(8,128)(2,1)} %bitcast.15, ...), custom_call_target="tpu_custom_call" | custom-call | flops 1048576 | bytes 1048576 | tf_op jit(solution)/shard_map/pallas_call | solution.py:261
  1.3 4.5 %collective-permute-start.1 = (bf16[2,32,512]{2,1,0:T(8,128)(2,1)S(1)}, bf16[2,32,512]{2,1,0:T(8,128)(2,1)S(1)}, u32[]{:S(2)}, u32[]{:S(2)}) collective-permute-start(bf16[2,32,512]{2,1,0:T(8,128)(2,1)S(1)} %get-tuple-element.21), channel_id=1, source_target_pairs={{1,2},{2,1},{3,4},{4,3},{5,6},{6,5},{7,8},{8,7},{9,10},{10,9},{11,... | collective-permute-start | bytes 196616 | tf_op jit(solution)/shard_map/ppermute | solution.py:268
  5.9 4.9 %collective-permute-start = (bf16[2,32,512]{2,1,0:T(8,128)(2,1)S(1)}, bf16[2,32,512]{2,1,0:T(8,128)(2,1)S(1)}, u32[]{:S(2)}, u32[]{:S(2)}) collective-permute-start(bf16[2,32,512]{2,1,0:T(8,128)(2,1)S(1)} %get-tuple-element.20.refs_1_), channel_id=1, source_target_pairs={{0,1},{1,0},{2,3},{3,2},{4,5},{5,4},{6,7},{7,6},{8,9},{9,8},{10,11... | collective-permute-start | bytes 196616 | tf_op jit(solution)/shard_map/ppermute | solution.py:269
  11.5 0.0 copy-start.1
  11.5 0.1 shard_map.101.refs_7_
  11.6 0.0 copy-start
  11.6 0.0 collective-permute-done.1.refs_6_
  11.6 0.1 collective-permute-done.refs_5_
  11.7 0.7 shard_map.102.refs_0_.own_ref
  12.4 2.3 %collective-permute-start.2 = (bf16[2,128,512]{2,1,0:T(8,128)(2,1)S(1)}, bf16[2,128,512]{2,1,0:T(8,128)(2,1)S(1)}, u32[]{:S(2)}, u32[]{:S(2)}) collective-permute-start(bf16[2,128,512]{2,1,0:T(8,128)(2,1)S(1)} %shard_map.102.refs_0_.own_ref), channel_id=1, source_target_pairs={{0,1},{1,0},{2,3},{3,2},{4,5},{5,4},{6,7},{7,6},{8,9},{9,8},{10,11... | collective-permute-start | bytes 786440 | tf_op jit(solution)/shard_map/ppermute | solution.py:276
  14.6 0.0 copy-done.2
  14.6 0.0 copy-done.1
  14.7 0.0 copy-done
  14.7 0.5 shard_map.103
  15.2 0.6 collective-permute-done.2.refs_3_
  15.8 0.8 shard_map.104
  16.6 15.5 %all_to_all.25.refs_1_ = bf16[8,96,512]{2,1,0:T(8,128)(2,1)S(1)} all-to-all(bf16[8,96,512]{2,1,0:T(8,128)(2,1)S(1)} %shard_map.104), channel_id=1, replica_groups=mesh['head'=2,'far'=4,'near'=4,'row_0'=2,'row_1'=4,'row_2'=2] {'row_0','..., dimensions={0} | all-to-all | bytes 1572864 | tf_op jit(solution)/shard_map/all_to_all | solution.py:29
  32.1 0.1 shard_map.105
  32.2 9.6 %all_to_all.26.x_ref = bf16[4,8,1664]{2,1,0:T(8,128)(2,1)S(1)} all-to-all(bf16[4,8,1664]{2,1,0:T(8,128)(2,1)S(1)} %shard_map.105), channel_id=1, replica_groups=mesh['head'=2,'far'=4,'near'=4,'row_0'=2,'row_1'=4,'row_2'=2] {'near'}, dimensions={0} | all-to-all | bytes 212992 | tf_op jit(solution)/shard_map/all_to_all | solution.py:29
  41.8 16.6 %all_to_all.27.x_ref = bf16[4,8,1664]{2,1,0:T(8,128)(2,1)S(1)} all-to-all(bf16[4,8,1664]{2,1,0:T(8,128)(2,1)S(1)} %shard_map.106), channel_id=1, replica_groups={{128,192,0,64},{144,208,16,80},{160,224,32,96},{176,240,48,112},{129,19..., dimensions={0} | all-to-all | bytes 212992 | tf_op jit(solution)/shard_map/all_to_all | solution.py:288
  58.4 0.2 shard_map.107
  58.6 7.2 %all_to_all.28.x_ref = bf16[4,8,1536]{2,1,0:T(8,128)(2,1)S(1)} all-to-all(bf16[4,8,1536]{2,1,0:T(8,128)(2,1)S(1)} %shard_map.107), channel_id=1, replica_groups=mesh['head'=2,'far'=4,'near'=4,'row_0'=2,'row_1'=4,'row_2'=2] {'near'}, dimensions={0} | all-to-all | bytes 196608 | tf_op jit(solution)/shard_map/all_to_all | solution.py:29
  65.8 0.1 shard_map.108
  65.9 12.2 %all_to_all.29.mine_ref = bf16[8,96,512]{2,1,0:T(8,128)(2,1)S(1)} all-to-all(bf16[8,96,512]{2,1,0:T(8,128)(2,1)S(1)} %shard_map.108), channel_id=1, replica_groups=mesh['head'=2,'far'=4,'near'=4,'row_0'=2,'row_1'=4,'row_2'=2] {'row_0','..., dimensions={0} | all-to-all | bytes 1572864 | tf_op jit(solution)/shard_map/all_to_all | solution.py:29
  78.1 7.6 %collective-permute-start.3 = (bf16[8,96,512]{2,1,0:T(8,128)(2,1)S(1)}, bf16[8,96,512]{2,1,0:T(8,128)(2,1)S(1)}, u32[]{:S(2)}, u32[]{:S(2)}) collective-permute-start(bf16[8,96,512]{2,1,0:T(8,128)(2,1)S(1)} %all_to_all.29.mine_ref), channel_id=1, source_target_pairs={{0,1},{1,0},{2,3},{3,2},{4,5},{5,4},{6,7},{7,6},{8,9},{9,8},{10,11... | collective-permute-start | bytes 2359304 | tf_op jit(solution)/shard_map/ppermute | solution.py:293
  85.7 0.2 shard_map.109.part_ref
  86.0 1.7 %collective-permute-done.3.theirs_ref = bf16[8,96,512]{2,1,0:T(8,128)(2,1)S(1)} collective-permute-done((bf16[8,96,512]{2,1,0:T(8,128)(2,1)S(1)}, bf16[8,96,512]{2,1,0:T(8,128)(2,1)S(1)}, u32[]{:S(2)}, u32[]{:S(2)}) %collective-permute-start.3) | collective-permute-done | bytes 786464 | tf_op jit(solution)/shard_map/ppermute | solution.py:293
  87.6 1.1 %shard_map.110 = bf16[128,512]{1,0:T(8,128)(2,1)} custom-call(bf16[2,128,512]{2,1,0:T(8,128)(2,1)S(1)} %shard_map.102.refs_0_.own_ref, f32[2,128,512]{2,1,0:T(8,128)S(1)} %shard_map.109.part_ref, bf16[8,96,512]{2,1,0:T(8,128)(2,1)S(1)} %all_to_all.29.mine_ref, bf16[8,96,512]{2,1,0:T(8,128)(2,1)S(1)} %collective-permute-done.3.theirs_ref), custom_call_target="tpu_custom_call" | custom-call | flops 1048576 | bytes 1048576 | tf_op jit(solution)/shard_map/pallas_call | solution.py:296
  (1 shorter events, 0.0 us)
Async XLA Ops:
  0.0 14.6 %copy-start.2 = (bf16[1,512,512]{2,1,0:T(8,128)(2,1)S(1)}, bf16[1,512,512]{2,1,0:T(8,128)(2,1)}, u32[]{:S(2)}) copy-start(bf16[1,512,512]{2,1,0:T(8,128)(2,1)} %param.19) | copy-start | bytes 1572868
  1.3 10.3 %collective-permute-start.1 = (bf16[2,32,512]{2,1,0:T(8,128)(2,1)S(1)}, bf16[2,32,512]{2,1,0:T(8,128)(2,1)S(1)}, u32[]{:S(2)}, u32[]{:S(2)}) collective-permute-start(bf16[2,32,512]{2,1,0:T(8,128)(2,1)S(1)} %get-tuple-element.21), channel_id=1, source_target_pairs={{1,2},{2,1},{3,4},{4,3},{5,6},{6,5},{7,8},{8,7},{9,10},{10,9},{11,... | collective-permute-start | bytes 196616 | tf_op jit(solution)/shard_map/ppermute | solution.py:268
  5.9 5.8 %collective-permute-start = (bf16[2,32,512]{2,1,0:T(8,128)(2,1)S(1)}, bf16[2,32,512]{2,1,0:T(8,128)(2,1)S(1)}, u32[]{:S(2)}, u32[]{:S(2)}) collective-permute-start(bf16[2,32,512]{2,1,0:T(8,128)(2,1)S(1)} %get-tuple-element.20.refs_1_), channel_id=1, source_target_pairs={{0,1},{1,0},{2,3},{3,2},{4,5},{5,4},{6,7},{7,6},{8,9},{9,8},{10,11... | collective-permute-start | bytes 196616 | tf_op jit(solution)/shard_map/ppermute | solution.py:269
  11.5 3.2 %copy-start.1 = (bf16[1,512,512]{2,1,0:T(8,128)(2,1)S(1)}, bf16[1,512,512]{2,1,0:T(8,128)(2,1)}, u32[]{:S(2)}) copy-start(bf16[1,512,512]{2,1,0:T(8,128)(2,1)} %param.18) | copy-start | bytes 1572868
  11.6 3.1 %copy-start = (bf16[1,512,512]{2,1,0:T(8,128)(2,1)S(1)}, bf16[1,512,512]{2,1,0:T(8,128)(2,1)}, u32[]{:S(2)}) copy-start(bf16[1,512,512]{2,1,0:T(8,128)(2,1)} %param.17) | copy-start | bytes 1572868
  12.4 3.4 %collective-permute-start.2 = (bf16[2,128,512]{2,1,0:T(8,128)(2,1)S(1)}, bf16[2,128,512]{2,1,0:T(8,128)(2,1)S(1)}, u32[]{:S(2)}, u32[]{:S(2)}) collective-permute-start(bf16[2,128,512]{2,1,0:T(8,128)(2,1)S(1)} %shard_map.102.refs_0_.own_ref), channel_id=1, source_target_pairs={{0,1},{1,0},{2,3},{3,2},{4,5},{5,4},{6,7},{7,6},{8,9},{9,8},{10,11... | collective-permute-start | bytes 786440 | tf_op jit(solution)/shard_map/ppermute | solution.py:276
  78.1 9.5 %collective-permute-start.3 = (bf16[8,96,512]{2,1,0:T(8,128)(2,1)S(1)}, bf16[8,96,512]{2,1,0:T(8,128)(2,1)S(1)}, u32[]{:S(2)}, u32[]{:S(2)}) collective-permute-start(bf16[8,96,512]{2,1,0:T(8,128)(2,1)S(1)} %all_to_all.29.mine_ref), channel_id=1, source_target_pairs={{0,1},{1,0},{2,3},{3,2},{4,5},{5,4},{6,7},{7,6},{8,9},{9,8},{10,11... | collective-permute-start | bytes 2359304 | tf_op jit(solution)/shard_map/ppermute | solution.py:293

commit v8 on v6

--- a/solution.py
+++ b/solution.py
@@ -25,8 +25,14 @@
     return lax.dot_general(a, b, (((ca,), (cb,)), ((), ())), preferred_element_type=F32)
 
 
-def exchange(x, axes):
-    return lax.all_to_all(x, axes, 0, 0, tiled=True)
+def led(axes, leader):
+    order = list(range(lax.axis_size(axes)))
+    order[0], order[leader] = leader, 0
+    return order
+
+
+def exchange(x, axes, order):
+    return lax.all_to_all(x, axes, 0, 0, tiled=True, axis_index_groups=[order])
 
 
 def iota(shape, dim):
@@ -152,10 +158,10 @@
         old_ref[:, k * HD : (k + 1) * HD] = dot(pick, ref[pl.ds(base, share), :])
 
 
-def grads_kernel(n_plane, own_ref, mine_ref, mine_gated_ref, other_ref, w1_ref, w3_ref, w2_ref, out_ref):
+def grads_kernel(order, own_ref, mine_ref, mine_gated_ref, other_ref, w1_ref, w3_ref, w2_ref, out_ref):
     core = lax.axis_index("row_2")
     half = HD // 2
-    share = half // n_plane
+    share = half // len(order)
     back_first, back_third, gated = forward(other_ref[0], other_ref[1], w1_ref, w3_ref, w2_ref)
     lanes = pl.ds(pl.multiple_of(core * half, half), half)
     both = lambda a, b: jnp.concatenate([a, b], 0)
@@ -168,22 +174,23 @@
     )
     for k, (a, b) in enumerate(pairs):
         g = dot(a, b, 0, 0).astype(BF)
-        out_ref[:, k * share : (k + 1) * share, :] = g.reshape(n_plane, share, HD)
-
-
-def spread_kernel(n_near, few, count_ref, x_ref, out_ref):
+        for n, p in enumerate(order):
+            out_ref[n, k * share : (k + 1) * share, :] = g[p * share : (p + 1) * share]
+
+
+def spread_kernel(order, few, count_ref, x_ref, out_ref):
     total = jnp.sum(x_ref[...].astype(F32), 0)
     share = total.shape[0] // 3
     for k in range(3):
-        for u in range(n_near):
+        for n, u in enumerate(order):
             at = k * share + u * few
-            out_ref[u, :, k * HD : (k + 1) * HD] = total[at : at + few].astype(BF)
+            out_ref[n, :, k * HD : (k + 1) * HD] = total[at : at + few].astype(BF)
     count = count_ref[0]
     lane = iota((few, 128), 1)
     digits = jnp.where(lane == 0, count % 16, jnp.where(lane == 1, (count // 16) % 16, count // 256))
     digits = digits.astype(F32).astype(BF)
-    for u in range(n_near):
-        out_ref[u, :, 3 * HD :] = digits
+    for n in range(len(order)):
+        out_ref[n, :, 3 * HD :] = digits
 
 
 def gather_kernel(x_ref, out_ref):
@@ -207,38 +214,37 @@
             out_ref[u, :, lanes] = new
 
 
-def order_kernel(x_ref, out_ref):
-    n_near = x_ref.shape[0]
+def order_kernel(order, x_ref, out_ref):
     x = x_ref[...].astype(F32)
-    lines = jnp.concatenate([x[u, :, k * HD : (k + 1) * HD] for k in range(3) for u in range(n_near)], 0).astype(BF)
+    lines = jnp.concatenate([x[n, :, k * HD : (k + 1) * HD] for k in range(3) for n in order], 0).astype(BF)
     out_ref[...] = jnp.broadcast_to(lines[None], out_ref.shape)
 
 
-def matrix(ref, k):
+def matrix(order, ref, k):
     share = ref.shape[1] // 3
-    return ref[:, k * share : (k + 1) * share, :].reshape(ref.shape[0] * share, HD)
-
-
-def half_kernel(own_ref, mine_ref, out_ref):
+    return jnp.concatenate([ref[n, k * share : (k + 1) * share, :] for n in order], 0)
+
+
+def half_kernel(order, own_ref, mine_ref, out_ref):
     half = HD // 2
     keys = own_ref[0, :, pl.ds(pl.multiple_of(lax.axis_index("row_2") * half, half), half)]
-    out_ref[0] = dot(keys, matrix(mine_ref, 0))
-    out_ref[1] = dot(keys, matrix(mine_ref, 1))
-
-
-def apply_kernel(own_ref, part_ref, mine_ref, theirs_ref, out_hbm, out_ref, sems):
+    out_ref[0] = dot(keys, matrix(order, mine_ref, 0))
+    out_ref[1] = dot(keys, matrix(order, mine_ref, 1))
+
+
+def apply_kernel(order, own_ref, part_ref, mine_ref, theirs_ref, out_hbm, out_ref, sems):
     core = lax.axis_index("row_2")
     half = HD // 2
     keys = own_ref[0, :, pl.ds(pl.multiple_of((1 - core) * half, half), half)]
-    first = part_ref[0] + dot(keys, matrix(theirs_ref, 0))
-    third = part_ref[1] + dot(keys, matrix(theirs_ref, 1))
+    first = part_ref[0] + dot(keys, matrix(order, theirs_ref, 0))
+    third = part_ref[1] + dot(keys, matrix(order, theirs_ref, 1))
     applied = first * jax.nn.sigmoid(first) * third
     a_mine, a_theirs = own_half(applied, core).astype(BF), own_half(applied, 1 - core).astype(BF)
     rows = out_ref.shape[0] // 2
     copies = []
     for n in range(2):
         lines = slice(n * rows, (n + 1) * rows)
-        out_ref[lines, :] = (dot(a_mine[lines], matrix(mine_ref, 2)) + dot(a_theirs[lines], matrix(theirs_ref, 2))).astype(BF)
+        out_ref[lines, :] = (dot(a_mine[lines], matrix(order, mine_ref, 2)) + dot(a_theirs[lines], matrix(order, theirs_ref, 2))).astype(BF)
         at = pl.ds(n * rows, rows)
         copies.append(pltpu.make_async_copy(out_ref.at[at], out_hbm.at[at], sems.at[n]))
         copies[n].start()
@@ -277,22 +283,23 @@
     ws = w_first[0], w_third[0], w_second[0]
     ahead = lambda *refs: forward_kernel(n_plane, n_near, *refs)
     back, gated, old = call(ahead, [((2, tokens, width), BF), ((tokens, width // 2), BF), ((few, 3 * width), F32)], [VMEM] * 4)(own, *ws)
-    grads = lambda *refs: grads_kernel(n_plane, *refs)
+    planes, nears = led(PLANE, n_plane - 2), led("near", n_near - 2)
+    grads = lambda *refs: grads_kernel(planes, *refs)
     part = call(grads, ((n_plane, 3 * share, width), BF), [VMEM] * 7)(own, back, gated, other, *ws)
-    part = exchange(part, PLANE)
-    spread = lambda *refs: spread_kernel(n_near, few, *refs)
+    part = exchange(part, PLANE, planes)
+    spread = lambda *refs: spread_kernel(nears, few, *refs)
     part = call(spread, ((n_near, few, 3 * width + 128), BF), [SMEM, VMEM])(view_counts, part)
-    part = exchange(part, "near")
+    part = exchange(part, "near", nears)
     part = call(gather_kernel, ((n_far, few, 3 * width + 128), BF), [VMEM])(part)
-    part = exchange(part, "far")
+    part = exchange(part, "far", led("far", n_far // 2))
     new = call(renew_kernel, ((n_near, few, 3 * width), BF), [VMEM] * 2)(part, old)
-    new = exchange(new, "near")
-    lines = call(order_kernel, ((n_plane, 3 * share, width), BF), [VMEM])(new)
-    mine = exchange(lines, PLANE)
+    new = exchange(new, "near", nears)
+    lines = call(lambda *refs: order_kernel(nears, *refs), ((n_plane, 3 * share, width), BF), [VMEM])(new)
+    mine = exchange(lines, PLANE, planes)
     theirs = lax.ppermute(mine, "row_2", SWAP)
-    part = call(half_kernel, ((2, tokens, width), F32), [VMEM] * 2)(own, mine)
+    part = call(lambda *refs: half_kernel(planes, *refs), ((2, tokens, width), F32), [VMEM] * 2)(own, mine)
     scratch = [pltpu.VMEM((tokens, width), BF), pltpu.SemaphoreType.DMA((2,))]
-    out = call(apply_kernel, block, [VMEM] * 4, scratch, HBM)(own, part, mine, theirs)
+    out = call(lambda *refs: apply_kernel(planes, *refs), block, [VMEM] * 4, scratch, HBM)(own, part, mine, theirs)
     return out.reshape(1, rows, cols, width)
 
 

time: 96.7 us -> 86.4 us (0.89)
  blocking collectives: 67.7 us -> 57.1 us
    all_to_all x5, blocking collectives: 67.7 us -> 57.1 us  [exchange(): return lax.all_to_all(x, axes, 0, 0, tiled=True, axis_index_groups=[order])]
where the time goes in v8:
time: 86.4 us; the launch traced here: 86.1 us
  blocking collectives  57.1 us (66%)
  starting transfers between devices  20.6 us (24%)
  Pallas kernels  5.2 us (6%)
  waiting for transfers between devices  2.36 us (3%)
    all_to_all x5, blocking collectives, exchange(): return lax.all_to_all(x, axes, 0, 0, tiled=True, axis_index_groups=[order])  57.1 us
    ppermute x1, starting transfers between devices, per_device(): theirs = lax.ppermute(mine, 'row_2', SWAP)  8.91 us
    ppermute x1, starting transfers between devices, per_device(): from_core = lax.ppermute(to_core, 'row_2', SWAP)  4.94 us
    ppermute x1, starting transfers between devices, per_device(): from_chip = lax.ppermute(to_chip, ROW, next_chip)  4.51 us
    ppermute x1, starting transfers between devices, per_device(): other = lax.ppermute(own, 'row_2', SWAP)  2.26 us
  transfers between devices with their start and end apart: 4, of which 3 were waited for; matrix products, arithmetic and copies ran while one was open for 0% of the time, Pallas kernels for 1%

profile of v8, /device:TPU:1, one launch (start us, length us, event | category | flops | bytes accessed | tf_op | source)
XLA Modules:
  0.0 86.1 jit_solution(17995518848216587692)
XLA Ops:
  0.0 0.0 copy-start.2
  0.0 1.3 %shard_map.100 = (bf16[2,32,512]{2,1,0:T(8,128)(2,1)S(1)}, bf16[2,32,512]{2,1,0:T(8,128)(2,1)S(1)}, bf16[128,512]{1,0:T(8,128)(2,1)S(1)}, bf16[128,512]{1,0:T(8,...) custom-call(bf16[128,512]{1,0:T(8,128)(2,1)} %bitcast.15, ...), custom_call_target="tpu_custom_call" | custom-call | flops 1048576 | bytes 1048576 | tf_op jit(solution)/shard_map/pallas_call | solution.py:267
  1.3 4.5 %collective-permute-start.1 = (bf16[2,32,512]{2,1,0:T(8,128)(2,1)S(1)}, bf16[2,32,512]{2,1,0:T(8,128)(2,1)S(1)}, u32[]{:S(2)}, u32[]{:S(2)}) collective-permute-start(bf16[2,32,512]{2,1,0:T(8,128)(2,1)S(1)} %get-tuple-element.21), channel_id=1, source_target_pairs={{1,2},{2,1},{3,4},{4,3},{5,6},{6,5},{7,8},{8,7},{9,10},{10,9},{11,... | collective-permute-start | bytes 196616 | tf_op jit(solution)/shard_map/ppermute | solution.py:274
  5.9 4.9 %collective-permute-start = (bf16[2,32,512]{2,1,0:T(8,128)(2,1)S(1)}, bf16[2,32,512]{2,1,0:T(8,128)(2,1)S(1)}, u32[]{:S(2)}, u32[]{:S(2)}) collective-permute-start(bf16[2,32,512]{2,1,0:T(8,128)(2,1)S(1)} %get-tuple-element.20.refs_1_), channel_id=1, source_target_pairs={{0,1},{1,0},{2,3},{3,2},{4,5},{5,4},{6,7},{7,6},{8,9},{9,8},{10,11... | collective-permute-start | bytes 196616 | tf_op jit(solution)/shard_map/ppermute | solution.py:275
  11.5 0.0 copy-start.1
  11.5 0.1 shard_map.101.refs_7_
  11.6 0.0 copy-start
  11.6 0.0 collective-permute-done.1.refs_6_
  11.6 0.1 collective-permute-done.refs_5_
  11.7 0.7 shard_map.102.refs_0_
  12.4 2.3 %collective-permute-start.2 = (bf16[2,128,512]{2,1,0:T(8,128)(2,1)S(1)}, bf16[2,128,512]{2,1,0:T(8,128)(2,1)S(1)}, u32[]{:S(2)}, u32[]{:S(2)}) collective-permute-start(bf16[2,128,512]{2,1,0:T(8,128)(2,1)S(1)} %shard_map.102.refs_0_), channel_id=1, source_target_pairs={{0,1},{1,0},{2,3},{3,2},{4,5},{5,4},{6,7},{7,6},{8,9},{9,8},{10,11... | collective-permute-start | bytes 786440 | tf_op jit(solution)/shard_map/ppermute | solution.py:282
  14.6 0.0 copy-done.2
  14.6 0.0 copy-done.1
  14.7 0.0 copy-done
  14.7 0.5 shard_map.103
  15.2 0.6 collective-permute-done.2.refs_3_
  15.8 0.8 shard_map.104
  16.6 15.0 %all_to_all.25.refs_1_ = bf16[8,96,512]{2,1,0:T(8,128)(2,1)S(1)} all-to-all(bf16[8,96,512]{2,1,0:T(8,128)(2,1)S(1)} %shard_map.104), channel_id=1, replica_groups={{12,2,4,6,8,10,0,14},{13,3,5,7,9,11,1,15},{28,18,20,22,24,26,16,30},{29..., dimensions={0} | all-to-all | bytes 1572864 | tf_op jit(solution)/shard_map/all_to_all | solution.py:35
  31.6 0.1 shard_map.105
  31.7 7.4 %all_to_all.26.x_ref = bf16[4,8,1664]{2,1,0:T(8,128)(2,1)S(1)} all-to-all(bf16[4,8,1664]{2,1,0:T(8,128)(2,1)S(1)} %shard_map.105), channel_id=1, replica_groups={{32,16,0,48},{33,17,1,49},{34,18,2,50},{35,19,3,51},{36,20,4,52},{37,21..., dimensions={0} | all-to-all | bytes 212992 | tf_op jit(solution)/shard_map/all_to_all | solution.py:35
  39.2 17.1 %all_to_all.27.x_ref = bf16[4,8,1664]{2,1,0:T(8,128)(2,1)S(1)} all-to-all(bf16[4,8,1664]{2,1,0:T(8,128)(2,1)S(1)} %shard_map.106), channel_id=1, replica_groups={{128,64,0,192},{129,65,1,193},{130,66,2,194},{131,67,3,195},{132,68,4,1..., dimensions={0} | all-to-all | bytes 212992 | tf_op jit(solution)/shard_map/all_to_all | solution.py:35
  56.3 0.2 shard_map.107
  56.5 6.9 %all_to_all.28.refs_0_ = bf16[4,8,1536]{2,1,0:T(8,128)(2,1)S(1)} all-to-all(bf16[4,8,1536]{2,1,0:T(8,128)(2,1)S(1)} %shard_map.107), channel_id=1, replica_groups={{32,16,0,48},{33,17,1,49},{34,18,2,50},{35,19,3,51},{36,20,4,52},{37,21..., dimensions={0} | all-to-all | bytes 196608 | tf_op jit(solution)/shard_map/all_to_all | solution.py:35
  63.5 0.1 shard_map.108
  63.5 10.6 %all_to_all.29.refs_1_.refs_2_ = bf16[8,96,512]{2,1,0:T(8,128)(2,1)S(1)} all-to-all(bf16[8,96,512]{2,1,0:T(8,128)(2,1)S(1)} %shard_map.108), channel_id=1, replica_groups={{12,2,4,6,8,10,0,14},{13,3,5,7,9,11,1,15},{28,18,20,22,24,26,16,30},{29..., dimensions={0} | all-to-all | bytes 1572864 | tf_op jit(solution)/shard_map/all_to_all | solution.py:35
  74.1 8.9 %collective-permute-start.3 = (bf16[8,96,512]{2,1,0:T(8,128)(2,1)S(1)}, bf16[8,96,512]{2,1,0:T(8,128)(2,1)S(1)}, u32[]{:S(2)}, u32[]{:S(2)}) collective-permute-start(bf16[8,96,512]{2,1,0:T(8,128)(2,1)S(1)} %all_to_all.29.refs_1_.refs_2_), channel_id=1, source_target_pairs={{0,1},{1,0},{2,3},{3,2},{4,5},{5,4},{6,7},{7,6},{8,9},{9,8},{10,11... | collective-permute-start | bytes 2359304 | tf_op jit(solution)/shard_map/ppermute | solution.py:299
  83.0 0.2 shard_map.109.refs_1_
  83.3 1.7 %collective-permute-done.3.refs_3_ = bf16[8,96,512]{2,1,0:T(8,128)(2,1)S(1)} collective-permute-done((bf16[8,96,512]{2,1,0:T(8,128)(2,1)S(1)}, bf16[8,96,512]{2,1,0:T(8,128)(2,1)S(1)}, u32[]{:S(2)}, u32[]{:S(2)}) %collective-permute-start.3) | collective-permute-done | bytes 786464 | tf_op jit(solution)/shard_map/ppermute | solution.py:299
  84.9 1.1 %shard_map.110 = bf16[128,512]{1,0:T(8,128)(2,1)} custom-call(bf16[2,128,512]{2,1,0:T(8,128)(2,1)S(1)} %shard_map.102.refs_0_, f32[2,128,512]{2,1,0:T(8,128)S(1)} %shard_map.109.refs_1_, bf16[8,96,512]{2,1,0:T(8,128)(2,1)S(1)} %all_to_all.29.refs_1_.refs_2_, bf16[8,96,512]{2,1,0:T(8,128)(2,1)S(1)} %collective-permute-done.3.refs_3_), custom_call_target="tpu_custom_call" | custom-call | flops 1048576 | bytes 1048576 | tf_op jit(solution)/shard_map/pallas_call | solution.py:302
  (1 shorter events, 0.0 us)
Async XLA Ops:
  0.0 14.6 %copy-start.2 = (bf16[1,512,512]{2,1,0:T(8,128)(2,1)S(1)}, bf16[1,512,512]{2,1,0:T(8,128)(2,1)}, u32[]{:S(2)}) copy-start(bf16[1,512,512]{2,1,0:T(8,128)(2,1)} %param.19) | copy-start | bytes 1572868
  1.3 10.3 %collective-permute-start.1 = (bf16[2,32,512]{2,1,0:T(8,128)(2,1)S(1)}, bf16[2,32,512]{2,1,0:T(8,128)(2,1)S(1)}, u32[]{:S(2)}, u32[]{:S(2)}) collective-permute-start(bf16[2,32,512]{2,1,0:T(8,128)(2,1)S(1)} %get-tuple-element.21), channel_id=1, source_target_pairs={{1,2},{2,1},{3,4},{4,3},{5,6},{6,5},{7,8},{8,7},{9,10},{10,9},{11,... | collective-permute-start | bytes 196616 | tf_op jit(solution)/shard_map/ppermute | solution.py:274
  5.9 5.8 %collective-permute-start = (bf16[2,32,512]{2,1,0:T(8,128)(2,1)S(1)}, bf16[2,32,512]{2,1,0:T(8,128)(2,1)S(1)}, u32[]{:S(2)}, u32[]{:S(2)}) collective-permute-start(bf16[2,32,512]{2,1,0:T(8,128)(2,1)S(1)} %get-tuple-element.20.refs_1_), channel_id=1, source_target_pairs={{0,1},{1,0},{2,3},{3,2},{4,5},{5,4},{6,7},{7,6},{8,9},{9,8},{10,11... | collective-permute-start | bytes 196616 | tf_op jit(solution)/shard_map/ppermute | solution.py:275
  11.5 3.2 %copy-start.1 = (bf16[1,512,512]{2,1,0:T(8,128)(2,1)S(1)}, bf16[1,512,512]{2,1,0:T(8,128)(2,1)}, u32[]{:S(2)}) copy-start(bf16[1,512,512]{2,1,0:T(8,128)(2,1)} %param.18) | copy-start | bytes 1572868
  11.6 3.1 %copy-start = (bf16[1,512,512]{2,1,0:T(8,128)(2,1)S(1)}, bf16[1,512,512]{2,1,0:T(8,128)(2,1)}, u32[]{:S(2)}) copy-start(bf16[1,512,512]{2,1,0:T(8,128)(2,1)} %param.17) | copy-start | bytes 1572868
  12.4 3.4 %collective-permute-start.2 = (bf16[2,128,512]{2,1,0:T(8,128)(2,1)S(1)}, bf16[2,128,512]{2,1,0:T(8,128)(2,1)S(1)}, u32[]{:S(2)}, u32[]{:S(2)}) collective-permute-start(bf16[2,128,512]{2,1,0:T(8,128)(2,1)S(1)} %shard_map.102.refs_0_), channel_id=1, source_target_pairs={{0,1},{1,0},{2,3},{3,2},{4,5},{5,4},{6,7},{7,6},{8,9},{9,8},{10,11... | collective-permute-start | bytes 786440 | tf_op jit(solution)/shard_map/ppermute | solution.py:282
  74.1 10.8 %collective-permute-start.3 = (bf16[8,96,512]{2,1,0:T(8,128)(2,1)S(1)}, bf16[8,96,512]{2,1,0:T(8,128)(2,1)S(1)}, u32[]{:S(2)}, u32[]{:S(2)}) collective-permute-start(bf16[8,96,512]{2,1,0:T(8,128)(2,1)S(1)} %all_to_all.29.refs_1_.refs_2_), channel_id=1, source_target_pairs={{0,1},{1,0},{2,3},{3,2},{4,5},{5,4},{6,7},{7,6},{8,9},{9,8},{10,11... | collective-permute-start | bytes 2359304 | tf_op jit(solution)/shard_map/ppermute | solution.py:299

commit v9 on v8

--- a/solution.py
+++ b/solution.py
@@ -26,9 +26,7 @@
 
 
 def led(axes, leader):
-    order = list(range(lax.axis_size(axes)))
-    order[0], order[leader] = leader, 0
-    return order
+    return [leader ^ i for i in range(lax.axis_size(axes))]
 
 
 def exchange(x, axes, order):
@@ -60,18 +58,15 @@
     return copies
 
 
-def edges_kernel(
-    cols, q_in, k_in, v_in, t_in, rate_in, reach_in, core_ref, chip_ref, q_ref, k_ref, v_ref, t_ref, rate_ref, reach_ref, sems, reach_smem
-):
+def edges_kernel(cols, k_in, v_in, rate_in, reach_in, core_ref, chip_ref, rate_ref, reach_ref, sems, reach_smem):
     core = lax.axis_index("row_2")
     near = HALO * cols
     end = k_in.shape[0] - near
     to_core = pl.ds(pl.multiple_of((1 - core) * end, near), near)
     to_chip = pl.ds(pl.multiple_of(core * end, near), near)
-    pairs = [(reach_in, reach_smem)]
+    pairs = [(reach_in, reach_smem), (rate_in, rate_ref)]
     for i, ref in enumerate((k_in, v_in)):
         pairs += [(ref.at[to_core], core_ref.at[i]), (ref.at[to_chip], chip_ref.at[i])]
-    pairs += [(rate_in, rate_ref), (t_in, t_ref), (q_in, q_ref), (k_in, k_ref), (v_in, v_ref)]
     copies = start_all(pairs, sems)
     copies[0].wait()
     line = iota(reach_ref.shape, 1) // cols
@@ -83,12 +78,17 @@
         c.wait()
 
 
-def scale_kernel(tokens, count_ref, edge_ref, rate_ref, t_ref, out_ref):
+def load_kernel(count_ref, edge_ref, rate_ref, t_in, q_in, k_in, v_in, scaled_ref, q_ref, k_ref, v_ref, sems, t_ref):
+    copies = start_all([(t_in, t_ref), (q_in, q_ref), (k_in, k_ref), (v_in, v_ref)], sems)
+    tokens = t_ref.shape[0]
     diagonal = iota((tokens, tokens), 0) == iota((tokens, tokens), 1)
     q_tok = lax.axis_index(ROW) * tokens + iota((1, tokens), 1)
     valid = jnp.where(q_tok < count_ref[0], 1.0, 0.0)
     rates = jnp.sum(jnp.where(diagonal, rate_ref[...] * valid, 0.0), 1, keepdims=True)
-    out_ref[...] = (rates * t_ref[...].astype(F32)).astype(BF)
+    copies[0].wait()
+    scaled_ref[...] = (rates * t_ref[...].astype(F32)).astype(BF)
+    for c in copies[1:]:
+        c.wait()
 
 
 def attend_kernel(rows, cols, grid_rows, count_ref, reach_ref, q_ref, k_ref, v_ref, core_ref, chip_ref, scaled_ref, out_ref):
@@ -264,26 +264,27 @@
     block, edge = ((tokens, width), BF), ((2, near, width), BF)
     query, key, value, aim = (in_hbm(flat(x)) for x in (query_feats, key_feats, value_feats, target))
     row_of = lambda dtype: ((1, tokens), dtype)
-    to_core, to_chip, query, key, value, aim, rates, reach = call(
+    to_core, to_chip, rates, reach = call(
         lambda *refs: edges_kernel(cols, *refs),
-        [edge] * 2 + [block] * 4 + [row_of(F32), row_of(jnp.int32)],
-        [HBM] * 6,
-        [pltpu.SemaphoreType.DMA((10,)), pltpu.SMEM(row_reach.shape, jnp.int32)],
-    )(query, key, value, aim, in_hbm(token_rates[0]), in_hbm(row_reach))
+        [edge] * 2 + [row_of(F32), row_of(jnp.int32)],
+        [HBM] * 4,
+        [pltpu.SemaphoreType.DMA((6,)), pltpu.SMEM(row_reach.shape, jnp.int32)],
+    )(key, value, *(in_hbm(x) for x in (token_rates[0], row_reach)))
     next_chip = [p for i in range(1, n_row - 1, 2) for p in ((i, i + 1), (i + 1, i))]
     from_chip = lax.ppermute(to_chip, ROW, next_chip)
     from_core = lax.ppermute(to_core, "row_2", SWAP)
 
-    scaled = call(lambda *refs: scale_kernel(tokens, *refs), block, [SMEM] + [VMEM] * 3)(view_counts, to_core, rates, aim)
+    scaled, query, key, value = call(
+        load_kernel, [block] * 4, [SMEM] + [VMEM] * 2 + [HBM] * 4, [pltpu.SemaphoreType.DMA((4,)), pltpu.VMEM((tokens, width), BF)]
+    )(view_counts, to_core, rates, aim, query, key, value)
     attend = lambda *refs: attend_kernel(rows, cols, n_row * rows, *refs)
-    own = call(attend, ((2, tokens, width), BF), [SMEM] + [VMEM] * 7)(
-        view_counts, reach, query, key, value, from_core, from_chip, scaled
-    )
+    own = call(attend, ((2, tokens, width), BF), [SMEM] + [VMEM] * 7)(view_counts, reach, query, key, value, from_core, from_chip, scaled)
     other = lax.ppermute(own, "row_2", SWAP)
     ws = w_first[0], w_third[0], w_second[0]
     ahead = lambda *refs: forward_kernel(n_plane, n_near, *refs)
     back, gated, old = call(ahead, [((2, tokens, width), BF), ((tokens, width // 2), BF), ((few, 3 * width), F32)], [VMEM] * 4)(own, *ws)
-    planes, nears = led(PLANE, n_plane - 2), led("near", n_near - 2)
+    planes, nears = led(PLANE, n_plane - 1), led("near", n_near - 2)
+    planes_late, nears_late = led(PLANE, n_plane - 2), led("near", n_near - 1)
     grads = lambda *refs: grads_kernel(planes, *refs)
     part = call(grads, ((n_plane, 3 * share, width), BF), [VMEM] * 7)(own, back, gated, other, *ws)
     part = exchange(part, PLANE, planes)
@@ -293,13 +294,13 @@
     part = call(gather_kernel, ((n_far, few, 3 * width + 128), BF), [VMEM])(part)
     part = exchange(part, "far", led("far", n_far // 2))
     new = call(renew_kernel, ((n_near, few, 3 * width), BF), [VMEM] * 2)(part, old)
-    new = exchange(new, "near", nears)
-    lines = call(lambda *refs: order_kernel(nears, *refs), ((n_plane, 3 * share, width), BF), [VMEM])(new)
-    mine = exchange(lines, PLANE, planes)
+    new = exchange(new, "near", nears_late)
+    lines = call(lambda *refs: order_kernel(nears_late, *refs), ((n_plane, 3 * share, width), BF), [VMEM])(new)
+    mine = exchange(lines, PLANE, planes_late)
     theirs = lax.ppermute(mine, "row_2", SWAP)
-    part = call(lambda *refs: half_kernel(planes, *refs), ((2, tokens, width), F32), [VMEM] * 2)(own, mine)
+    part = call(lambda *refs: half_kernel(planes_late, *refs), ((2, tokens, width), F32), [VMEM] * 2)(own, mine)
     scratch = [pltpu.VMEM((tokens, width), BF), pltpu.SemaphoreType.DMA((2,))]
-    out = call(lambda *refs: apply_kernel(planes, *refs), block, [VMEM] * 4, scratch, HBM)(own, part, mine, theirs)
+    out = call(lambda *refs: apply_kernel(planes_late, *refs), block, [VMEM] * 4, scratch, HBM)(own, part, mine, theirs)
     return out.reshape(1, rows, cols, width)
 
 

time: 86.4 us -> 85.7 us (level)
  blocking collectives: 57.1 us -> 55.8 us
    all_to_all x5, blocking collectives: 57.1 us -> 55.8 us  [exchange(): return lax.all_to_all(x, axes, 0, 0, tiled=True, axis_index_groups=[order])]
  transfers between devices with their start and end apart: 4 -> 4, of which waited for: 3 -> 2; matrix products, arithmetic and copies ran while one was open for 0% -> 0% of each run, Pallas kernels for 1% -> 2%
where the time goes in v9:
time: 85.7 us; the launch traced here: 85.3 us
  blocking collectives  55.8 us (65%)
  starting transfers between devices  20.1 us (23%)
  Pallas kernels  5.9 us (7%)
  waiting for transfers between devices  2.62 us (3%)
    all_to_all x5, blocking collectives, exchange(): return lax.all_to_all(x, axes, 0, 0, tiled=True, axis_index_groups=[order])  55.8 us
    ppermute x1, starting transfers between devices, per_device(): theirs = lax.ppermute(mine, 'row_2', SWAP)  8.76 us
    ppermute x1, starting transfers between devices, per_device(): from_core = lax.ppermute(to_core, 'row_2', SWAP)  4.94 us
    ppermute x1, starting transfers between devices, per_device(): from_chip = lax.ppermute(to_chip, ROW, next_chip)  4.51 us
    ppermute x1, starting transfers between devices, per_device(): other = lax.ppermute(own, 'row_2', SWAP)  1.92 us
  transfers between devices with their start and end apart: 4, of which 2 were waited for; matrix products, arithmetic and copies ran while one was open for 0% of the time, Pallas kernels for 2%

profile of v9, /device:TPU:1, one launch (start us, length us, event | category | flops | bytes accessed | tf_op | source)
XLA Modules:
  0.0 85.3 jit_solution(5036724409483872918)
XLA Ops:
  0.0 0.0 copy-start.2
  0.0 0.9 %shard_map.100 = (bf16[2,32,512]{2,1,0:T(8,128)(2,1)S(1)}, bf16[2,32,512]{2,1,0:T(8,128)(2,1)S(1)}, f32[1,128]{1,0:T(1,128)S(1)}, s32[1,128]{1,0:T(1,128)S(1)}) custom-call(bf16[128,512]{1,0:T(8,128)(2,1)} %bitcast.15, bf16[128,512]{1,0:T(8,128)(2,1)} %bitcast.17, f32[1,128]{1,0:T(1,128)} %bitcast.21, s32[8]{0:T(128)} %refs_3_.1), custom_call_target="tpu_custom_call" | custom-call | flops 1048576 | bytes 1048576 | tf_op jit(solution)/shard_map/pallas_call | solution.py:267
  0.9 4.5 %collective-permute-start.1 = (bf16[2,32,512]{2,1,0:T(8,128)(2,1)S(1)}, bf16[2,32,512]{2,1,0:T(8,128)(2,1)S(1)}, u32[]{:S(2)}, u32[]{:S(2)}) collective-permute-start(bf16[2,32,512]{2,1,0:T(8,128)(2,1)S(1)} %get-tuple-element.22), channel_id=1, source_target_pairs={{1,2},{2,1},{3,4},{4,3},{5,6},{6,5},{7,8},{8,7},{9,10},{10,9},{11,... | collective-permute-start | bytes 196616 | tf_op jit(solution)/shard_map/ppermute | solution.py:274
  5.5 4.9 %collective-permute-start = (bf16[2,32,512]{2,1,0:T(8,128)(2,1)S(1)}, bf16[2,32,512]{2,1,0:T(8,128)(2,1)S(1)}, u32[]{:S(2)}, u32[]{:S(2)}) collective-permute-start(bf16[2,32,512]{2,1,0:T(8,128)(2,1)S(1)} %get-tuple-element.17.edge_ref), channel_id=1, source_target_pairs={{0,1},{1,0},{2,3},{3,2},{4,5},{5,4},{6,7},{7,6},{8,9},{9,8},{10,11... | collective-permute-start | bytes 196616 | tf_op jit(solution)/shard_map/ppermute | solution.py:275
  11.1 0.0 copy-start.1
  11.1 1.2 %shard_map.101 = (bf16[128,512]{1,0:T(8,128)(2,1)S(1)}, bf16[128,512]{1,0:T(8,128)(2,1)S(1)}, bf16[128,512]{1,0:T(8,128)(2,1)S(1)}, bf16[128,512]{1,0:T(8,128)(2,1)S(1)}) custom-call(s32[1]{0:T(128)S(6)} %copy.11.count_ref.refs_0_, bf16[2,32,512]{2,1,0:T(8,128)(2,1)S(1)} %get-tuple-element.17.edge_ref, f32[1,128]{1,0:T(1,128)S(1)} %get-tuple-element.18.rate_ref, ...), custom_call_target="tpu_custom_call" | custom-call | flops 1048576 | bytes 1048576 | tf_op jit(solution)/shard_map/pallas_call | solution.py:277
  12.3 0.0 copy-start
  12.3 0.0 collective-permute-done.1.refs_6_
  12.3 0.0 collective-permute-done.refs_5_
  12.3 0.7 shard_map.102.refs_0_
  13.0 1.9 %collective-permute-start.2 = (bf16[2,128,512]{2,1,0:T(8,128)(2,1)S(1)}, bf16[2,128,512]{2,1,0:T(8,128)(2,1)S(1)}, u32[]{:S(2)}, u32[]{:S(2)}) collective-permute-start(bf16[2,128,512]{2,1,0:T(8,128)(2,1)S(1)} %shard_map.102.refs_0_), channel_id=1, source_target_pairs={{0,1},{1,0},{2,3},{3,2},{4,5},{5,4},{6,7},{7,6},{8,9},{9,8},{10,11... | collective-permute-start | bytes 786440 | tf_op jit(solution)/shard_map/ppermute | solution.py:282
  14.9 0.0 copy-done.2
  14.9 0.0 copy-done.1
  14.9 0.0 copy-done
  14.9 0.5 shard_map.103
  15.4 1.0 %collective-permute-done.2.refs_3_ = bf16[2,128,512]{2,1,0:T(8,128)(2,1)S(1)} collective-permute-done((bf16[2,128,512]{2,1,0:T(8,128)(2,1)S(1)}, bf16[2,128,512]{2,1,0:T(8,128)(2,1)S(1)}, u32[]{:S(2)}, u32[]{:S(2)}) %collective-permute-start.2) | collective-permute-done | bytes 262176 | tf_op jit(solution)/shard_map/ppermute | solution.py:282
  16.4 0.9 %shard_map.104 = bf16[8,96,512]{2,1,0:T(8,128)(2,1)S(1)} custom-call(bf16[2,128,512]{2,1,0:T(8,128)(2,1)S(1)} %shard_map.102.refs_0_, bf16[2,128,512]{2,1,0:T(8,128)(2,1)S(1)} %get-tuple-element.24.refs_1_, bf16[128,256]{1,0:T(8,128)(2,1)S(1)} %get-tuple-element.25.refs_2_, bf16[2,128,512]{2,1,0:T(8,128)(2,1)S(1)} %collective-permute-done.2.refs_3_, ...), custom_call_target="tpu_custom_call" | custom-call | flops 1048576 | bytes 1048576 | tf_op jit(solution)/shard_map/pallas_call | solution.py:289
  17.3 14.5 %all_to_all.25.refs_1_ = bf16[8,96,512]{2,1,0:T(8,128)(2,1)S(1)} all-to-all(bf16[8,96,512]{2,1,0:T(8,128)(2,1)S(1)} %shard_map.104), channel_id=1, replica_groups={{14,12,10,8,6,4,2,0},{15,13,11,9,7,5,3,1},{30,28,26,24,22,20,18,16},{31..., dimensions={0} | all-to-all | bytes 1572864 | tf_op jit(solution)/shard_map/all_to_all | solution.py:33
  31.8 0.1 shard_map.105
  31.9 6.2 %all_to_all.26.x_ref = bf16[4,8,1664]{2,1,0:T(8,128)(2,1)S(1)} all-to-all(bf16[4,8,1664]{2,1,0:T(8,128)(2,1)S(1)} %shard_map.105), channel_id=1, replica_groups={{32,48,0,16},{33,49,1,17},{34,50,2,18},{35,51,3,19},{36,52,4,20},{37,53..., dimensions={0} | all-to-all | bytes 212992 | tf_op jit(solution)/shard_map/all_to_all | solution.py:33
  38.1 17.2 %all_to_all.27.x_ref = bf16[4,8,1664]{2,1,0:T(8,128)(2,1)S(1)} all-to-all(bf16[4,8,1664]{2,1,0:T(8,128)(2,1)S(1)} %shard_map.106), channel_id=1, replica_groups={{128,192,0,64},{129,193,1,65},{130,194,2,66},{131,195,3,67},{132,196,4,..., dimensions={0} | all-to-all | bytes 212992 | tf_op jit(solution)/shard_map/all_to_all | solution.py:33
  55.3 0.2 shard_map.107
  55.5 7.1 %all_to_all.28.refs_0_ = bf16[4,8,1536]{2,1,0:T(8,128)(2,1)S(1)} all-to-all(bf16[4,8,1536]{2,1,0:T(8,128)(2,1)S(1)} %shard_map.107), channel_id=1, replica_groups={{48,32,16,0},{49,33,17,1},{50,34,18,2},{51,35,19,3},{52,36,20,4},{53,37..., dimensions={0} | all-to-all | bytes 196608 | tf_op jit(solution)/shard_map/all_to_all | solution.py:33
  62.6 0.1 shard_map.108
  62.7 10.8 %all_to_all.29.refs_1_.refs_2_ = bf16[8,96,512]{2,1,0:T(8,128)(2,1)S(1)} all-to-all(bf16[8,96,512]{2,1,0:T(8,128)(2,1)S(1)} %shard_map.108), channel_id=1, replica_groups={{12,14,8,10,4,6,0,2},{13,15,9,11,5,7,1,3},{28,30,24,26,20,22,16,18},{29..., dimensions={0} | all-to-all | bytes 1572864 | tf_op jit(solution)/shard_map/all_to_all | solution.py:33
  73.5 8.8 %collective-permute-start.3 = (bf16[8,96,512]{2,1,0:T(8,128)(2,1)S(1)}, bf16[8,96,512]{2,1,0:T(8,128)(2,1)S(1)}, u32[]{:S(2)}, u32[]{:S(2)}) collective-permute-start(bf16[8,96,512]{2,1,0:T(8,128)(2,1)S(1)} %all_to_all.29.refs_1_.refs_2_), channel_id=1, source_target_pairs={{0,1},{1,0},{2,3},{3,2},{4,5},{5,4},{6,7},{7,6},{8,9},{9,8},{10,11... | collective-permute-start | bytes 2359304 | tf_op jit(solution)/shard_map/ppermute | solution.py:300
  82.3 0.2 shard_map.109.refs_1_
  82.5 1.7 %collective-permute-done.3.refs_3_ = bf16[8,96,512]{2,1,0:T(8,128)(2,1)S(1)} collective-permute-done((bf16[8,96,512]{2,1,0:T(8,128)(2,1)S(1)}, bf16[8,96,512]{2,1,0:T(8,128)(2,1)S(1)}, u32[]{:S(2)}, u32[]{:S(2)}) %collective-permute-start.3) | collective-permute-done | bytes 786464 | tf_op jit(solution)/shard_map/ppermute | solution.py:300
  84.2 1.1 %shard_map.110 = bf16[128,512]{1,0:T(8,128)(2,1)} custom-call(bf16[2,128,512]{2,1,0:T(8,128)(2,1)S(1)} %shard_map.102.refs_0_, f32[2,128,512]{2,1,0:T(8,128)S(1)} %shard_map.109.refs_1_, bf16[8,96,512]{2,1,0:T(8,128)(2,1)S(1)} %all_to_all.29.refs_1_.refs_2_, bf16[8,96,512]{2,1,0:T(8,128)(2,1)S(1)} %collective-permute-done.3.refs_3_), custom_call_target="tpu_custom_call" | custom-call | flops 1048576 | bytes 1048576 | tf_op jit(solution)/shard_map/pallas_call | solution.py:303
  (1 shorter events, 0.0 us)
Async XLA Ops:
  0.0 14.9 %copy-start.2 = (bf16[1,512,512]{2,1,0:T(8,128)(2,1)S(1)}, bf16[1,512,512]{2,1,0:T(8,128)(2,1)}, u32[]{:S(2)}) copy-start(bf16[1,512,512]{2,1,0:T(8,128)(2,1)} %param.19) | copy-start | bytes 1572868
  0.9 11.3 %collective-permute-start.1 = (bf16[2,32,512]{2,1,0:T(8,128)(2,1)S(1)}, bf16[2,32,512]{2,1,0:T(8,128)(2,1)S(1)}, u32[]{:S(2)}, u32[]{:S(2)}) collective-permute-start(bf16[2,32,512]{2,1,0:T(8,128)(2,1)S(1)} %get-tuple-element.22), channel_id=1, source_target_pairs={{1,2},{2,1},{3,4},{4,3},{5,6},{6,5},{7,8},{8,7},{9,10},{10,9},{11,... | collective-permute-start | bytes 196616 | tf_op jit(solution)/shard_map/ppermute | solution.py:274
  5.5 6.8 %collective-permute-start = (bf16[2,32,512]{2,1,0:T(8,128)(2,1)S(1)}, bf16[2,32,512]{2,1,0:T(8,128)(2,1)S(1)}, u32[]{:S(2)}, u32[]{:S(2)}) collective-permute-start(bf16[2,32,512]{2,1,0:T(8,128)(2,1)S(1)} %get-tuple-element.17.edge_ref), channel_id=1, source_target_pairs={{0,1},{1,0},{2,3},{3,2},{4,5},{5,4},{6,7},{7,6},{8,9},{9,8},{10,11... | collective-permute-start | bytes 196616 | tf_op jit(solution)/shard_map/ppermute | solution.py:275
  11.1 3.9 %copy-start.1 = (bf16[1,512,512]{2,1,0:T(8,128)(2,1)S(1)}, bf16[1,512,512]{2,1,0:T(8,128)(2,1)}, u32[]{:S(2)}) copy-start(bf16[1,512,512]{2,1,0:T(8,128)(2,1)} %param.18) | copy-start | bytes 1572868
  12.3 2.7 %copy-start = (bf16[1,512,512]{2,1,0:T(8,128)(2,1)S(1)}, bf16[1,512,512]{2,1,0:T(8,128)(2,1)}, u32[]{:S(2)}) copy-start(bf16[1,512,512]{2,1,0:T(8,128)(2,1)} %param.17) | copy-start | bytes 1572868
  13.0 3.4 %collective-permute-start.2 = (bf16[2,128,512]{2,1,0:T(8,128)(2,1)S(1)}, bf16[2,128,512]{2,1,0:T(8,128)(2,1)S(1)}, u32[]{:S(2)}, u32[]{:S(2)}) collective-permute-start(bf16[2,128,512]{2,1,0:T(8,128)(2,1)S(1)} %shard_map.102.refs_0_), channel_id=1, source_target_pairs={{0,1},{1,0},{2,3},{3,2},{4,5},{5,4},{6,7},{7,6},{8,9},{9,8},{10,11... | collective-permute-start | bytes 786440 | tf_op jit(solution)/shard_map/ppermute | solution.py:282
  73.5 10.7 %collective-permute-start.3 = (bf16[8,96,512]{2,1,0:T(8,128)(2,1)S(1)}, bf16[8,96,512]{2,1,0:T(8,128)(2,1)S(1)}, u32[]{:S(2)}, u32[]{:S(2)}) collective-permute-start(bf16[8,96,512]{2,1,0:T(8,128)(2,1)S(1)} %all_to_all.29.refs_1_.refs_2_), channel_id=1, source_target_pairs={{0,1},{1,0},{2,3},{3,2},{4,5},{5,4},{6,7},{7,6},{8,9},{9,8},{10,11... | collective-permute-start | bytes 2359304 | tf_op jit(solution)/shard_map/ppermute | solution.py:300

commit v10 on v9

--- a/solution.py
+++ b/solution.py
@@ -17,7 +17,6 @@
 BF = jnp.bfloat16
 F32 = jnp.float32
 VMEM = pl.BlockSpec(memory_space=pltpu.VMEM)
-SMEM = pl.BlockSpec(memory_space=pltpu.SMEM)
 HBM = pl.BlockSpec(memory_space=pltpu.HBM)
 
 
@@ -83,7 +82,7 @@
     tokens = t_ref.shape[0]
     diagonal = iota((tokens, tokens), 0) == iota((tokens, tokens), 1)
     q_tok = lax.axis_index(ROW) * tokens + iota((1, tokens), 1)
-    valid = jnp.where(q_tok < count_ref[0], 1.0, 0.0)
+    valid = jnp.where(q_tok < count_ref[...], 1.0, 0.0)
     rates = jnp.sum(jnp.where(diagonal, rate_ref[...] * valid, 0.0), 1, keepdims=True)
     copies[0].wait()
     scaled_ref[...] = (rates * t_ref[...].astype(F32)).astype(BF)
@@ -107,7 +106,7 @@
     q_at = iota((1, tokens), 1)
     q_row = base + q_at // cols
     q_tok = base * cols + q_at
-    valid = (k_tok < count_ref[0]) & (k_row >= 0) & (k_row < grid_rows)
+    valid = (k_tok < count_ref[...]) & (k_row >= 0) & (k_row < grid_rows)
     k_row = jnp.where(valid, k_row, -(1 << 20))
     allowed = (jnp.abs(k_row - q_row) <= reach_ref[...]) | (k_tok == q_tok)
     heads = [slice(at, at + ATT_HD) for at in range(0, q_ref.shape[1], ATT_HD)]
@@ -185,8 +184,8 @@
         for n, u in enumerate(order):
             at = k * share + u * few
             out_ref[n, :, k * HD : (k + 1) * HD] = total[at : at + few].astype(BF)
-    count = count_ref[0]
     lane = iota((few, 128), 1)
+    count = jnp.broadcast_to(count_ref[...], lane.shape)
     digits = jnp.where(lane == 0, count % 16, jnp.where(lane == 1, (count // 16) % 16, count // 256))
     digits = digits.astype(F32).astype(BF)
     for n in range(len(order)):
@@ -263,6 +262,7 @@
 
     block, edge = ((tokens, width), BF), ((2, near, width), BF)
     query, key, value, aim = (in_hbm(flat(x)) for x in (query_feats, key_feats, value_feats, target))
+    count = view_counts.reshape(1, 1)
     row_of = lambda dtype: ((1, tokens), dtype)
     to_core, to_chip, rates, reach = call(
         lambda *refs: edges_kernel(cols, *refs),
@@ -275,10 +275,10 @@
     from_core = lax.ppermute(to_core, "row_2", SWAP)
 
     scaled, query, key, value = call(
-        load_kernel, [block] * 4, [SMEM] + [VMEM] * 2 + [HBM] * 4, [pltpu.SemaphoreType.DMA((4,)), pltpu.VMEM((tokens, width), BF)]
-    )(view_counts, to_core, rates, aim, query, key, value)
+        load_kernel, [block] * 4, [VMEM] * 3 + [HBM] * 4, [pltpu.SemaphoreType.DMA((4,)), pltpu.VMEM((tokens, width), BF)]
+    )(count, to_core, rates, aim, query, key, value)
     attend = lambda *refs: attend_kernel(rows, cols, n_row * rows, *refs)
-    own = call(attend, ((2, tokens, width), BF), [SMEM] + [VMEM] * 7)(view_counts, reach, query, key, value, from_core, from_chip, scaled)
+    own = call(attend, ((2, tokens, width), BF), [VMEM] * 8)(count, reach, query, key, value, from_core, from_chip, scaled)
     other = lax.ppermute(own, "row_2", SWAP)
     ws = w_first[0], w_third[0], w_second[0]
     ahead = lambda *refs: forward_kernel(n_plane, n_near, *refs)
@@ -289,7 +289,7 @@
     part = call(grads, ((n_plane, 3 * share, width), BF), [VMEM] * 7)(own, back, gated, other, *ws)
     part = exchange(part, PLANE, planes)
     spread = lambda *refs: spread_kernel(nears, few, *refs)
-    part = call(spread, ((n_near, few, 3 * width + 128), BF), [SMEM, VMEM])(view_counts, part)
+    part = call(spread, ((n_near, few, 3 * width + 128), BF), [VMEM] * 2)(count, part)
     part = exchange(part, "near", nears)
     part = call(gather_kernel, ((n_far, few, 3 * width + 128), BF), [VMEM])(part)
     part = exchange(part, "far", led("far", n_far // 2))

time: 85.7 us -> 85.7 us (level)
  no operation moved by 1% of the time
where the time goes in v10:
time: 85.7 us; the launch traced here: 85.3 us
  blocking collectives  55.8 us (65%)
  starting transfers between devices  20.1 us (23%)
  Pallas kernels  5.93 us (7%)
  waiting for transfers between devices  2.61 us (3%)
    all_to_all x5, blocking collectives, exchange(): return lax.all_to_all(x, axes, 0, 0, tiled=True, axis_index_groups=[order])  55.8 us
    ppermute x1, starting transfers between devices, per_device(): theirs = lax.ppermute(mine, 'row_2', SWAP)  8.77 us
    ppermute x1, starting transfers between devices, per_device(): from_core = lax.ppermute(to_core, 'row_2', SWAP)  4.94 us
    ppermute x1, starting transfers between devices, per_device(): from_chip = lax.ppermute(to_chip, ROW, next_chip)  4.51 us
    ppermute x1, starting transfers between devices, per_device(): other = lax.ppermute(own, 'row_2', SWAP)  1.92 us
  transfers between devices with their start and end apart: 4, of which 2 were waited for; matrix products, arithmetic and copies ran while one was open for 0% of the time, Pallas kernels for 2%

profile of v10, /device:TPU:1, one launch (start us, length us, event | category | flops | bytes accessed | tf_op | source)
XLA Modules:
  0.0 85.3 jit_solution(14612903717828319126)
XLA Ops:
  0.0 0.0 copy-start.2
  0.0 0.9 %shard_map.100 = (bf16[2,32,512]{2,1,0:T(8,128)(2,1)S(1)}, bf16[2,32,512]{2,1,0:T(8,128)(2,1)S(1)}, f32[1,128]{1,0:T(1,128)S(1)}, s32[1,128]{1,0:T(1,128)S(1)}) custom-call(bf16[128,512]{1,0:T(8,128)(2,1)} %bitcast.19, bf16[128,512]{1,0:T(8,128)(2,1)} %bitcast.21, f32[1,128]{1,0:T(1,128)} %bitcast.25, s32[8]{0:T(128)} %refs_3_.1), custom_call_target="tpu_custom_call" | custom-call | flops 1048576 | bytes 1048576 | tf_op jit(solution)/shard_map/pallas_call | solution.py:267
  0.9 4.5 %collective-permute-start.1 = (bf16[2,32,512]{2,1,0:T(8,128)(2,1)S(1)}, bf16[2,32,512]{2,1,0:T(8,128)(2,1)S(1)}, u32[]{:S(2)}, u32[]{:S(2)}) collective-permute-start(bf16[2,32,512]{2,1,0:T(8,128)(2,1)S(1)} %get-tuple-element.22), channel_id=1, source_target_pairs={{1,2},{2,1},{3,4},{4,3},{5,6},{6,5},{7,8},{8,7},{9,10},{10,9},{11,... | collective-permute-start | bytes 196616 | tf_op jit(solution)/shard_map/ppermute | solution.py:274
  5.5 4.9 %collective-permute-start = (bf16[2,32,512]{2,1,0:T(8,128)(2,1)S(1)}, bf16[2,32,512]{2,1,0:T(8,128)(2,1)S(1)}, u32[]{:S(2)}, u32[]{:S(2)}) collective-permute-start(bf16[2,32,512]{2,1,0:T(8,128)(2,1)S(1)} %get-tuple-element.17.edge_ref), channel_id=1, source_target_pairs={{0,1},{1,0},{2,3},{3,2},{4,5},{5,4},{6,7},{7,6},{8,9},{9,8},{10,11... | collective-permute-start | bytes 196616 | tf_op jit(solution)/shard_map/ppermute | solution.py:275
  11.1 0.0 copy-start.1
  11.1 1.2 %shard_map.101 = (bf16[128,512]{1,0:T(8,128)(2,1)S(1)}, bf16[128,512]{1,0:T(8,128)(2,1)S(1)}, bf16[128,512]{1,0:T(8,128)(2,1)S(1)}, bf16[128,512]{1,0:T(8,128)(2,1)S(1)}) custom-call(s32[1,1]{1,0:T(1,128)} %bitcast.10.count_ref, bf16[2,32,512]{2,1,0:T(8,128)(2,1)S(1)} %get-tuple-element.17.edge_ref, f32[1,128]{1,0:T(1,128)S(1)} %get-tuple-element.18.rate_ref, ...), custom_call_target="tpu_custom_call" | custom-call | flops 1048576 | bytes 1048576 | tf_op jit(solution)/shard_map/pallas_call | solution.py:277
  12.3 0.0 copy-start
  12.3 0.0 collective-permute-done.1.refs_6_
  12.3 0.0 collective-permute-done.refs_5_
  12.3 0.6 shard_map.102.refs_0_
  12.9 1.9 %collective-permute-start.2 = (bf16[2,128,512]{2,1,0:T(8,128)(2,1)S(1)}, bf16[2,128,512]{2,1,0:T(8,128)(2,1)S(1)}, u32[]{:S(2)}, u32[]{:S(2)}) collective-permute-start(bf16[2,128,512]{2,1,0:T(8,128)(2,1)S(1)} %shard_map.102.refs_0_), channel_id=1, source_target_pairs={{0,1},{1,0},{2,3},{3,2},{4,5},{5,4},{6,7},{7,6},{8,9},{9,8},{10,11... | collective-permute-start | bytes 786440 | tf_op jit(solution)/shard_map/ppermute | solution.py:282
  14.9 0.0 copy-done.2
  14.9 0.0 copy-done.1
  14.9 0.0 copy-done
  14.9 0.5 shard_map.103
  15.4 1.0 %collective-permute-done.2.refs_3_ = bf16[2,128,512]{2,1,0:T(8,128)(2,1)S(1)} collective-permute-done((bf16[2,128,512]{2,1,0:T(8,128)(2,1)S(1)}, bf16[2,128,512]{2,1,0:T(8,128)(2,1)S(1)}, u32[]{:S(2)}, u32[]{:S(2)}) %collective-permute-start.2) | collective-permute-done | bytes 262176 | tf_op jit(solution)/shard_map/ppermute | solution.py:282
  16.4 0.9 %shard_map.104 = bf16[8,96,512]{2,1,0:T(8,128)(2,1)S(1)} custom-call(bf16[2,128,512]{2,1,0:T(8,128)(2,1)S(1)} %shard_map.102.refs_0_, bf16[2,128,512]{2,1,0:T(8,128)(2,1)S(1)} %get-tuple-element.24.refs_1_, bf16[128,256]{1,0:T(8,128)(2,1)S(1)} %get-tuple-element.25.refs_2_, bf16[2,128,512]{2,1,0:T(8,128)(2,1)S(1)} %collective-permute-done.2.refs_3_, ...), custom_call_target="tpu_custom_call" | custom-call | flops 1048576 | bytes 1048576 | tf_op jit(solution)/shard_map/pallas_call | solution.py:289
  17.2 14.5 %all_to_all.25.refs_1_ = bf16[8,96,512]{2,1,0:T(8,128)(2,1)S(1)} all-to-all(bf16[8,96,512]{2,1,0:T(8,128)(2,1)S(1)} %shard_map.104), channel_id=1, replica_groups={{14,12,10,8,6,4,2,0},{15,13,11,9,7,5,3,1},{30,28,26,24,22,20,18,16},{31..., dimensions={0} | all-to-all | bytes 1572864 | tf_op jit(solution)/shard_map/all_to_all | solution.py:32
  31.8 0.2 shard_map.105
  31.9 6.2 %all_to_all.26.x_ref = bf16[4,8,1664]{2,1,0:T(8,128)(2,1)S(1)} all-to-all(bf16[4,8,1664]{2,1,0:T(8,128)(2,1)S(1)} %shard_map.105), channel_id=1, replica_groups={{32,48,0,16},{33,49,1,17},{34,50,2,18},{35,51,3,19},{36,52,4,20},{37,53..., dimensions={0} | all-to-all | bytes 212992 | tf_op jit(solution)/shard_map/all_to_all | solution.py:32
  38.1 17.2 %all_to_all.27.x_ref = bf16[4,8,1664]{2,1,0:T(8,128)(2,1)S(1)} all-to-all(bf16[4,8,1664]{2,1,0:T(8,128)(2,1)S(1)} %shard_map.106), channel_id=1, replica_groups={{128,192,0,64},{129,193,1,65},{130,194,2,66},{131,195,3,67},{132,196,4,..., dimensions={0} | all-to-all | bytes 212992 | tf_op jit(solution)/shard_map/all_to_all | solution.py:32
  55.3 0.2 shard_map.107
  55.5 7.1 %all_to_all.28.refs_0_ = bf16[4,8,1536]{2,1,0:T(8,128)(2,1)S(1)} all-to-all(bf16[4,8,1536]{2,1,0:T(8,128)(2,1)S(1)} %shard_map.107), channel_id=1, replica_groups={{48,32,16,0},{49,33,17,1},{50,34,18,2},{51,35,19,3},{52,36,20,4},{53,37..., dimensions={0} | all-to-all | bytes 196608 | tf_op jit(solution)/shard_map/all_to_all | solution.py:32
  62.7 0.1 shard_map.108
  62.7 10.8 %all_to_all.29.refs_1_.refs_2_ = bf16[8,96,512]{2,1,0:T(8,128)(2,1)S(1)} all-to-all(bf16[8,96,512]{2,1,0:T(8,128)(2,1)S(1)} %shard_map.108), channel_id=1, replica_groups={{12,14,8,10,4,6,0,2},{13,15,9,11,5,7,1,3},{28,30,24,26,20,22,16,18},{29..., dimensions={0} | all-to-all | bytes 1572864 | tf_op jit(solution)/shard_map/all_to_all | solution.py:32
  73.5 8.8 %collective-permute-start.3 = (bf16[8,96,512]{2,1,0:T(8,128)(2,1)S(1)}, bf16[8,96,512]{2,1,0:T(8,128)(2,1)S(1)}, u32[]{:S(2)}, u32[]{:S(2)}) collective-permute-start(bf16[8,96,512]{2,1,0:T(8,128)(2,1)S(1)} %all_to_all.29.refs_1_.refs_2_), channel_id=1, source_target_pairs={{0,1},{1,0},{2,3},{3,2},{4,5},{5,4},{6,7},{7,6},{8,9},{9,8},{10,11... | collective-permute-start | bytes 2359304 | tf_op jit(solution)/shard_map/ppermute | solution.py:300
  82.3 0.2 shard_map.109.refs_1_
  82.5 1.7 %collective-permute-done.3.refs_3_ = bf16[8,96,512]{2,1,0:T(8,128)(2,1)S(1)} collective-permute-done((bf16[8,96,512]{2,1,0:T(8,128)(2,1)S(1)}, bf16[8,96,512]{2,1,0:T(8,128)(2,1)S(1)}, u32[]{:S(2)}, u32[]{:S(2)}) %collective-permute-start.3) | collective-permute-done | bytes 786464 | tf_op jit(solution)/shard_map/ppermute | solution.py:300
  84.2 1.1 %shard_map.110 = bf16[128,512]{1,0:T(8,128)(2,1)} custom-call(bf16[2,128,512]{2,1,0:T(8,128)(2,1)S(1)} %shard_map.102.refs_0_, f32[2,128,512]{2,1,0:T(8,128)S(1)} %shard_map.109.refs_1_, bf16[8,96,512]{2,1,0:T(8,128)(2,1)S(1)} %all_to_all.29.refs_1_.refs_2_, bf16[8,96,512]{2,1,0:T(8,128)(2,1)S(1)} %collective-permute-done.3.refs_3_), custom_call_target="tpu_custom_call" | custom-call | flops 1048576 | bytes 1048576 | tf_op jit(solution)/shard_map/pallas_call | solution.py:303
  (1 shorter events, 0.0 us)
Async XLA Ops:
  0.0 14.9 %copy-start.2 = (bf16[1,512,512]{2,1,0:T(8,128)(2,1)S(1)}, bf16[1,512,512]{2,1,0:T(8,128)(2,1)}, u32[]{:S(2)}) copy-start(bf16[1,512,512]{2,1,0:T(8,128)(2,1)} %param.19) | copy-start | bytes 1572868
  0.9 11.3 %collective-permute-start.1 = (bf16[2,32,512]{2,1,0:T(8,128)(2,1)S(1)}, bf16[2,32,512]{2,1,0:T(8,128)(2,1)S(1)}, u32[]{:S(2)}, u32[]{:S(2)}) collective-permute-start(bf16[2,32,512]{2,1,0:T(8,128)(2,1)S(1)} %get-tuple-element.22), channel_id=1, source_target_pairs={{1,2},{2,1},{3,4},{4,3},{5,6},{6,5},{7,8},{8,7},{9,10},{10,9},{11,... | collective-permute-start | bytes 196616 | tf_op jit(solution)/shard_map/ppermute | solution.py:274
  5.5 6.8 %collective-permute-start = (bf16[2,32,512]{2,1,0:T(8,128)(2,1)S(1)}, bf16[2,32,512]{2,1,0:T(8,128)(2,1)S(1)}, u32[]{:S(2)}, u32[]{:S(2)}) collective-permute-start(bf16[2,32,512]{2,1,0:T(8,128)(2,1)S(1)} %get-tuple-element.17.edge_ref), channel_id=1, source_target_pairs={{0,1},{1,0},{2,3},{3,2},{4,5},{5,4},{6,7},{7,6},{8,9},{9,8},{10,11... | collective-permute-start | bytes 196616 | tf_op jit(solution)/shard_map/ppermute | solution.py:275
  11.1 3.8 %copy-start.1 = (bf16[1,512,512]{2,1,0:T(8,128)(2,1)S(1)}, bf16[1,512,512]{2,1,0:T(8,128)(2,1)}, u32[]{:S(2)}) copy-start(bf16[1,512,512]{2,1,0:T(8,128)(2,1)} %param.18) | copy-start | bytes 1572868
  12.3 2.6 %copy-start = (bf16[1,512,512]{2,1,0:T(8,128)(2,1)S(1)}, bf16[1,512,512]{2,1,0:T(8,128)(2,1)}, u32[]{:S(2)}) copy-start(bf16[1,512,512]{2,1,0:T(8,128)(2,1)} %param.17) | copy-start | bytes 1572868
  12.9 3.4 %collective-permute-start.2 = (bf16[2,128,512]{2,1,0:T(8,128)(2,1)S(1)}, bf16[2,128,512]{2,1,0:T(8,128)(2,1)S(1)}, u32[]{:S(2)}, u32[]{:S(2)}) collective-permute-start(bf16[2,128,512]{2,1,0:T(8,128)(2,1)S(1)} %shard_map.102.refs_0_), channel_id=1, source_target_pairs={{0,1},{1,0},{2,3},{3,2},{4,5},{5,4},{6,7},{7,6},{8,9},{9,8},{10,11... | collective-permute-start | bytes 786440 | tf_op jit(solution)/shard_map/ppermute | solution.py:282
  73.5 10.7 %collective-permute-start.3 = (bf16[8,96,512]{2,1,0:T(8,128)(2,1)S(1)}, bf16[8,96,512]{2,1,0:T(8,128)(2,1)S(1)}, u32[]{:S(2)}, u32[]{:S(2)}) collective-permute-start(bf16[8,96,512]{2,1,0:T(8,128)(2,1)S(1)} %all_to_all.29.refs_1_.refs_2_), channel_id=1, source_target_pairs={{0,1},{1,0},{2,3},{3,2},{4,5},{5,4},{6,7},{7,6},{8,9},{9,8},{10,11... | collective-permute-start | bytes 2359304 | tf_op jit(solution)/shard_map/ppermute | solution.py:300
